TPU v7x, 32 devices: a whole 2x2x4 slice. The times are simulated.
32 devices in a mesh: leaf: 8 (over z, core), front: 4 (over y, x).
Axes of the slice: x: 2, y: 2, z: 4, core: 2. Of those that a mesh axis runs over, the one named last changes fastest.
Arguments:
- parent_border_inverse: float32 [8, 1536, 1536], P('leaf', 'front')
- parent_border_rows: float32 [8, 1536, 768], P('leaf', 'front'), may hold values from -0.09 to 0.09
- parent_diagonal_inverse: float32 [8, 768, 768], P('leaf', 'front')
- child_border_rows: float32 [16, 1024, 512], P('leaf', 'front'), may hold values from -0.13 to 0.13
- child_factor_inverse: float32 [16, 512, 512], P('leaf', 'front')
- child_index: int32 [16, 1024], replicated, may hold values from 0 to 2303, as said below
- child_parent: int32 [16], replicated, may hold values from 0 to 7, as said below
Outputs:
- parent_variance: float32 [8, 768], P('leaf')
- child_variance: float32 [16, 512], P('leaf')
Inputs may be any that keep to these rules, and one draw needn't show every extreme that they name: `child_index`: each row holds 1024 distinct positions in increasing order, the first 0 and the last 2303. `child_parent`: child c's parent is c // 2 or c // 2 with its lowest bit flipped, and every parent has exactly two children.
All inputs are finite; a program needn't handle non-finite values.
Results may differ from a plain program's by a relative error of at most 0.0003.
Values sent between devices are 32-bit elements; how exact they have to be, the bound alone decides.
No kernel may reach another device: no remote copies, remote signals or barrier semaphores. Data moves between devices by JAX's collectives and lax.ppermute only.
A program may use at most 64 MiB of HBM per device.

v0:
```python
import functools

import jax
import jax.numpy as jnp
from jax import lax
from jax.experimental import pallas as pl
from jax.experimental.pallas import tpu as pltpu
from jax.sharding import PartitionSpec as P

MIB = 1024 * 1024
COLS = 256
LANES = 128
ROWS = 8


def shape_of(shape, dtype=jnp.float32):
    return jax.ShapeDtypeStruct(shape, dtype)


def exchange(value, leaf_mask, front_mask):
    fronts = lax.axis_size("front")
    pairs = [
        (leaf * fronts + front, (leaf ^ leaf_mask) * fronts + (front ^ front_mask))
        for leaf in range(lax.axis_size("leaf"))
        for front in range(fronts)
    ]
    return lax.ppermute(value, ("leaf", "front"), pairs)


def cross(value):
    fronts = lax.axis_size("front")
    pairs = []
    for leaf in range(lax.axis_size("leaf")):
        for front in range(fronts):
            flip = (leaf ^ front) & 1
            pairs.append((leaf * fronts + front, (leaf ^ flip) * fronts + (front ^ flip)))
    return lax.ppermute(value, ("leaf", "front"), pairs)


def after(value, *others):
    return lax.optimization_barrier((value, *others))[0]


def kids_of(parent_ref, owner):
    partner = owner ^ 1
    pool = [2 * owner, 2 * owner + 1, 2 * partner, 2 * partner + 1]
    member = [parent_ref[kid] == owner for kid in pool]
    first = jnp.where(member[0], 0, jnp.where(member[1], 1, 2))
    second = jnp.where(member[3], 3, jnp.where(member[2], 2, 1))
    ids = [2 * jnp.where(slot < 2, owner, partner) + (slot & 1) for slot in (first, second)]
    return (first, second), ids


def place_of():
    front, leaf = lax.axis_index("front"), lax.axis_index("leaf")
    owner = (leaf & -2) | (front & 1)
    block = (front & -2) | (leaf & 1)
    return owner, block


def rounded(value):
    return value.astype(jnp.bfloat16)


def halves(value):
    high = rounded(value)
    return high, rounded(value - high.astype(jnp.float32))


def dot(left, right):
    return jnp.dot(left, right, preferred_element_type=jnp.float32)


def product(left, right):
    (left_high, left_low), (right_high, right_low) = left, right
    return dot(left_high, right_high) + (dot(left_high, right_low) + dot(left_low, right_high))


def column_sum(value):
    return jnp.sum(value, axis=0, keepdims=True)


def spans(width):
    return [slice(start, start + COLS) for start in range(0, width, COLS)]


def select_kernel(parent_ref, *refs):
    slots, _ = kids_of(parent_ref, lax.axis_index("leaf"))
    half = len(refs) // 3
    for own, other, out in zip(refs[:half], refs[half : 2 * half], refs[2 * half :]):
        for place, slot in enumerate(slots):
            for source in range(4):

                @pl.when(slot == source)
                def _(own=own, other=other, out=out, place=place, source=source):
                    out[place] = (own if source < 2 else other)[source % 2]


def tiles_of(ref, start, rows, column, lanes):
    return jnp.concatenate([ref[pl.ds(start + (row * lanes + column) * ROWS, ROWS), :] for row in range(rows)], axis=0)


def kid_kernel(pieces, parent_ref, index_ref, factor, *refs):
    diagonal, kid_inverse, kid_rows = refs[:pieces], refs[pieces : 2 * pieces], refs[2 * pieces : 3 * pieces]
    reduced, lower_high, weights, lift_high, diag_high, diag_low, parent_sum, kid_sum = refs[
        3 * pieces : 3 * pieces + 8
    ]
    placed, kid_tiles, inv_high, inv_low, up_high, up_low, lifted = refs[3 * pieces + 8 :]
    owner, block = place_of()
    _, ids = kids_of(parent_ref, owner)
    size, border_size = diag_high.shape[0], lower_high.shape[1]
    own_rows, own_border = diagonal[0].shape[0], factor.shape[0]
    kid_size = kid_inverse[0].shape[2]
    kid_block, inv_block = kid_rows[0].shape[1], kid_inverse[0].shape[1]
    lanes = kid_size // LANES
    batch = 8 * ROWS

    parent_sum[...] = column_sum(diagonal[0][...] * diagonal[0][...])
    for mask in range(pieces):
        start = pl.multiple_of((block ^ mask) * own_rows, 16)
        high, low = halves(diagonal[mask][...])
        diag_high[pl.ds(start, own_rows), :] = high
        diag_low[pl.ds(start, own_rows), :] = low
    factor_halves = halves(factor[...])
    for span in spans(size):
        weights[:, span] = product(factor_halves, (diag_high[:, span], diag_low[:, span]))

    for kid in range(2):
        own_sum = column_sum(kid_inverse[0][kid] * kid_inverse[0][kid])
        for mask in range(pieces):
            start = pl.multiple_of((block ^ mask) * inv_block, 16)
            high, low = halves(kid_inverse[mask][kid])
            inv_high[pl.ds(start, inv_block), :] = high
            inv_low[pl.ds(start, inv_block), :] = low

        def clear(step, carry):
            placed[pl.ds(pl.multiple_of(step * 512, 512), 512), :] = jnp.zeros((512, LANES), jnp.float32)
            return carry

        lax.fori_loop(0, placed.shape[0] // 512, clear, 0)
        for mask in range(pieces):
            kid_weight = product(halves(kid_rows[mask][kid]), (inv_high[...], inv_low[...]))
            for row in range(kid_block // ROWS):
                for column in range(lanes):
                    kid_tiles[pl.ds((row * lanes + column) * ROWS, ROWS), :] = kid_weight[
                        row * ROWS : (row + 1) * ROWS, column * LANES : (column + 1) * LANES
                    ]
            start = (block ^ mask) * kid_block

            def put(step, carry, kid=kid, start=start):
                for row in range(ROWS):
                    target = index_ref[ids[kid], start + step * ROWS + row]
                    place = (target >> 3) * (lanes * ROWS) + (target & 7)
                    placed[pl.ds(place, lanes, stride=ROWS), :] = kid_tiles[
                        pl.ds(step * (lanes * ROWS) + row, lanes, stride=ROWS), :
                    ]
                return carry

            lax.fori_loop(0, kid_block // ROWS, put, 0, unroll=2)

        def upper(step, carry):
            start = pl.multiple_of(step * (batch * lanes), batch * lanes)
            for column in range(lanes):
                high, low = halves(tiles_of(placed, start, 8, column, lanes))
                target = pl.ds(pl.multiple_of(step * batch, batch), batch)
                up_high[target, column * LANES : (column + 1) * LANES] = high
                up_low[target, column * LANES : (column + 1) * LANES] = low
            return carry

        lax.fori_loop(0, size // batch, upper, 0)

        def lower(step, carry, kid=kid):
            start = pl.multiple_of(step * (batch * lanes) + size * lanes, batch * lanes)
            for column in range(lanes):
                target = pl.ds(pl.multiple_of(step * batch, batch), batch)
                lower_high[kid, target, column * LANES : (column + 1) * LANES] = rounded(
                    tiles_of(placed, start, 8, column, lanes)
                )
            return carry

        lax.fori_loop(0, border_size // batch, lower, 0)

        own_start = pl.multiple_of((size + block * own_border) * lanes, ROWS)
        for span in spans(kid_size):
            lifted[...] = product((diag_high[...], diag_low[...]), (up_high[:, span], up_low[:, span]))
            lift_high[kid, :, span] = rounded(lifted[...])
            own = lifted[pl.ds(pl.multiple_of(block * own_rows, 16), own_rows), :]
            kid_sum[kid : kid + 1, span] = own_sum[:, span] + column_sum(own * own)
            image = dot(factor_halves[0], lift_high[kid, :, span])
            for half in range(COLS // LANES):
                column = span.start // LANES + half
                own_lower = tiles_of(placed, own_start, own_border // ROWS, column, lanes)
                reduced[kid, :, column * LANES : (column + 1) * LANES] = (
                    own_lower - image[:, half * LANES : (half + 1) * LANES]
                )


def border_kernel(border, lower_high, border_high, border_lower):
    border_high[...] = rounded(border[...])
    for kid in range(2):
        for span in spans(lower_high.shape[2]):
            border_lower[kid, :, span] = dot(border_high[...], lower_high[kid, :, span])


def image_kernel(pieces, *refs):
    factor = refs[:pieces]
    border_high, border_lower, reduced, weights, lift_high, diag_high, diag_low, parent_sum, kid_sum, out = refs[
        pieces : pieces + 10
    ]
    factor_high, fold_high, fold_low = refs[pieces + 10 :]
    _, block = place_of()
    own_border, size = factor[0].shape
    kid_size = reduced.shape[2]
    for mask in range(pieces):
        start = pl.multiple_of((block ^ mask) * own_border, 16)
        factor_high[pl.ds(start, own_border), :] = rounded(factor[mask][...])
    for span in spans(size):
        fold_high[:, span], fold_low[:, span] = halves(dot(border_high[...], factor_high[:, span]))
    fold = fold_high[...], fold_low[...]
    for span in spans(size):
        image = product(fold, (diag_high[:, span], diag_low[:, span]))
        out[:, span] = parent_sum[:, span] + column_sum(weights[:, span] * image)
    for kid in range(2):
        for span in spans(kid_size):
            image = border_lower[kid, :, span] - dot(fold[0], lift_high[kid, :, span])
            target = size + kid * kid_size + span.start
            out[:, target : target + COLS] = kid_sum[kid : kid + 1, span] + column_sum(reduced[kid, :, span] * image)


def finish_kernel(count, parent_ref, *refs):
    partials, (parent_out, kid_out) = refs[:count], refs[count:]
    leaf = lax.axis_index("leaf")
    size, kid_size = parent_out.shape[1], kid_out.shape[1]
    sums = []
    for group in (partials[: count // 2], partials[count // 2 :]):
        terms = [group[at][...] + group[at + 1][...] for at in range(0, len(group), 2)]
        sums.append(functools.reduce(jnp.add, terms))
    owner, _ = place_of()
    parent_out[...] = jnp.where(owner == leaf, sums[0][:, :size], sums[1][:, :size])
    for parent, total in ((owner, sums[0]), (owner ^ 1, sums[1])):
        _, ids = kids_of(parent_ref, parent)
        for place in range(2):
            for kid in range(2):

                @pl.when(ids[place] == 2 * leaf + kid)
                def _(total=total, place=place, kid=kid):
                    start = size + place * kid_size
                    kid_out[kid : kid + 1] = total[:, start : start + kid_size]


def call(kernel, out_shape, scalars, limit, scratch=(), flops=0, moved=0):
    def run(*args):
        specs = [pl.BlockSpec(memory_space=pltpu.SMEM if at < scalars else pltpu.VMEM) for at in range(len(args))]
        args = [
            value if at < scalars else pltpu.with_memory_space_constraint(value, pltpu.VMEM)
            for at, value in enumerate(args)
        ]
        return pl.pallas_call(
            kernel,
            out_shape=jax.tree.map(lambda leaf: pltpu.VMEM(leaf.shape, leaf.dtype), out_shape),
            in_specs=specs,
            out_specs=jax.tree.map(lambda _: pl.BlockSpec(memory_space=pltpu.VMEM), out_shape),
            scratch_shapes=scratch,
            compiler_params=pltpu.CompilerParams(vmem_limit_bytes=limit * MIB),
            cost_estimate=pl.CostEstimate(flops=flops, bytes_accessed=moved, transcendentals=0),
        )(*args)

    return run


def shards(border, factor, diagonal, kid_rows, kid_inverse, child_index, child_parent):
    border, factor, diagonal = border[0], factor[0], diagonal[0]
    pieces = lax.axis_size("front")
    size, kid_size, border_size = diagonal.shape[1], kid_rows.shape[2], border.shape[1]
    own_border = border.shape[0]
    lanes = kid_size // LANES
    half = jnp.bfloat16

    def over_fronts(value):
        parts = {0: value}
        bit = 2
        while bit < pieces:
            for mask in list(parts):
                parts[mask | bit] = exchange(parts[mask], 0, bit)
            bit *= 2
        return parts

    def over_cores(parts, *others):
        return {mask | 1: exchange(after(part, *others), 1, 0) for mask, part in parts.items()}

    def spread(parts, gate_own, gate_rest):
        own = {0: parts[0]}
        rest = {mask: part for mask, part in parts.items() if mask}
        return parts | over_cores(own, gate_own) | over_cores(rest, gate_rest)

    def listed(parts):
        return [parts[mask] for mask in range(pieces)]

    last = pieces - 2
    crossed_diagonal = cross(diagonal)
    kid_bytes = kid_rows.size * 4 + kid_inverse.size * 4
    own_inverse, own_kids = call(
        select_kernel, (shape_of(kid_inverse.shape), shape_of(kid_rows.shape)), 1, 4, moved=3 * kid_bytes
    )(child_parent, kid_inverse, kid_rows, exchange(kid_inverse, 1, 0), exchange(kid_rows, 1, 0))
    own_inverse = cross(after(own_inverse, crossed_diagonal))
    own_kids = cross(after(own_kids, crossed_diagonal))
    own_factor = cross(after(factor, own_kids))
    own_border_rows = cross(after(border, own_factor))

    diagonal_parts = over_fronts(crossed_diagonal)
    inverse_parts = over_fronts(after(own_inverse, diagonal_parts[last]))
    kid_parts = over_fronts(after(own_kids, inverse_parts[0]))
    arrived = kid_parts[last]
    diagonal_parts = spread(diagonal_parts, own_kids, arrived)
    inverse_parts = spread(inverse_parts, own_kids, arrived)
    kid_parts = spread(kid_parts, own_kids, arrived)
    factor_parts = over_fronts(after(own_factor, inverse_parts[last | 1]))
    factor_parts[0] = own_factor

    reduced, lower_high, *state = call(
        functools.partial(kid_kernel, pieces),
        (
            shape_of((2, own_border, kid_size)),
            shape_of((2, border_size, kid_size), half),
            shape_of((own_border, size)),
            shape_of((2, size, kid_size), half),
            shape_of((size, size), half),
            shape_of((size, size), half),
            shape_of((1, size)),
            shape_of((2, kid_size)),
        ),
        2,
        22,
        [
            pltpu.VMEM(((size + border_size) * lanes, LANES), jnp.float32),
            pltpu.VMEM((kid_rows.shape[1] * lanes, LANES), jnp.float32),
            pltpu.VMEM((kid_size, kid_size), half),
            pltpu.VMEM((kid_size, kid_size), half),
            pltpu.VMEM((size, kid_size), half),
            pltpu.VMEM((size, kid_size), half),
            pltpu.VMEM((size, COLS), jnp.float32),
        ],
        flops=10_000_000_000,
        moved=10_000_000,
    )(child_parent, child_index, own_factor, *listed(diagonal_parts), *listed(inverse_parts), *listed(kid_parts))

    factor_parts = spread(factor_parts, arrived, state[0])

    border_high, border_lower = call(
        border_kernel,
        (shape_of(border.shape, half), shape_of((2, own_border, kid_size))),
        0,
        8,
        flops=1_200_000_000,
        moved=1_000_000,
    )(own_border_rows, lower_high)

    total = call(
        functools.partial(image_kernel, pieces),
        shape_of((1, size + 2 * kid_size)),
        0,
        16,
        [
            pltpu.VMEM((border_size, size), half),
            pltpu.VMEM((own_border, size), half),
            pltpu.VMEM((own_border, size), half),
        ],
        flops=3_000_000_000,
        moved=1_000_000,
    )(*listed(factor_parts), border_high, border_lower, reduced, *state)

    bit = 4
    while bit < pieces:
        total = total + exchange(total, 0, bit)
        bit *= 2
    low = range(min(pieces, 4))
    order = [(core, mask) for parity in (0, 1) for mask in low if mask % 2 == parity for core in (0, 1)]
    partials = [exchange(total, core, mask) if core or mask else total for core, mask in order]
    return call(
        functools.partial(finish_kernel, len(partials)), (shape_of((1, size)), shape_of((2, kid_size))), 1, 4
    )(child_parent, *partials)


def solution(mesh):
    whole = P("leaf", "front", None)
    return jax.shard_map(
        shards,
        mesh=mesh,
        in_specs=(whole,) * 5 + (P(), P()),
        out_specs=(P("leaf", None), P("leaf", None)),
        check_vma=False,
    )
```

profile of v0, /device:TPU:0, one launch (start us, length us, event | category | flops | bytes accessed | tf_op | source)
XLA Modules:
  0.0 113.5 jit_solution(12162272998045995485)
XLA Ops:
  0.6 0.5 collective-permute-start.1
  1.2 1.8 %collective-permute-start.2 = (f32[192,768]{1,0:T(8,128)}, f32[192,768]{1,0:T(8,128)S(1)}, u32[]{:S(2)}, u32[]{:S(2)}) collective-permute-start(f32[192,768]{1,0:T(8,128)} %bitcast.5), channel_id=1, source_target_pairs={{0,0},{1,4},{2,2},{3,6},{4,1},{5,5},{6,3},{7,7},{8,8},{9,12},{10,1... | collective-permute-start | bytes 1769480 | tf_op jit(solution)/shard_map/ppermute | solution.py:37
  3.0 2.8 %collective-permute-start = (f32[2,128,512]{2,1,0:T(8,128)}, f32[2,128,512]{2,1,0:T(8,128)S(1)}, u32[]{:S(2)}, u32[]{:S(2)}) collective-permute-start(f32[2,128,512]{2,1,0:T(8,128)} %refs_0_.1), channel_id=1, source_target_pairs={{0,4},{1,5},{2,6},{3,7},{4,0},{5,1},{6,2},{7,3},{8,12},{9,13},{10,... | collective-permute-start | bytes 1572872 | tf_op jit(solution)/shard_map/ppermute | solution.py:27
  5.8 1.7 %collective-permute-done.refs_2_ = f32[2,128,512]{2,1,0:T(8,128)S(1)} collective-permute-done((f32[2,128,512]{2,1,0:T(8,128)}, f32[2,128,512]{2,1,0:T(8,128)S(1)}, u32[]{:S(2)}, u32[]{:S(2)}) %collective-permute-start) | collective-permute-done | bytes 524320 | tf_op jit(solution)/shard_map/ppermute | solution.py:27
  7.5 0.0 collective-permute-done.1.refs_3_
  7.5 1.2 %copy-done = f32[2,256,512]{2,1,0:T(8,128)S(1)} copy-done((f32[2,256,512]{2,1,0:T(8,128)S(1)}, f32[2,256,512]{2,1,0:T(8,128)}, u32[]{:S(2)}) %copy-start) | copy-done | bytes 1048600
  8.7 1.0 copy-done.1
  9.8 0.7 copy-done.2
  10.4 0.7 shard_map.86
  11.2 0.0 collective-permute-done.2.refs_0_
  11.2 0.9 collective-permute-start.3
  12.0 1.6 %collective-permute-start.6 = (f32[192,768]{1,0:T(8,128)S(1)}, f32[192,768]{1,0:T(8,128)S(1)}, u32[]{:S(2)}, u32[]{:S(2)}) collective-permute-start(f32[192,768]{1,0:T(8,128)S(1)} %collective-permute-done.2.refs_0_), channel_id=1, source_target_pairs={{0,2},{1,3},{2,0},{3,1},{4,6},{5,7},{6,4},{7,5},{8,10},{9,11},{10,... | collective-permute-start | bytes 1769480 | tf_op jit(solution)/shard_map/ppermute | solution.py:27
  13.6 0.7 collective-permute-start.5
  14.3 9.8 %collective-permute-done.6.refs_2_ = f32[192,768]{1,0:T(8,128)S(1)} collective-permute-done((f32[192,768]{1,0:T(8,128)S(1)}, f32[192,768]{1,0:T(8,128)S(1)}, u32[]{:S(2)}, u32[]{:S(2)}) %collective-permute-start.6) | collective-permute-done | bytes 589856 | tf_op jit(solution)/shard_map/ppermute | solution.py:27
  24.1 0.0 collective-permute-done.5.refs_4_
  24.1 0.0 collective-permute-done.3.refs_8_
  24.1 1.5 %collective-permute-start.7 = (f32[2,256,512]{2,1,0:T(8,128)S(1)}, f32[2,256,512]{2,1,0:T(8,128)S(1)}, u32[]{:S(2)}, u32[]{:S(2)}) collective-permute-start(f32[2,256,512]{2,1,0:T(8,128)S(1)} %collective-permute-done.3.refs_8_), channel_id=1, source_target_pairs={{0,2},{1,3},{2,0},{3,1},{4,6},{5,7},{6,4},{7,5},{8,10},{9,11},{10,... | collective-permute-start | bytes 3145736 | tf_op jit(solution)/shard_map/ppermute | solution.py:27
  25.7 1.9 %collective-permute-start.4 = (f32[384,768]{1,0:T(8,128)}, f32[384,768]{1,0:T(8,128)S(1)}, u32[]{:S(2)}, u32[]{:S(2)}) collective-permute-start(f32[384,768]{1,0:T(8,128)} %bitcast.4), channel_id=1, source_target_pairs={{0,0},{1,4},{2,2},{3,6},{4,1},{5,5},{6,3},{7,7},{8,8},{9,12},{10,1... | collective-permute-start | bytes 3538952 | tf_op jit(solution)/shard_map/ppermute | solution.py:37
  27.6 0.5 collective-permute-start.9
  28.1 12.5 %collective-permute-start.14 = (f32[2,128,512]{2,1,0:T(8,128)S(1)}, f32[2,128,512]{2,1,0:T(8,128)S(1)}, u32[]{:S(2)}, u32[]{:S(2)}) collective-permute-start(f32[2,128,512]{2,1,0:T(8,128)S(1)} %collective-permute-done.5.refs_4_), channel_id=1, source_target_pairs={{0,4},{1,5},{2,6},{3,7},{4,0},{5,1},{6,2},{7,3},{8,12},{9,13},{10,... | collective-permute-start | bytes 1572872 | tf_op jit(solution)/shard_map/ppermute | solution.py:27
  40.6 0.0 collective-permute-start.15
  40.6 0.0 collective-permute-done.7.refs_10_
  40.6 15.6 %collective-permute-start.16 = (f32[2,256,512]{2,1,0:T(8,128)S(1)}, f32[2,256,512]{2,1,0:T(8,128)S(1)}, u32[]{:S(2)}, u32[]{:S(2)}) collective-permute-start(f32[2,256,512]{2,1,0:T(8,128)S(1)} %collective-permute-done.7.refs_10_), channel_id=1, source_target_pairs={{0,4},{1,5},{2,6},{3,7},{4,0},{5,1},{6,2},{7,3},{8,12},{9,13},{10,... | collective-permute-start | bytes 3145736 | tf_op jit(solution)/shard_map/ppermute | solution.py:27
  56.2 0.0 collective-permute-done.9.refs_6_
  56.2 5.6 %collective-permute-start.10 = (f32[2,128,512]{2,1,0:T(8,128)S(1)}, f32[2,128,512]{2,1,0:T(8,128)S(1)}, u32[]{:S(2)}, u32[]{:S(2)}) collective-permute-start(f32[2,128,512]{2,1,0:T(8,128)S(1)} %collective-permute-done.9.refs_6_), channel_id=1, source_target_pairs={{0,4},{1,5},{2,6},{3,7},{4,0},{5,1},{6,2},{7,3},{8,12},{9,13},{10,... | collective-permute-start | bytes 1572872 | tf_op jit(solution)/shard_map/ppermute | solution.py:27
  61.8 0.0 collective-permute-done.14.refs_5_
  61.8 0.0 collective-permute-start.12
  61.8 0.0 collective-permute-done.4.factor.refs_0_
  61.8 0.5 collective-permute-start.13
  62.3 1.0 collective-permute-done.10.refs_7_
  63.4 0.0 copy-done.5
  63.4 0.8 collective-permute-start.18
  64.2 0.0 collective-permute-done.12.refs_1_
  64.2 1.6 %collective-permute-start.11 = (f32[384,768]{1,0:T(8,128)S(1)}, f32[384,768]{1,0:T(8,128)S(1)}, u32[]{:S(2)}, u32[]{:S(2)}) collective-permute-start(f32[384,768]{1,0:T(8,128)S(1)} %collective-permute-done.4.factor.refs_0_), channel_id=1, source_target_pairs={{0,2},{1,3},{2,0},{3,1},{4,6},{5,7},{6,4},{7,5},{8,10},{9,11},{10,... | collective-permute-start | bytes 3538952 | tf_op jit(solution)/shard_map/ppermute | solution.py:27
  65.8 0.0 collective-permute-done.15.refs_9_
  65.8 1.7 %collective-permute-start.8 = (f32[384,768]{1,0:T(8,128)S(1)}, f32[384,768]{1,0:T(8,128)S(1)}, u32[]{:S(2)}, u32[]{:S(2)}) collective-permute-start(f32[384,768]{1,0:T(8,128)S(1)} %collective-permute-done.4.factor.refs_0_), channel_id=1, source_target_pairs={{0,4},{1,5},{2,6},{3,7},{4,0},{5,1},{6,2},{7,3},{8,12},{9,13},{10,... | collective-permute-start | bytes 3538952 | tf_op jit(solution)/shard_map/ppermute | solution.py:27
  67.4 0.0 collective-permute-done.13.refs_3_
  67.4 0.0 collective-permute-done.16.refs_11_
  67.4 0.0 copy-done.3
  67.5 28.3 %shard_map.87 = (f32[2,384,512]{2,1,0:T(8,128)S(1)}, bf16[2,1536,512]{2,1,0:T(8,128)(2,1)S(1)}, f32[384,768]{1,0:T(8,128)S(1)}, bf16[2,768,512]{2,1,0:T(8,128)(2...) custom-call(s32[16]{0:T(128)S(1)} %copy-done.3, ...), custom_call_target="tpu_custom_call" | custom-call | flops 10000000000 | bytes 10000000 | tf_op jit(solution)/shard_map/pallas_call | solution.py:258
  95.8 0.0 collective-permute-done.11.refs_2_
  95.8 0.1 collective-permute-start.17
  95.9 0.0 collective-permute-done.18.border
  95.9 1.4 %shard_map.88 = (bf16[384,1536]{1,0:T(8,128)(2,1)S(1)}, f32[2,384,512]{2,1,0:T(8,128)S(1)}) custom-call(f32[384,1536]{1,0:T(8,128)S(1)} %collective-permute-done.18.border, bf16[2,1536,512]{2,1,0:T(8,128)(2,1)S(1)} %get-tuple-element.47.lower_high), custom_call_target="tpu_custom_call" | custom-call | flops 1200000000 | bytes 1000000 | tf_op jit(solution)/shard_map/pallas_call | solution.py:258
  97.3 0.0 collective-permute-done.8.refs_1_
  97.3 1.4 %collective-permute-done.17.refs_3_ = f32[384,768]{1,0:T(8,128)S(1)} collective-permute-done((f32[384,768]{1,0:T(8,128)S(1)}, f32[384,768]{1,0:T(8,128)S(1)}, u32[]{:S(2)}, u32[]{:S(2)}) %collective-permute-start.17) | collective-permute-done | bytes 1179680 | tf_op jit(solution)/shard_map/ppermute | solution.py:27
  98.7 3.5 %shard_map.89.refs_0_ = f32[1,1792]{1,0:T(1,128)S(1)} custom-call(f32[384,768]{1,0:T(8,128)S(1)} %collective-permute-done.4.factor.refs_0_, f32[384,768]{1,0:T(8,128)S(1)} %collective-permute-done.8.refs_1_, f32[384,768]{1,0:T(8,128)S(1)} %collective-permute-done.11.refs_2_, f32[384,768]{1,0:T(8,128)S(1)} %collective-permute-done.17.refs_3_, ...), custom_call_target="tpu_custom_call" | custom-call | flops 3000000000 | bytes 1000000 | tf_op jit(solution)/shard_map/pallas_call | solution.py:258
  102.2 0.2 collective-permute-start.19
  102.4 0.4 collective-permute-start.20
  102.8 1.3 %collective-permute-start.21 = (f32[1,1792]{1,0:T(1,128)S(1)}, f32[1,1792]{1,0:T(1,128)S(1)}, u32[]{:S(2)}, u32[]{:S(2)}) collective-permute-start(f32[1,1792]{1,0:T(1,128)S(1)} %shard_map.89.refs_0_), channel_id=1, source_target_pairs={{0,6},{1,7},{2,4},{3,5},{4,2},{5,3},{6,0},{7,1},{8,14},{9,15},{10,... | collective-permute-start | bytes 21512 | tf_op jit(solution)/shard_map/ppermute | solution.py:27
  104.2 1.6 %collective-permute-start.22 = (f32[1,1792]{1,0:T(1,128)S(1)}, f32[1,1792]{1,0:T(1,128)S(1)}, u32[]{:S(2)}, u32[]{:S(2)}) collective-permute-start(f32[1,1792]{1,0:T(1,128)S(1)} %shard_map.89.refs_0_), channel_id=1, source_target_pairs={{0,1},{1,0},{2,3},{3,2},{4,5},{5,4},{6,7},{7,6},{8,9},{9,8},{10,11... | collective-permute-start | bytes 21512 | tf_op jit(solution)/shard_map/ppermute | solution.py:27
  105.7 0.3 collective-permute-start.23
  106.0 0.0 collective-permute-done.19.refs_1_
  106.0 1.7 %collective-permute-start.24 = (f32[1,1792]{1,0:T(1,128)S(1)}, f32[1,1792]{1,0:T(1,128)S(1)}, u32[]{:S(2)}, u32[]{:S(2)}) collective-permute-start(f32[1,1792]{1,0:T(1,128)S(1)} %shard_map.89.refs_0_), channel_id=1, source_target_pairs={{0,3},{1,2},{2,1},{3,0},{4,7},{5,6},{6,5},{7,4},{8,11},{9,10},{10,... | collective-permute-start | bytes 21512 | tf_op jit(solution)/shard_map/ppermute | solution.py:27
  107.7 0.0 collective-permute-done.20.refs_2_
  107.7 0.9 collective-permute-start.25
  108.6 0.0 collective-permute-done.21.refs_3_
  108.6 0.0 collective-permute-done.22.refs_4_
  108.6 0.3 collective-permute-done.23.refs_5_
  108.8 1.8 %collective-permute-done.24.refs_6_ = f32[1,1792]{1,0:T(1,128)S(1)} collective-permute-done((f32[1,1792]{1,0:T(1,128)S(1)}, f32[1,1792]{1,0:T(1,128)S(1)}, u32[]{:S(2)}, u32[]{:S(2)}) %collective-permute-start.24) | collective-permute-done | bytes 7200 | tf_op jit(solution)/shard_map/ppermute | solution.py:27
  110.6 1.1 collective-permute-done.25.refs_7_
  111.7 0.6 shard_map.90
  112.3 0.6 copy.10
  112.9 0.6 copy.9
  (7 shorter events, 0.0 us)
Async XLA Ops:
  0.6 6.9 %collective-permute-start.1 = (f32[2,256,512]{2,1,0:T(8,128)}, f32[2,256,512]{2,1,0:T(8,128)S(1)}, u32[]{:S(2)}, u32[]{:S(2)}) collective-permute-start(f32[2,256,512]{2,1,0:T(8,128)} %refs_1_.1), channel_id=1, source_target_pairs={{0,4},{1,5},{2,6},{3,7},{4,0},{5,1},{6,2},{7,3},{8,12},{9,13},{10,... | collective-permute-start | bytes 3145736 | tf_op jit(solution)/shard_map/ppermute | solution.py:27
  1.1 66.3 %copy-start.3 = (s32[16]{0:T(128)S(1)}, s32[16]{0:T(128)}, u32[]{:S(2)}) copy-start(s32[16]{0:T(128)} %parent_ref.5) | copy-start | bytes 196
  1.2 10.0 %collective-permute-start.2 = (f32[192,768]{1,0:T(8,128)}, f32[192,768]{1,0:T(8,128)S(1)}, u32[]{:S(2)}, u32[]{:S(2)}) collective-permute-start(f32[192,768]{1,0:T(8,128)} %bitcast.5), channel_id=1, source_target_pairs={{0,0},{1,4},{2,2},{3,6},{4,1},{5,5},{6,3},{7,7},{8,8},{9,12},{10,1... | collective-permute-start | bytes 1769480 | tf_op jit(solution)/shard_map/ppermute | solution.py:37
  3.0 4.5 %collective-permute-start = (f32[2,128,512]{2,1,0:T(8,128)}, f32[2,128,512]{2,1,0:T(8,128)S(1)}, u32[]{:S(2)}, u32[]{:S(2)}) collective-permute-start(f32[2,128,512]{2,1,0:T(8,128)} %refs_0_.1), channel_id=1, source_target_pairs={{0,4},{1,5},{2,6},{3,7},{4,0},{5,1},{6,2},{7,3},{8,12},{9,13},{10,... | collective-permute-start | bytes 1572872 | tf_op jit(solution)/shard_map/ppermute | solution.py:27
  7.5 1.2 %copy-start = (f32[2,256,512]{2,1,0:T(8,128)S(1)}, f32[2,256,512]{2,1,0:T(8,128)}, u32[]{:S(2)}) copy-start(f32[2,256,512]{2,1,0:T(8,128)} %refs_1_.1) | copy-start | bytes 3145732
  8.7 1.0 copy-start.1
  9.8 0.7 copy-start.2
  10.4 52.9 %copy-start.5 = (f32[1,384,1536]{2,1,0:T(8,128)S(1)}, f32[1,384,1536]{2,1,0:T(8,128)}, u32[]{:S(2)}) copy-start(f32[1,384,1536]{2,1,0:T(8,128)} %param.7) | copy-start | bytes 7077892
  10.4 57.0 %copy-start.4 = (s32[16,1024]{1,0:T(8,128)S(1)}, s32[16,1024]{1,0:T(8,128)}, u32[]{:S(2)}) copy-start(s32[16,1024]{1,0:T(8,128)} %index_ref.1) | copy-start | bytes 196612
  11.2 13.0 %collective-permute-start.3 = (f32[2,256,512]{2,1,0:T(8,128)S(1)}, f32[2,256,512]{2,1,0:T(8,128)S(1)}, u32[]{:S(2)}, u32[]{:S(2)}) collective-permute-start(f32[2,256,512]{2,1,0:T(8,128)S(1)} %get-tuple-element.30), channel_id=1, source_target_pairs={{0,0},{1,4},{2,2},{3,6},{4,1},{5,5},{6,3},{7,7},{8,8},{9,12},{10,1... | collective-permute-start | bytes 3145736 | tf_op jit(solution)/shard_map/ppermute | solution.py:37
  12.0 12.1 %collective-permute-start.6 = (f32[192,768]{1,0:T(8,128)S(1)}, f32[192,768]{1,0:T(8,128)S(1)}, u32[]{:S(2)}, u32[]{:S(2)}) collective-permute-start(f32[192,768]{1,0:T(8,128)S(1)} %collective-permute-done.2.refs_0_), channel_id=1, source_target_pairs={{0,2},{1,3},{2,0},{3,1},{4,6},{5,7},{6,4},{7,5},{8,10},{9,11},{10,... | collective-permute-start | bytes 1769480 | tf_op jit(solution)/shard_map/ppermute | solution.py:27
  13.6 10.5 %collective-permute-start.5 = (f32[2,128,512]{2,1,0:T(8,128)S(1)}, f32[2,128,512]{2,1,0:T(8,128)S(1)}, u32[]{:S(2)}, u32[]{:S(2)}) collective-permute-start(f32[2,128,512]{2,1,0:T(8,128)S(1)} %get-tuple-element.33), channel_id=1, source_target_pairs={{0,0},{1,4},{2,2},{3,6},{4,1},{5,5},{6,3},{7,7},{8,8},{9,12},{10,1... | collective-permute-start | bytes 1572872 | tf_op jit(solution)/shard_map/ppermute | solution.py:37
  24.1 16.5 %collective-permute-start.7 = (f32[2,256,512]{2,1,0:T(8,128)S(1)}, f32[2,256,512]{2,1,0:T(8,128)S(1)}, u32[]{:S(2)}, u32[]{:S(2)}) collective-permute-start(f32[2,256,512]{2,1,0:T(8,128)S(1)} %collective-permute-done.3.refs_8_), channel_id=1, source_target_pairs={{0,2},{1,3},{2,0},{3,1},{4,6},{5,7},{6,4},{7,5},{8,10},{9,11},{10,... | collective-permute-start | bytes 3145736 | tf_op jit(solution)/shard_map/ppermute | solution.py:27
  25.7 36.2 %collective-permute-start.4 = (f32[384,768]{1,0:T(8,128)}, f32[384,768]{1,0:T(8,128)S(1)}, u32[]{:S(2)}, u32[]{:S(2)}) collective-permute-start(f32[384,768]{1,0:T(8,128)} %bitcast.4), channel_id=1, source_target_pairs={{0,0},{1,4},{2,2},{3,6},{4,1},{5,5},{6,3},{7,7},{8,8},{9,12},{10,1... | collective-permute-start | bytes 3538952 | tf_op jit(solution)/shard_map/ppermute | solution.py:37
  27.6 28.6 %collective-permute-start.9 = (f32[2,128,512]{2,1,0:T(8,128)S(1)}, f32[2,128,512]{2,1,0:T(8,128)S(1)}, u32[]{:S(2)}, u32[]{:S(2)}) collective-permute-start(f32[2,128,512]{2,1,0:T(8,128)S(1)} %collective-permute-done.5.refs_4_), channel_id=1, source_target_pairs={{0,2},{1,3},{2,0},{3,1},{4,6},{5,7},{6,4},{7,5},{8,10},{9,11},{10,... | collective-permute-start | bytes 1572872 | tf_op jit(solution)/shard_map/ppermute | solution.py:27
  28.1 33.7 %collective-permute-start.14 = (f32[2,128,512]{2,1,0:T(8,128)S(1)}, f32[2,128,512]{2,1,0:T(8,128)S(1)}, u32[]{:S(2)}, u32[]{:S(2)}) collective-permute-start(f32[2,128,512]{2,1,0:T(8,128)S(1)} %collective-permute-done.5.refs_4_), channel_id=1, source_target_pairs={{0,4},{1,5},{2,6},{3,7},{4,0},{5,1},{6,2},{7,3},{8,12},{9,13},{10,... | collective-permute-start | bytes 1572872 | tf_op jit(solution)/shard_map/ppermute | solution.py:27
  40.6 25.1 %collective-permute-start.15 = (f32[2,256,512]{2,1,0:T(8,128)S(1)}, f32[2,256,512]{2,1,0:T(8,128)S(1)}, u32[]{:S(2)}, u32[]{:S(2)}) collective-permute-start(f32[2,256,512]{2,1,0:T(8,128)S(1)} %collective-permute-done.3.refs_8_), channel_id=1, source_target_pairs={{0,4},{1,5},{2,6},{3,7},{4,0},{5,1},{6,2},{7,3},{8,12},{9,13},{10,... | collective-permute-start | bytes 3145736 | tf_op jit(solution)/shard_map/ppermute | solution.py:27
  40.6 26.8 %collective-permute-start.16 = (f32[2,256,512]{2,1,0:T(8,128)S(1)}, f32[2,256,512]{2,1,0:T(8,128)S(1)}, u32[]{:S(2)}, u32[]{:S(2)}) collective-permute-start(f32[2,256,512]{2,1,0:T(8,128)S(1)} %collective-permute-done.7.refs_10_), channel_id=1, source_target_pairs={{0,4},{1,5},{2,6},{3,7},{4,0},{5,1},{6,2},{7,3},{8,12},{9,13},{10,... | collective-permute-start | bytes 3145736 | tf_op jit(solution)/shard_map/ppermute | solution.py:27
  56.2 7.2 %collective-permute-start.10 = (f32[2,128,512]{2,1,0:T(8,128)S(1)}, f32[2,128,512]{2,1,0:T(8,128)S(1)}, u32[]{:S(2)}, u32[]{:S(2)}) collective-permute-start(f32[2,128,512]{2,1,0:T(8,128)S(1)} %collective-permute-done.9.refs_6_), channel_id=1, source_target_pairs={{0,4},{1,5},{2,6},{3,7},{4,0},{5,1},{6,2},{7,3},{8,12},{9,13},{10,... | collective-permute-start | bytes 1572872 | tf_op jit(solution)/shard_map/ppermute | solution.py:27
  61.8 2.4 %collective-permute-start.12 = (f32[192,768]{1,0:T(8,128)S(1)}, f32[192,768]{1,0:T(8,128)S(1)}, u32[]{:S(2)}, u32[]{:S(2)}) collective-permute-start(f32[192,768]{1,0:T(8,128)S(1)} %collective-permute-done.2.refs_0_), channel_id=1, source_target_pairs={{0,4},{1,5},{2,6},{3,7},{4,0},{5,1},{6,2},{7,3},{8,12},{9,13},{10,... | collective-permute-start | bytes 1769480 | tf_op jit(solution)/shard_map/ppermute | solution.py:27
  61.8 5.6 %collective-permute-start.13 = (f32[192,768]{1,0:T(8,128)S(1)}, f32[192,768]{1,0:T(8,128)S(1)}, u32[]{:S(2)}, u32[]{:S(2)}) collective-permute-start(f32[192,768]{1,0:T(8,128)S(1)} %collective-permute-done.6.refs_2_), channel_id=1, source_target_pairs={{0,4},{1,5},{2,6},{3,7},{4,0},{5,1},{6,2},{7,3},{8,12},{9,13},{10,... | collective-permute-start | bytes 1769480 | tf_op jit(solution)/shard_map/ppermute | solution.py:27
  63.4 32.5 %collective-permute-start.18 = (f32[384,1536]{1,0:T(8,128)S(1)}, f32[384,1536]{1,0:T(8,128)S(1)}, u32[]{:S(2)}, u32[]{:S(2)}) collective-permute-start(f32[384,1536]{1,0:T(8,128)S(1)} %bitcast.3), channel_id=1, source_target_pairs={{0,0},{1,4},{2,2},{3,6},{4,1},{5,5},{6,3},{7,7},{8,8},{9,12},{10,1... | collective-permute-start | bytes 7077896 | tf_op jit(solution)/shard_map/ppermute | solution.py:37
  64.2 31.6 %collective-permute-start.11 = (f32[384,768]{1,0:T(8,128)S(1)}, f32[384,768]{1,0:T(8,128)S(1)}, u32[]{:S(2)}, u32[]{:S(2)}) collective-permute-start(f32[384,768]{1,0:T(8,128)S(1)} %collective-permute-done.4.factor.refs_0_), channel_id=1, source_target_pairs={{0,2},{1,3},{2,0},{3,1},{4,6},{5,7},{6,4},{7,5},{8,10},{9,11},{10,... | collective-permute-start | bytes 3538952 | tf_op jit(solution)/shard_map/ppermute | solution.py:27
  65.8 31.5 %collective-permute-start.8 = (f32[384,768]{1,0:T(8,128)S(1)}, f32[384,768]{1,0:T(8,128)S(1)}, u32[]{:S(2)}, u32[]{:S(2)}) collective-permute-start(f32[384,768]{1,0:T(8,128)S(1)} %collective-permute-done.4.factor.refs_0_), channel_id=1, source_target_pairs={{0,4},{1,5},{2,6},{3,7},{4,0},{5,1},{6,2},{7,3},{8,12},{9,13},{10,... | collective-permute-start | bytes 3538952 | tf_op jit(solution)/shard_map/ppermute | solution.py:27
  95.8 2.9 %collective-permute-start.17 = (f32[384,768]{1,0:T(8,128)S(1)}, f32[384,768]{1,0:T(8,128)S(1)}, u32[]{:S(2)}, u32[]{:S(2)}) collective-permute-start(f32[384,768]{1,0:T(8,128)S(1)} %collective-permute-done.11.refs_2_), channel_id=1, source_target_pairs={{0,4},{1,5},{2,6},{3,7},{4,0},{5,1},{6,2},{7,3},{8,12},{9,13},{10,... | collective-permute-start | bytes 3538952 | tf_op jit(solution)/shard_map/ppermute | solution.py:27
  102.2 3.8 %collective-permute-start.19 = (f32[1,1792]{1,0:T(1,128)S(1)}, f32[1,1792]{1,0:T(1,128)S(1)}, u32[]{:S(2)}, u32[]{:S(2)}) collective-permute-start(f32[1,1792]{1,0:T(1,128)S(1)} %shard_map.89.refs_0_), channel_id=1, source_target_pairs={{0,4},{1,5},{2,6},{3,7},{4,0},{5,1},{6,2},{7,3},{8,12},{9,13},{10,... | collective-permute-start | bytes 21512 | tf_op jit(solution)/shard_map/ppermute | solution.py:27
  102.4 5.3 %collective-permute-start.20 = (f32[1,1792]{1,0:T(1,128)S(1)}, f32[1,1792]{1,0:T(1,128)S(1)}, u32[]{:S(2)}, u32[]{:S(2)}) collective-permute-start(f32[1,1792]{1,0:T(1,128)S(1)} %shard_map.89.refs_0_), channel_id=1, source_target_pairs={{0,2},{1,3},{2,0},{3,1},{4,6},{5,7},{6,4},{7,5},{8,10},{9,11},{10,... | collective-permute-start | bytes 21512 | tf_op jit(solution)/shard_map/ppermute | solution.py:27
  102.8 5.8 %collective-permute-start.21 = (f32[1,1792]{1,0:T(1,128)S(1)}, f32[1,1792]{1,0:T(1,128)S(1)}, u32[]{:S(2)}, u32[]{:S(2)}) collective-permute-start(f32[1,1792]{1,0:T(1,128)S(1)} %shard_map.89.refs_0_), channel_id=1, source_target_pairs={{0,6},{1,7},{2,4},{3,5},{4,2},{5,3},{6,0},{7,1},{8,14},{9,15},{10,... | collective-permute-start | bytes 21512 | tf_op jit(solution)/shard_map/ppermute | solution.py:27
  104.2 4.4 %collective-permute-start.22 = (f32[1,1792]{1,0:T(1,128)S(1)}, f32[1,1792]{1,0:T(1,128)S(1)}, u32[]{:S(2)}, u32[]{:S(2)}) collective-permute-start(f32[1,1792]{1,0:T(1,128)S(1)} %shard_map.89.refs_0_), channel_id=1, source_target_pairs={{0,1},{1,0},{2,3},{3,2},{4,5},{5,4},{6,7},{7,6},{8,9},{9,8},{10,11... | collective-permute-start | bytes 21512 | tf_op jit(solution)/shard_map/ppermute | solution.py:27
  105.7 3.1 %collective-permute-start.23 = (f32[1,1792]{1,0:T(1,128)S(1)}, f32[1,1792]{1,0:T(1,128)S(1)}, u32[]{:S(2)}, u32[]{:S(2)}) collective-permute-start(f32[1,1792]{1,0:T(1,128)S(1)} %shard_map.89.refs_0_), channel_id=1, source_target_pairs={{0,5},{1,4},{2,7},{3,6},{4,1},{5,0},{6,3},{7,2},{8,13},{9,12},{10,... | collective-permute-start | bytes 21512 | tf_op jit(solution)/shard_map/ppermute | solution.py:27
  106.0 4.5 %collective-permute-start.24 = (f32[1,1792]{1,0:T(1,128)S(1)}, f32[1,1792]{1,0:T(1,128)S(1)}, u32[]{:S(2)}, u32[]{:S(2)}) collective-permute-start(f32[1,1792]{1,0:T(1,128)S(1)} %shard_map.89.refs_0_), channel_id=1, source_target_pairs={{0,3},{1,2},{2,1},{3,0},{4,7},{5,6},{6,5},{7,4},{8,11},{9,10},{10,... | collective-permute-start | bytes 21512 | tf_op jit(solution)/shard_map/ppermute | solution.py:27
  107.7 4.0 %collective-permute-start.25 = (f32[1,1792]{1,0:T(1,128)S(1)}, f32[1,1792]{1,0:T(1,128)S(1)}, u32[]{:S(2)}, u32[]{:S(2)}) collective-permute-start(f32[1,1792]{1,0:T(1,128)S(1)} %shard_map.89.refs_0_), channel_id=1, source_target_pairs={{0,7},{1,6},{2,5},{3,4},{4,3},{5,2},{6,1},{7,0},{8,15},{9,14},{10,... | collective-permute-start | bytes 21512 | tf_op jit(solution)/shard_map/ppermute | solution.py:27
where the time goes:
time: 114 us; the launch traced here: 113 us
  starting transfers between devices  56.8 us (50%)
  Pallas kernels  34.6 us (30%)
  waiting for transfers between devices  17.2 us (15%)
  local copies, waits for them, and re-layouts  4.1 us (4%)
    ppermute x21, starting transfers between devices, exchange(): return lax.ppermute(value, ('leaf', 'front'), pairs)  50.7 us
    pallas_call x5, Pallas kernels, run(): pl.pallas_call(kernel, out_shape=jax.tree.map(lambda leaf: pltpu.VMEM(lea...  34.6 us
    ppermute x21, waiting for transfers between devices, exchange(): return lax.ppermute(value, ('leaf', 'front'), pairs)  17.2 us
    ppermute x5, starting transfers between devices, cross(): return lax.ppermute(value, ('leaf', 'front'), pairs)  6.1 us
    unnamed x14, local copies, waits for them, and re-layouts  4.1 us
  transfers between devices with their start and end apart: 26, of which 7 were waited for; matrix products, arithmetic and copies ran while one was open for 0% of the time, Pallas kernels for 27%

commit v1 on v0

v1 whole, which is shorter than its diff:
```python
import functools

import jax
import jax.numpy as jnp
from jax import lax
from jax.experimental import pallas as pl
from jax.experimental.pallas import tpu as pltpu
from jax.sharding import PartitionSpec as P

MIB = 1024 * 1024
COLS = 256


def shape_of(shape, dtype=jnp.float32):
    return jax.ShapeDtypeStruct(shape, dtype)


def exchange(value, leaf_mask, front_mask):
    fronts = lax.axis_size("front")
    pairs = [
        (leaf * fronts + front, (leaf ^ leaf_mask) * fronts + (front ^ front_mask))
        for leaf in range(lax.axis_size("leaf"))
        for front in range(fronts)
    ]
    return lax.ppermute(value, ("leaf", "front"), pairs)


def cross(value):
    fronts = lax.axis_size("front")
    pairs = []
    for leaf in range(lax.axis_size("leaf")):
        for front in range(fronts):
            flip = (leaf ^ front) & 1
            pairs.append((leaf * fronts + front, (leaf ^ flip) * fronts + (front ^ flip)))
    return lax.ppermute(value, ("leaf", "front"), pairs)


def after(value, *others):
    return lax.optimization_barrier((value, *others))[0]


def kids_of(parent_ref, owner):
    partner = owner ^ 1
    pool = [2 * owner, 2 * owner + 1, 2 * partner, 2 * partner + 1]
    member = [parent_ref[kid] == owner for kid in pool]
    first = jnp.where(member[0], 0, jnp.where(member[1], 1, 2))
    second = jnp.where(member[3], 3, jnp.where(member[2], 2, 1))
    ids = [2 * jnp.where(slot < 2, owner, partner) + (slot & 1) for slot in (first, second)]
    return (first, second), ids


def place_of():
    front, leaf = lax.axis_index("front"), lax.axis_index("leaf")
    owner = (leaf & -2) | (front & 1)
    block = (front & -2) | (leaf & 1)
    return owner, block


def rounded(value):
    return value.astype(jnp.bfloat16)


def halves(value):
    high = rounded(value)
    return high, rounded(value - high.astype(jnp.float32))


def dot(left, right):
    return jnp.dot(left, right, preferred_element_type=jnp.float32)


def product(left, right):
    (left_high, left_low), (right_high, right_low) = left, right
    return dot(left_high, right_high) + (dot(left_high, right_low) + dot(left_low, right_high))


def column_sum(value):
    return jnp.sum(value, axis=0, keepdims=True)


def spans(width):
    return [slice(start, start + COLS) for start in range(0, width, COLS)]


def select_kernel(parent_ref, index_ref, own_rows, own_inverse, other_rows, other_inverse, kid_out, index_out):
    leaf = lax.axis_index("leaf")
    slots, _ = kids_of(parent_ref, leaf)
    split = own_rows.shape[1]
    for place, slot in enumerate(slots):
        for source in range(4):
            rows, inverse = (own_rows, own_inverse) if source < 2 else (other_rows, other_inverse)

            @pl.when(slot == source)
            def _(rows=rows, inverse=inverse, place=place, source=source):
                kid_out[place, :split] = rows[source % 2]
                kid_out[place, split:] = inverse[source % 2]

    owner, block = place_of()
    _, ids = kids_of(parent_ref, owner)
    for place, kid in enumerate(ids):
        for mask in range(index_out.shape[1]):
            index_out[place, mask : mask + 1, :] = index_ref[kid, pl.ds(block ^ mask, 1), :]


def picks(index, first, rows):
    position = lax.broadcasted_iota(jnp.int32, (rows, index.shape[1]), 0) + first
    return rounded(jnp.where(position == index, 1.0, 0.0))


def diagonal_kernel(pieces, index, *refs):
    diagonal = refs[:pieces]
    diag_high, diag_low, pick_high, pick_low, parent_sum = refs[pieces:]
    _, block = place_of()
    own_rows, size = diagonal[0].shape
    parent_sum[...] = column_sum(diagonal[0][...] * diagonal[0][...])
    for mask in range(pieces):
        start = pl.multiple_of((block ^ mask) * own_rows, 16)
        high, low = halves(diagonal[mask][...])
        diag_high[pl.ds(start, own_rows), :] = high
        diag_low[pl.ds(start, own_rows), :] = low
    for kid in range(2):
        for mask in range(pieces):
            pick = picks(index[kid, mask : mask + 1, :], 0, size)
            pick_high[kid, mask] = rounded(dot(diag_high[...], pick))
            pick_low[kid, mask] = rounded(dot(diag_low[...], pick))


def kid_kernel(pieces, index, pick_high, pick_low, head, tail, *refs):
    kids = refs[:pieces]
    reduced, lift_high, kid_high, kid_sum, inv_high, inv_low, lifted = refs[pieces:]
    _, block = place_of()
    size, own_border = lifted.shape[0], head.shape[0] + tail.shape[0]
    kid_block = kid_high.shape[2]
    inv_block, own_rows = kids[0].shape[1] - kid_block, size // pieces
    factor_high = jnp.concatenate([rounded(head[...]), rounded(tail[...])], axis=0)
    for kid in range(2):
        own_inverse = kids[0][kid, kid_block:]
        for mask in range(pieces):
            start = pl.multiple_of((block ^ mask) * inv_block, 16)
            high, low = halves(kids[mask][kid, kid_block:])
            inv_high[pl.ds(start, inv_block), :] = high
            inv_low[pl.ds(start, inv_block), :] = low
        inverse = inv_high[...], inv_low[...]
        for mask in range(pieces):
            weight = halves(product(halves(kids[mask][kid, :kid_block]), inverse))
            kid_high[kid, mask] = weight[0]
            lifted_part = product((pick_high[kid, mask], pick_low[kid, mask]), weight)
            pick = picks(index[kid, mask : mask + 1, :], size + block * own_border, own_border)
            lower_part = dot(pick, weight[0]) + dot(pick, weight[1])
            lifted[...] = lifted_part if mask == 0 else lifted[...] + lifted_part
            reduced[kid] = lower_part if mask == 0 else reduced[kid] + lower_part
        own = lifted[pl.ds(pl.multiple_of(block * own_rows, 16), own_rows), :]
        kid_sum[kid : kid + 1] = column_sum(own_inverse * own_inverse) + column_sum(own * own)
        lift_high[kid] = rounded(lifted[...])
        reduced[kid] = reduced[kid] - dot(factor_high, lift_high[kid])


def border_kernel(index, border, head, tail, diag_high, diag_low, kid_high, border_high, border_lower, weights):
    border_high[...] = rounded(border[...])
    size, border_size = head.shape[1], border.shape[1]
    for kid in range(2):
        for mask in range(kid_high.shape[1]):
            pick = picks(index[kid, mask : mask + 1, :], size, border_size)
            rows = rounded(dot(border_high[...], pick))
            part = dot(rows, kid_high[kid, mask])
            border_lower[kid] = part if mask == 0 else border_lower[kid] + part
    for part, start in ((head, 0), (tail, head.shape[0])):
        part_halves = halves(part[...])
        rows = slice(start, start + part.shape[0])
        for span in spans(size):
            weights[rows, span] = product(part_halves, (diag_high[:, span], diag_low[:, span]))


def image_kernel(pieces, *refs):
    heads, tails = refs[:pieces], refs[pieces : 2 * pieces]
    border_high, border_lower, weights, reduced, lift_high, diag_high, diag_low, parent_sum, kid_sum, out = refs[
        2 * pieces : 2 * pieces + 10
    ]
    factor_high, fold_high, fold_low = refs[2 * pieces + 10 :]
    _, block = place_of()
    head, size = heads[0].shape
    tail = tails[0].shape[0]
    kid_size = reduced.shape[2]
    for mask in range(pieces):
        start = pl.multiple_of((block ^ mask) * (head + tail), 16)
        factor_high[pl.ds(start, head), :] = rounded(heads[mask][...])
        factor_high[pl.ds(pl.multiple_of(start + head, 16), tail), :] = rounded(tails[mask][...])
    for span in spans(size):
        fold_high[:, span], fold_low[:, span] = halves(dot(border_high[...], factor_high[:, span]))
    fold = fold_high[...], fold_low[...]
    for span in spans(size):
        image = product(fold, (diag_high[:, span], diag_low[:, span]))
        out[:, span] = parent_sum[:, span] + column_sum(weights[:, span] * image)
    for kid in range(2):
        for span in spans(kid_size):
            image = border_lower[kid, :, span] - dot(fold[0], lift_high[kid, :, span])
            target = size + kid * kid_size + span.start
            out[:, target : target + COLS] = kid_sum[kid : kid + 1, span] + column_sum(reduced[kid, :, span] * image)


def finish_kernel(parent_ref, *refs):
    partials, (parent_out, kid_out) = refs[:-2], refs[-2:]
    leaf = lax.axis_index("leaf")
    size, kid_size = parent_out.shape[1], kid_out.shape[1]
    half = len(partials) // 2
    sums = [functools.reduce(jnp.add, [ref[...] for ref in group]) for group in (partials[:half], partials[half:])]
    owner, _ = place_of()
    parent_out[...] = jnp.where(owner == leaf, sums[0][:, :size], sums[1][:, :size])
    for parent, total in ((owner, sums[0]), (owner ^ 1, sums[1])):
        _, ids = kids_of(parent_ref, parent)
        for place in range(2):
            for kid in range(2):

                @pl.when(ids[place] == 2 * leaf + kid)
                def _(total=total, place=place, kid=kid):
                    start = size + place * kid_size
                    kid_out[kid : kid + 1] = total[:, start : start + kid_size]


def call(kernel, out_shape, limit, scalars=0, loose=0, keep=True, scratch=(), moved=1_000):
    def run(*args):
        specs = [pl.BlockSpec(memory_space=pltpu.SMEM if at < scalars else pltpu.VMEM) for at in range(len(args))]
        args = [
            pltpu.with_memory_space_constraint(value, pltpu.HBM if at < loose else pltpu.VMEM)
            for at, value in enumerate(args)
        ]
        results = out_shape
        if keep:
            results = jax.tree.map(lambda leaf: pltpu.VMEM(leaf.shape, leaf.dtype), results)
        return pl.pallas_call(
            kernel,
            out_shape=results,
            in_specs=specs,
            out_specs=jax.tree.map(lambda _: pl.BlockSpec(memory_space=pltpu.VMEM), out_shape),
            scratch_shapes=scratch,
            compiler_params=pltpu.CompilerParams(vmem_limit_bytes=limit * MIB),
            cost_estimate=pl.CostEstimate(flops=0, bytes_accessed=moved, transcendentals=0),
        )(*args)

    return run


def shards(border, factor, diagonal, kid_rows, kid_inverse, child_index, child_parent):
    border, factor, diagonal = border[0], factor[0], diagonal[0]
    pieces = lax.axis_size("front")
    size, kid_size, border_size = diagonal.shape[1], kid_rows.shape[2], border.shape[1]
    own_border = border.shape[0]
    kid_block = kid_rows.shape[1]
    half = jnp.bfloat16

    def over_fronts(value):
        parts = {0: value}
        bit = 2
        while bit < pieces:
            for mask in list(parts):
                parts[mask | bit] = exchange(parts[mask], 0, bit)
            bit *= 2
        return parts

    def spread(parts, gate_own, gate_rest):
        shared = {1: exchange(after(parts[0], *gate_own), 1, 0)}
        for mask in list(parts)[1:]:
            shared[mask | 1] = exchange(after(parts[mask], *gate_rest), 1, 0)
        parts = parts | shared
        return [parts[mask] for mask in range(pieces)]

    last = pieces - 2
    head = -(-own_border // 64) * 16
    factor_head, factor_tail = factor[:head], factor[head:]
    raw_heads = over_fronts(factor_head)
    own_diagonal = cross(diagonal)
    index = child_index.reshape(child_index.shape[0], pieces, kid_block)
    kid_shape = (2, kid_block + kid_inverse.shape[1], kid_size)
    own_kids, index = call(
        select_kernel,
        (shape_of(kid_shape), shape_of((2, pieces, kid_block), jnp.int32)),
        6,
        scalars=1,
        loose=4,
    )(child_parent, index, kid_rows, kid_inverse, exchange(kid_rows, 1, 0), exchange(kid_inverse, 1, 0))
    own_kids = cross(after(own_kids, own_diagonal, raw_heads[last]))
    own_tail = cross(after(factor_tail, own_kids))
    heads = {mask: cross(after(value, own_kids)) for mask, value in raw_heads.items()}
    own_border_rows = cross(after(border, own_kids))

    diagonal_parts = over_fronts(own_diagonal)
    kid_parts = over_fronts(after(own_kids, diagonal_parts[last]))
    diagonal_parts = spread(diagonal_parts, [own_kids], [own_kids])
    diag_high, diag_low, pick_high, pick_low, parent_sum = call(
        functools.partial(diagonal_kernel, pieces),
        (
            shape_of((size, size), half),
            shape_of((size, size), half),
            shape_of((2, pieces, size, kid_block), half),
            shape_of((2, pieces, size, kid_block), half),
            shape_of((1, size)),
        ),
        10,
    )(after(index, own_tail, *heads.values()), *diagonal_parts)
    kids_here = after(kid_parts[last], pick_high)
    tails = over_fronts(after(own_tail, kids_here))
    tails[0] = own_tail
    kid_parts = spread(kid_parts, [], [pick_high])
    own_head = heads[0]
    heads = spread(heads, [kids_here], [kids_here])

    reduced, lift_high, kid_high, kid_sum = call(
        functools.partial(kid_kernel, pieces),
        (
            shape_of((2, own_border, kid_size)),
            shape_of((2, size, kid_size), half),
            shape_of((2, pieces, kid_block, kid_size), half),
            shape_of((2, kid_size)),
        ),
        12,
        scratch=[
            pltpu.VMEM((kid_size, kid_size), half),
            pltpu.VMEM((kid_size, kid_size), half),
            pltpu.VMEM((size, kid_size), jnp.float32),
        ],
    )(index, pick_high, pick_low, own_head, after(own_tail, *heads), *kid_parts)

    border_high, border_lower, weights = call(
        border_kernel,
        (shape_of(border.shape, half), shape_of((2, own_border, kid_size)), shape_of((own_border, size))),
        12,
    )(index, own_border_rows, own_head, own_tail, diag_high, diag_low, kid_high)

    tails = spread(tails, [kids_here], [border_lower])
    total = call(
        functools.partial(image_kernel, pieces),
        shape_of((1, size + 2 * kid_size)),
        12,
        scratch=[
            pltpu.VMEM((border_size, size), half),
            pltpu.VMEM((own_border, size), half),
            pltpu.VMEM((own_border, size), half),
        ],
    )(
        *heads,
        *tails,
        border_high,
        border_lower,
        weights,
        reduced,
        lift_high,
        diag_high,
        diag_low,
        parent_sum,
        kid_sum,
    )

    total = total + exchange(total, 1, 0)
    bit = 4
    while bit < pieces:
        total = total + exchange(total, 0, bit)
        bit *= 2
    near = range(min(pieces, 4))
    order = [mask for parity in (0, 1) for mask in near if mask % 2 == parity]
    partials = [exchange(total, 0, mask) if mask else total for mask in order]
    return call(finish_kernel, (shape_of((1, size)), shape_of((2, kid_size))), 2, scalars=1, loose=1, keep=False)(
        child_parent, *partials
    )


def solution(mesh):
    whole = P("leaf", "front", None)
    return jax.shard_map(
        shards,
        mesh=mesh,
        in_specs=(whole,) * 5 + (P(), P()),
        out_specs=(P("leaf", None), P("leaf", None)),
        check_vma=False,
    )
```

time: 114 us -> 108 us (0.947)
  starting transfers between devices: 56.8 us -> 44.7 us
  waiting for transfers between devices: 17.2 us -> 28.5 us
  Pallas kernels: 34.6 us -> 31 us
  local copies, waits for them, and re-layouts: 4.1 us -> 2.53 us
    ppermute x21 -> x18, starting transfers between devices: 50.7 us -> 39.3 us  [exchange(): return lax.ppermute(value, ('leaf', 'front'), pairs)]
    ppermute x21 -> x18, waiting for transfers between devices: 17.2 us -> 28.5 us  [exchange(): return lax.ppermute(value, ('leaf', 'front'), pairs)]
    unnamed x14 -> x4, local copies, waits for them, and re-layouts: 4.1 us -> 0.01 us
    pallas_call x5 -> x6, Pallas kernels: 34.6 us -> 31 us  [run(): pl.pallas_call(kernel, out_shape=results, in_specs=specs, out_specs=jax.t...]
    reshape x0 -> x1, local copies, waits for them, and re-layouts: none -> 1.48 us  [shards(): index = child_index.reshape(child_index.shape[0], pieces, kid_block)]
    ppermute x5 -> x6, starting transfers between devices: 6.1 us -> 5.35 us  [cross(): return lax.ppermute(value, ('leaf', 'front'), pairs)]
  transfers between devices with their start and end apart: 26 -> 24, of which waited for: 7 -> 10; matrix products, arithmetic and copies ran while one was open for 0% -> 2% of each run, Pallas kernels for 27% -> 24%
where the time goes in v1:
time: 108 us; the launch traced here: 107 us
  starting transfers between devices  44.7 us (41%)
  Pallas kernels  31 us (29%)
  waiting for transfers between devices  28.5 us (26%)
  local copies, waits for them, and re-layouts  2.53 us (2%)
    ppermute x18, starting transfers between devices, exchange(): return lax.ppermute(value, ('leaf', 'front'), pairs)  39.3 us
    pallas_call x6, Pallas kernels, run(): pl.pallas_call(kernel, out_shape=results, in_specs=specs, out_specs=jax.t...  31 us
    ppermute x18, waiting for transfers between devices, exchange(): return lax.ppermute(value, ('leaf', 'front'), pairs)  28.5 us
    ppermute x6, starting transfers between devices, cross(): return lax.ppermute(value, ('leaf', 'front'), pairs)  5.35 us
  transfers between devices with their start and end apart: 24, of which 10 were waited for; matrix products, arithmetic and copies ran while one was open for 2% of the time, Pallas kernels for 24%

profile of v1, /device:TPU:0, one launch (start us, length us, event | category | flops | bytes accessed | tf_op | source)
XLA Modules:
  0.0 107.5 jit_solution(14739306705899016354)
XLA Ops:
  0.6 0.5 collective-permute-start
  1.1 1.7 %collective-permute-start.2 = (f32[192,768]{1,0:T(8,128)}, f32[192,768]{1,0:T(8,128)S(1)}, u32[]{:S(2)}, u32[]{:S(2)}) collective-permute-start(f32[192,768]{1,0:T(8,128)} %bitcast.7), channel_id=1, source_target_pairs={{0,0},{1,4},{2,2},{3,6},{4,1},{5,5},{6,3},{7,7},{8,8},{9,12},{10,1... | collective-permute-start | bytes 1769480 | tf_op jit(solution)/shard_map/ppermute | solution.py:35
  2.9 2.9 %collective-permute-start.1 = (f32[2,128,512]{2,1,0:T(8,128)}, f32[2,128,512]{2,1,0:T(8,128)S(1)}, u32[]{:S(2)}, u32[]{:S(2)}) collective-permute-start(f32[2,128,512]{2,1,0:T(8,128)} %own_inverse.1), channel_id=1, source_target_pairs={{0,4},{1,5},{2,6},{3,7},{4,0},{5,1},{6,2},{7,3},{8,12},{9,13},{10,... | collective-permute-start | bytes 1572872 | tf_op jit(solution)/shard_map/ppermute | solution.py:25
  5.7 1.0 slice_bitcast_fusion.1
  6.7 1.6 %collective-permute-start.3 = (f32[96,768]{1,0:T(8,128)S(1)}, f32[96,768]{1,0:T(8,128)S(1)}, u32[]{:S(2)}, u32[]{:S(2)}) collective-permute-start(f32[96,768]{1,0:T(8,128)S(1)} %slice_bitcast_fusion.1), channel_id=1, source_target_pairs={{0,2},{1,3},{2,0},{3,1},{4,6},{5,7},{6,4},{7,5},{8,10},{9,11},{10,... | collective-permute-start | bytes 884744 | tf_op jit(solution)/shard_map/ppermute | solution.py:25
  8.3 1.5 %reshape.9.index_ref = s32[16,4,256]{2,1,0:T(4,128)} reshape(s32[16,1024]{1,0:T(8,128)} %param.12) | data formatting | bytes 131072 | tf_op jit(solution)/shard_map/reshape | solution.py:272
  9.8 0.0 copy-start
  9.8 0.0 collective-permute-done.1.other_inverse
  9.8 0.0 collective-permute-done.other_rows
  9.8 0.0 copy-start.1
  9.8 1.7 %shard_map.86 = (f32[2,384,512]{2,1,0:T(8,128)S(1)}, s32[2,4,256]{2,1,0:T(4,128)S(1)}) custom-call(s32[16]{0:T(128)} %parent_ref.3, s32[16,4,256]{2,1,0:T(4,128)} %reshape.9.index_ref, f32[2,256,512]{2,1,0:T(8,128)} %own_rows.1, f32[2,128,512]{2,1,0:T(8,128)} %own_inverse.1, f32[2,256,512]{2,1,0:T(8,128)S(1)} %collective-permute-done.other_rows, ...), custom_call_target="tpu_custom_call" | custom-call | bytes 1000 | tf_op jit(solution)/shard_map/pallas_call | solution.py:230
  11.5 4.2 %collective-permute-done.3 = f32[96,768]{1,0:T(8,128)S(1)} collective-permute-done((f32[96,768]{1,0:T(8,128)S(1)}, f32[96,768]{1,0:T(8,128)S(1)}, u32[]{:S(2)}, u32[]{:S(2)}) %collective-permute-start.3) | collective-permute-done | bytes 294944 | tf_op jit(solution)/shard_map/ppermute | solution.py:25
  15.7 0.0 collective-permute-done.2.refs_0_
  15.7 0.8 collective-permute-start.4
  16.5 1.6 %collective-permute-start.6 = (f32[192,768]{1,0:T(8,128)S(1)}, f32[192,768]{1,0:T(8,128)S(1)}, u32[]{:S(2)}, u32[]{:S(2)}) collective-permute-start(f32[192,768]{1,0:T(8,128)S(1)} %collective-permute-done.2.refs_0_), channel_id=1, source_target_pairs={{0,2},{1,3},{2,0},{3,1},{4,6},{5,7},{6,4},{7,5},{8,10},{9,11},{10,... | collective-permute-start | bytes 1769480 | tf_op jit(solution)/shard_map/ppermute | solution.py:25
  18.1 13.6 %collective-permute-done.6.refs_2_ = f32[192,768]{1,0:T(8,128)S(1)} collective-permute-done((f32[192,768]{1,0:T(8,128)S(1)}, f32[192,768]{1,0:T(8,128)S(1)}, u32[]{:S(2)}, u32[]{:S(2)}) %collective-permute-start.6) | collective-permute-done | bytes 589856 | tf_op jit(solution)/shard_map/ppermute | solution.py:25
  31.7 0.0 collective-permute-done.4.refs_0_
  31.7 1.3 %collective-permute-start.7 = (f32[2,384,512]{2,1,0:T(8,128)S(1)}, f32[2,384,512]{2,1,0:T(8,128)S(1)}, u32[]{:S(2)}, u32[]{:S(2)}) collective-permute-start(f32[2,384,512]{2,1,0:T(8,128)S(1)} %collective-permute-done.4.refs_0_), channel_id=1, source_target_pairs={{0,2},{1,3},{2,0},{3,1},{4,6},{5,7},{6,4},{7,5},{8,10},{9,11},{10,... | collective-permute-start | bytes 4718600 | tf_op jit(solution)/shard_map/ppermute | solution.py:25
  32.9 0.0 copy-done
  33.0 0.1 slice_bitcast_fusion
  33.0 0.7 collective-permute-start.5
  33.7 0.7 collective-permute-start.8
  34.4 0.7 collective-permute-start.9
  35.1 0.0 copy-done.1
  35.1 0.8 collective-permute-start.16
  35.9 0.0 collective-permute-done.5.head.refs_0_
  36.0 13.7 %collective-permute-start.11 = (f32[192,768]{1,0:T(8,128)S(1)}, f32[192,768]{1,0:T(8,128)S(1)}, u32[]{:S(2)}, u32[]{:S(2)}) collective-permute-start(f32[192,768]{1,0:T(8,128)S(1)} %collective-permute-done.6.refs_2_), channel_id=1, source_target_pairs={{0,4},{1,5},{2,6},{3,7},{4,0},{5,1},{6,2},{7,3},{8,12},{9,13},{10,... | collective-permute-start | bytes 1769480 | tf_op jit(solution)/shard_map/ppermute | solution.py:25
  49.7 0.0 collective-permute-done.9.refs_2_
  49.7 10.2 %collective-permute-start.10 = (f32[192,768]{1,0:T(8,128)S(1)}, f32[192,768]{1,0:T(8,128)S(1)}, u32[]{:S(2)}, u32[]{:S(2)}) collective-permute-start(f32[192,768]{1,0:T(8,128)S(1)} %collective-permute-done.2.refs_0_), channel_id=1, source_target_pairs={{0,4},{1,5},{2,6},{3,7},{4,0},{5,1},{6,2},{7,3},{8,12},{9,13},{10,... | collective-permute-start | bytes 1769480 | tf_op jit(solution)/shard_map/ppermute | solution.py:25
  59.9 0.0 collective-permute-done.8.tail.refs_4_
  59.9 0.0 collective-permute-start.17
  59.9 0.0 collective-permute-done.11.refs_3_
  59.9 1.6 %collective-permute-done.10.refs_1_ = f32[192,768]{1,0:T(8,128)S(1)} collective-permute-done((f32[192,768]{1,0:T(8,128)S(1)}, f32[192,768]{1,0:T(8,128)S(1)}, u32[]{:S(2)}, u32[]{:S(2)}) %collective-permute-start.10) | collective-permute-done | bytes 589856 | tf_op jit(solution)/shard_map/ppermute | solution.py:25
  61.5 5.7 %shard_map.87 = (bf16[768,768]{1,0:T(8,128)(2,1)S(1)}, bf16[768,768]{1,0:T(8,128)(2,1)S(1)}, bf16[2,4,768,256]{3,2,1,0:T(8,128)(2,1)S(1)}, bf16[2,4,768,256]{3,2,1,0:T(8,128)(2,1)S(1)}, f32[1,768]{1,0:T(1,128)S(1)}) custom-call(s32[2,4,256]{2,1,0:T(4,128)S(1)} %get-tuple-element.38.index, f32[192,768]{1,0:T(8,128)S(1)} %collective-permute-done.2.refs_0_, ...), custom_call_target="tpu_custom_call" | custom-call | bytes 1000 | tf_op jit(solution)/shard_map/pallas_call | solution.py:230
  67.2 0.0 collective-permute-done.7.refs_2_
  67.2 1.5 %collective-permute-start.18 = (f32[2,384,512]{2,1,0:T(8,128)S(1)}, f32[2,384,512]{2,1,0:T(8,128)S(1)}, u32[]{:S(2)}, u32[]{:S(2)}) collective-permute-start(f32[2,384,512]{2,1,0:T(8,128)S(1)} %collective-permute-done.7.refs_2_), channel_id=1, source_target_pairs={{0,4},{1,5},{2,6},{3,7},{4,0},{5,1},{6,2},{7,3},{8,12},{9,13},{10,... | collective-permute-start | bytes 4718600 | tf_op jit(solution)/shard_map/ppermute | solution.py:25
  68.8 1.3 %collective-permute-start.15 = (f32[288,768]{1,0:T(8,128)S(1)}, f32[288,768]{1,0:T(8,128)S(1)}, u32[]{:S(2)}, u32[]{:S(2)}) collective-permute-start(f32[288,768]{1,0:T(8,128)S(1)} %collective-permute-done.8.tail.refs_4_), channel_id=1, source_target_pairs={{0,2},{1,3},{2,0},{3,1},{4,6},{5,7},{6,4},{7,5},{8,10},{9,11},{10,... | collective-permute-start | bytes 2654216 | tf_op jit(solution)/shard_map/ppermute | solution.py:25
  70.0 0.0 collective-permute-start.13
  70.0 2.2 %collective-permute-done.13.refs_3_ = f32[96,768]{1,0:T(8,128)S(1)} collective-permute-done((f32[96,768]{1,0:T(8,128)S(1)}, f32[96,768]{1,0:T(8,128)S(1)}, u32[]{:S(2)}, u32[]{:S(2)}) %collective-permute-start.13) | collective-permute-done | bytes 294944 | tf_op jit(solution)/shard_map/ppermute | solution.py:25
  72.2 0.4 collective-permute-start.12
  72.6 1.2 %collective-permute-done.12.refs_1_ = f32[96,768]{1,0:T(8,128)S(1)} collective-permute-done((f32[96,768]{1,0:T(8,128)S(1)}, f32[96,768]{1,0:T(8,128)S(1)}, u32[]{:S(2)}, u32[]{:S(2)}) %collective-permute-start.12) | collective-permute-done | bytes 294944 | tf_op jit(solution)/shard_map/ppermute | solution.py:25
  73.8 0.4 collective-permute-start.14
  74.2 0.0 collective-permute-done.17.refs_1_
  74.2 0.0 collective-permute-done.18.refs_3_
  74.2 12.8 %shard_map.88 = (f32[2,384,512]{2,1,0:T(8,128)S(1)}, bf16[2,768,512]{2,1,0:T(8,128)(2,1)S(1)}, bf16[2,4,256,512]{3,2,1,0:T(8,128)(2,1)S(1)}, f32[2,512]{1,0:T(2,128)S(1)}) custom-call(s32[2,4,256]{2,1,0:T(4,128)S(1)} %get-tuple-element.38.index, bf16[2,4,768,256]{3,2,1,0:T(8,128)(2,1)S(1)} %get-tuple-element.41.pick_high, ...), custom_call_target="tpu_custom_call" | custom-call | bytes 1000 | tf_op jit(solution)/shard_map/pallas_call | solution.py:230
  87.0 0.0 collective-permute-done.16.border
  87.0 6.0 %shard_map.89 = (bf16[384,1536]{1,0:T(8,128)(2,1)S(1)}, f32[2,384,512]{2,1,0:T(8,128)S(1)}, f32[384,768]{1,0:T(8,128)S(1)}) custom-call(s32[2,4,256]{2,1,0:T(4,128)S(1)} %get-tuple-element.38.index, f32[384,1536]{1,0:T(8,128)S(1)} %collective-permute-done.16.border, f32[96,768]{1,0:T(8,128)S(1)} %collective-permute-done.5.head.refs_0_, ...), custom_call_target="tpu_custom_call" | custom-call | bytes 1000 | tf_op jit(solution)/shard_map/pallas_call | solution.py:230
  93.0 0.0 collective-permute-done.15.refs_6_
  93.0 0.2 collective-permute-start.19
  93.2 0.0 collective-permute-done.14.refs_5_
  93.2 2.3 %collective-permute-done.19.refs_7_ = f32[288,768]{1,0:T(8,128)S(1)} collective-permute-done((f32[288,768]{1,0:T(8,128)S(1)}, f32[288,768]{1,0:T(8,128)S(1)}, u32[]{:S(2)}, u32[]{:S(2)}) %collective-permute-start.19) | collective-permute-done | bytes 884768 | tf_op jit(solution)/shard_map/ppermute | solution.py:25
  95.5 3.5 %shard_map.90 = f32[1,1792]{1,0:T(1,128)S(1)} custom-call(f32[96,768]{1,0:T(8,128)S(1)} %collective-permute-done.5.head.refs_0_, f32[96,768]{1,0:T(8,128)S(1)} %collective-permute-done.12.refs_1_, f32[96,768]{1,0:T(8,128)S(1)} %collective-permute-done.9.refs_2_, f32[96,768]{1,0:T(8,128)S(1)} %collective-permute-done.13.refs_3_, ...), custom_call_target="tpu_custom_call" | custom-call | bytes 1000 | tf_op jit(solution)/shard_map/pallas_call | solution.py:230
  99.0 0.2 collective-permute-start.20
  99.3 1.0 collective-permute-done.20
  100.3 1.3 %collective-permute-start.21 = (f32[1,1792]{1,0:T(1,128)S(1)}, f32[1,1792]{1,0:T(1,128)S(1)}, u32[]{:S(2)}, u32[]{:S(2)}) collective-permute-start(f32[1,1792]{1,0:T(1,128)S(1)} %add.3.refs_0_), channel_id=1, source_target_pairs={{0,2},{1,3},{2,0},{3,1},{4,6},{5,7},{6,4},{7,5},{8,10},{9,11},{10,... | collective-permute-start | bytes 21512 | tf_op jit(solution)/shard_map/ppermute | solution.py:25
  101.6 0.0 collective-permute-start.22
  101.6 2.2 %collective-permute-start.23 = (f32[1,1792]{1,0:T(1,128)S(1)}, f32[1,1792]{1,0:T(1,128)S(1)}, u32[]{:S(2)}, u32[]{:S(2)}) collective-permute-start(f32[1,1792]{1,0:T(1,128)S(1)} %add.3.refs_0_), channel_id=1, source_target_pairs={{0,3},{1,2},{2,1},{3,0},{4,7},{5,6},{6,5},{7,4},{8,11},{9,10},{10,... | collective-permute-start | bytes 21512 | tf_op jit(solution)/shard_map/ppermute | solution.py:25
  103.8 0.2 collective-permute-done.21.refs_1_
  104.0 1.3 %collective-permute-done.22.refs_2_ = f32[1,1792]{1,0:T(1,128)S(1)} collective-permute-done((f32[1,1792]{1,0:T(1,128)S(1)}, f32[1,1792]{1,0:T(1,128)S(1)}, u32[]{:S(2)}, u32[]{:S(2)}) %collective-permute-start.22) | collective-permute-done | bytes 7200 | tf_op jit(solution)/shard_map/ppermute | solution.py:25
  105.3 0.9 collective-permute-done.23.refs_3_
  106.2 1.3 %shard_map.91 = (f32[1,768]{1,0:T(1,128)}, f32[2,512]{1,0:T(2,128)}) custom-call(s32[16]{0:T(128)} %parent_ref.3, f32[1,1792]{1,0:T(1,128)S(1)} %add.3.refs_0_, f32[1,1792]{1,0:T(1,128)S(1)} %collective-permute-done.21.refs_1_, f32[1,1792]{1,0:T(1,128)S(1)} %collective-permute-done.22.refs_2_, f32[1,1792]{1,0:T(1,128)S(1)} %collective-permute-done.23.refs_3_), custom_call_target="tpu_custom_call" | custom-call | bytes 1000 | tf_op jit(solution)/shard_map/pallas_call | solution.py:230
  (1 shorter events, 0.0 us)
Async XLA Ops:
  0.6 9.2 %collective-permute-start = (f32[2,256,512]{2,1,0:T(8,128)}, f32[2,256,512]{2,1,0:T(8,128)S(1)}, u32[]{:S(2)}, u32[]{:S(2)}) collective-permute-start(f32[2,256,512]{2,1,0:T(8,128)} %own_rows.1), channel_id=1, source_target_pairs={{0,4},{1,5},{2,6},{3,7},{4,0},{5,1},{6,2},{7,3},{8,12},{9,13},{10,... | collective-permute-start | bytes 3145736 | tf_op jit(solution)/shard_map/ppermute | solution.py:25
  1.1 14.6 %collective-permute-start.2 = (f32[192,768]{1,0:T(8,128)}, f32[192,768]{1,0:T(8,128)S(1)}, u32[]{:S(2)}, u32[]{:S(2)}) collective-permute-start(f32[192,768]{1,0:T(8,128)} %bitcast.7), channel_id=1, source_target_pairs={{0,0},{1,4},{2,2},{3,6},{4,1},{5,5},{6,3},{7,7},{8,8},{9,12},{10,1... | collective-permute-start | bytes 1769480 | tf_op jit(solution)/shard_map/ppermute | solution.py:35
  2.9 6.9 %collective-permute-start.1 = (f32[2,128,512]{2,1,0:T(8,128)}, f32[2,128,512]{2,1,0:T(8,128)S(1)}, u32[]{:S(2)}, u32[]{:S(2)}) collective-permute-start(f32[2,128,512]{2,1,0:T(8,128)} %own_inverse.1), channel_id=1, source_target_pairs={{0,4},{1,5},{2,6},{3,7},{4,0},{5,1},{6,2},{7,3},{8,12},{9,13},{10,... | collective-permute-start | bytes 1572872 | tf_op jit(solution)/shard_map/ppermute | solution.py:25
  6.7 9.0 %collective-permute-start.3 = (f32[96,768]{1,0:T(8,128)S(1)}, f32[96,768]{1,0:T(8,128)S(1)}, u32[]{:S(2)}, u32[]{:S(2)}) collective-permute-start(f32[96,768]{1,0:T(8,128)S(1)} %slice_bitcast_fusion.1), channel_id=1, source_target_pairs={{0,2},{1,3},{2,0},{3,1},{4,6},{5,7},{6,4},{7,5},{8,10},{9,11},{10,... | collective-permute-start | bytes 884744 | tf_op jit(solution)/shard_map/ppermute | solution.py:25
  9.8 23.2 %copy-start = (f32[1,384,768]{2,1,0:T(8,128)S(1)}, f32[1,384,768]{2,1,0:T(8,128)}, u32[]{:S(2)}) copy-start(f32[1,384,768]{2,1,0:T(8,128)} %param.8) | copy-start | bytes 3538948
  9.8 25.3 %copy-start.1 = (f32[1,384,1536]{2,1,0:T(8,128)S(1)}, f32[1,384,1536]{2,1,0:T(8,128)}, u32[]{:S(2)}) copy-start(f32[1,384,1536]{2,1,0:T(8,128)} %param.7) | copy-start | bytes 7077892
  15.7 15.9 %collective-permute-start.4 = (f32[2,384,512]{2,1,0:T(8,128)S(1)}, f32[2,384,512]{2,1,0:T(8,128)S(1)}, u32[]{:S(2)}, u32[]{:S(2)}) collective-permute-start(f32[2,384,512]{2,1,0:T(8,128)S(1)} %get-tuple-element.32), channel_id=1, source_target_pairs={{0,0},{1,4},{2,2},{3,6},{4,1},{5,5},{6,3},{7,7},{8,8},{9,12},{10,1... | collective-permute-start | bytes 4718600 | tf_op jit(solution)/shard_map/ppermute | solution.py:35
  16.5 15.2 %collective-permute-start.6 = (f32[192,768]{1,0:T(8,128)S(1)}, f32[192,768]{1,0:T(8,128)S(1)}, u32[]{:S(2)}, u32[]{:S(2)}) collective-permute-start(f32[192,768]{1,0:T(8,128)S(1)} %collective-permute-done.2.refs_0_), channel_id=1, source_target_pairs={{0,2},{1,3},{2,0},{3,1},{4,6},{5,7},{6,4},{7,5},{8,10},{9,11},{10,... | collective-permute-start | bytes 1769480 | tf_op jit(solution)/shard_map/ppermute | solution.py:25
  31.7 35.5 %collective-permute-start.7 = (f32[2,384,512]{2,1,0:T(8,128)S(1)}, f32[2,384,512]{2,1,0:T(8,128)S(1)}, u32[]{:S(2)}, u32[]{:S(2)}) collective-permute-start(f32[2,384,512]{2,1,0:T(8,128)S(1)} %collective-permute-done.4.refs_0_), channel_id=1, source_target_pairs={{0,2},{1,3},{2,0},{3,1},{4,6},{5,7},{6,4},{7,5},{8,10},{9,11},{10,... | collective-permute-start | bytes 4718600 | tf_op jit(solution)/shard_map/ppermute | solution.py:25
  33.0 2.9 %collective-permute-start.5 = (f32[96,768]{1,0:T(8,128)S(1)}, f32[96,768]{1,0:T(8,128)S(1)}, u32[]{:S(2)}, u32[]{:S(2)}) collective-permute-start(f32[96,768]{1,0:T(8,128)S(1)} %slice_bitcast_fusion.1), channel_id=1, source_target_pairs={{0,0},{1,4},{2,2},{3,6},{4,1},{5,5},{6,3},{7,7},{8,8},{9,12},{10,1... | collective-permute-start | bytes 884744 | tf_op jit(solution)/shard_map/ppermute | solution.py:35
  33.7 26.2 %collective-permute-start.8 = (f32[288,768]{1,0:T(8,128)S(1)}, f32[288,768]{1,0:T(8,128)S(1)}, u32[]{:S(2)}, u32[]{:S(2)}) collective-permute-start(f32[288,768]{1,0:T(8,128)S(1)} %slice_bitcast_fusion), channel_id=1, source_target_pairs={{0,0},{1,4},{2,2},{3,6},{4,1},{5,5},{6,3},{7,7},{8,8},{9,12},{10,1... | collective-permute-start | bytes 2654216 | tf_op jit(solution)/shard_map/ppermute | solution.py:35
  34.4 15.3 %collective-permute-start.9 = (f32[96,768]{1,0:T(8,128)S(1)}, f32[96,768]{1,0:T(8,128)S(1)}, u32[]{:S(2)}, u32[]{:S(2)}) collective-permute-start(f32[96,768]{1,0:T(8,128)S(1)} %collective-permute-done.3), channel_id=1, source_target_pairs={{0,0},{1,4},{2,2},{3,6},{4,1},{5,5},{6,3},{7,7},{8,8},{9,12},{10,1... | collective-permute-start | bytes 884744 | tf_op jit(solution)/shard_map/ppermute | solution.py:35
  35.1 51.9 %collective-permute-start.16 = (f32[384,1536]{1,0:T(8,128)S(1)}, f32[384,1536]{1,0:T(8,128)S(1)}, u32[]{:S(2)}, u32[]{:S(2)}) collective-permute-start(f32[384,1536]{1,0:T(8,128)S(1)} %bitcast.6), channel_id=1, source_target_pairs={{0,0},{1,4},{2,2},{3,6},{4,1},{5,5},{6,3},{7,7},{8,8},{9,12},{10,1... | collective-permute-start | bytes 7077896 | tf_op jit(solution)/shard_map/ppermute | solution.py:35
  36.0 23.9 %collective-permute-start.11 = (f32[192,768]{1,0:T(8,128)S(1)}, f32[192,768]{1,0:T(8,128)S(1)}, u32[]{:S(2)}, u32[]{:S(2)}) collective-permute-start(f32[192,768]{1,0:T(8,128)S(1)} %collective-permute-done.6.refs_2_), channel_id=1, source_target_pairs={{0,4},{1,5},{2,6},{3,7},{4,0},{5,1},{6,2},{7,3},{8,12},{9,13},{10,... | collective-permute-start | bytes 1769480 | tf_op jit(solution)/shard_map/ppermute | solution.py:25
  49.7 11.8 %collective-permute-start.10 = (f32[192,768]{1,0:T(8,128)S(1)}, f32[192,768]{1,0:T(8,128)S(1)}, u32[]{:S(2)}, u32[]{:S(2)}) collective-permute-start(f32[192,768]{1,0:T(8,128)S(1)} %collective-permute-done.2.refs_0_), channel_id=1, source_target_pairs={{0,4},{1,5},{2,6},{3,7},{4,0},{5,1},{6,2},{7,3},{8,12},{9,13},{10,... | collective-permute-start | bytes 1769480 | tf_op jit(solution)/shard_map/ppermute | solution.py:25
  59.9 14.3 %collective-permute-start.17 = (f32[2,384,512]{2,1,0:T(8,128)S(1)}, f32[2,384,512]{2,1,0:T(8,128)S(1)}, u32[]{:S(2)}, u32[]{:S(2)}) collective-permute-start(f32[2,384,512]{2,1,0:T(8,128)S(1)} %collective-permute-done.4.refs_0_), channel_id=1, source_target_pairs={{0,4},{1,5},{2,6},{3,7},{4,0},{5,1},{6,2},{7,3},{8,12},{9,13},{10,... | collective-permute-start | bytes 4718600 | tf_op jit(solution)/shard_map/ppermute | solution.py:25
  67.2 7.0 %collective-permute-start.18 = (f32[2,384,512]{2,1,0:T(8,128)S(1)}, f32[2,384,512]{2,1,0:T(8,128)S(1)}, u32[]{:S(2)}, u32[]{:S(2)}) collective-permute-start(f32[2,384,512]{2,1,0:T(8,128)S(1)} %collective-permute-done.7.refs_2_), channel_id=1, source_target_pairs={{0,4},{1,5},{2,6},{3,7},{4,0},{5,1},{6,2},{7,3},{8,12},{9,13},{10,... | collective-permute-start | bytes 4718600 | tf_op jit(solution)/shard_map/ppermute | solution.py:25
  68.8 24.2 %collective-permute-start.15 = (f32[288,768]{1,0:T(8,128)S(1)}, f32[288,768]{1,0:T(8,128)S(1)}, u32[]{:S(2)}, u32[]{:S(2)}) collective-permute-start(f32[288,768]{1,0:T(8,128)S(1)} %collective-permute-done.8.tail.refs_4_), channel_id=1, source_target_pairs={{0,2},{1,3},{2,0},{3,1},{4,6},{5,7},{6,4},{7,5},{8,10},{9,11},{10,... | collective-permute-start | bytes 2654216 | tf_op jit(solution)/shard_map/ppermute | solution.py:25
  70.0 2.2 %collective-permute-start.13 = (f32[96,768]{1,0:T(8,128)S(1)}, f32[96,768]{1,0:T(8,128)S(1)}, u32[]{:S(2)}, u32[]{:S(2)}) collective-permute-start(f32[96,768]{1,0:T(8,128)S(1)} %collective-permute-done.9.refs_2_), channel_id=1, source_target_pairs={{0,4},{1,5},{2,6},{3,7},{4,0},{5,1},{6,2},{7,3},{8,12},{9,13},{10,... | collective-permute-start | bytes 884744 | tf_op jit(solution)/shard_map/ppermute | solution.py:25
  72.2 1.6 %collective-permute-start.12 = (f32[96,768]{1,0:T(8,128)S(1)}, f32[96,768]{1,0:T(8,128)S(1)}, u32[]{:S(2)}, u32[]{:S(2)}) collective-permute-start(f32[96,768]{1,0:T(8,128)S(1)} %collective-permute-done.5.head.refs_0_), channel_id=1, source_target_pairs={{0,4},{1,5},{2,6},{3,7},{4,0},{5,1},{6,2},{7,3},{8,12},{9,13},{10,... | collective-permute-start | bytes 884744 | tf_op jit(solution)/shard_map/ppermute | solution.py:25
  73.8 19.4 %collective-permute-start.14 = (f32[288,768]{1,0:T(8,128)S(1)}, f32[288,768]{1,0:T(8,128)S(1)}, u32[]{:S(2)}, u32[]{:S(2)}) collective-permute-start(f32[288,768]{1,0:T(8,128)S(1)} %collective-permute-done.8.tail.refs_4_), channel_id=1, source_target_pairs={{0,4},{1,5},{2,6},{3,7},{4,0},{5,1},{6,2},{7,3},{8,12},{9,13},{10,... | collective-permute-start | bytes 2654216 | tf_op jit(solution)/shard_map/ppermute | solution.py:25
  93.0 2.5 %collective-permute-start.19 = (f32[288,768]{1,0:T(8,128)S(1)}, f32[288,768]{1,0:T(8,128)S(1)}, u32[]{:S(2)}, u32[]{:S(2)}) collective-permute-start(f32[288,768]{1,0:T(8,128)S(1)} %collective-permute-done.15.refs_6_), channel_id=1, source_target_pairs={{0,4},{1,5},{2,6},{3,7},{4,0},{5,1},{6,2},{7,3},{8,12},{9,13},{10,... | collective-permute-start | bytes 2654216 | tf_op jit(solution)/shard_map/ppermute | solution.py:25
  99.0 1.2 %collective-permute-start.20 = (f32[1,1792]{1,0:T(1,128)S(1)}, f32[1,1792]{1,0:T(1,128)S(1)}, u32[]{:S(2)}, u32[]{:S(2)}) collective-permute-start(f32[1,1792]{1,0:T(1,128)S(1)} %shard_map.90), channel_id=1, source_target_pairs={{0,4},{1,5},{2,6},{3,7},{4,0},{5,1},{6,2},{7,3},{8,12},{9,13},{10,... | collective-permute-start | bytes 21512 | tf_op jit(solution)/shard_map/ppermute | solution.py:25
  100.3 3.7 %collective-permute-start.21 = (f32[1,1792]{1,0:T(1,128)S(1)}, f32[1,1792]{1,0:T(1,128)S(1)}, u32[]{:S(2)}, u32[]{:S(2)}) collective-permute-start(f32[1,1792]{1,0:T(1,128)S(1)} %add.3.refs_0_), channel_id=1, source_target_pairs={{0,2},{1,3},{2,0},{3,1},{4,6},{5,7},{6,4},{7,5},{8,10},{9,11},{10,... | collective-permute-start | bytes 21512 | tf_op jit(solution)/shard_map/ppermute | solution.py:25
  101.6 3.6 %collective-permute-start.22 = (f32[1,1792]{1,0:T(1,128)S(1)}, f32[1,1792]{1,0:T(1,128)S(1)}, u32[]{:S(2)}, u32[]{:S(2)}) collective-permute-start(f32[1,1792]{1,0:T(1,128)S(1)} %add.3.refs_0_), channel_id=1, source_target_pairs={{0,1},{1,0},{2,3},{3,2},{4,5},{5,4},{6,7},{7,6},{8,9},{9,8},{10,11... | collective-permute-start | bytes 21512 | tf_op jit(solution)/shard_map/ppermute | solution.py:25
  101.6 4.5 %collective-permute-start.23 = (f32[1,1792]{1,0:T(1,128)S(1)}, f32[1,1792]{1,0:T(1,128)S(1)}, u32[]{:S(2)}, u32[]{:S(2)}) collective-permute-start(f32[1,1792]{1,0:T(1,128)S(1)} %add.3.refs_0_), channel_id=1, source_target_pairs={{0,3},{1,2},{2,1},{3,0},{4,7},{5,6},{6,5},{7,4},{8,11},{9,10},{10,... | collective-permute-start | bytes 21512 | tf_op jit(solution)/shard_map/ppermute | solution.py:25

commit v2 on v1

--- a/solution.py
+++ b/solution.py
@@ -97,9 +97,15 @@
 
     owner, block = place_of()
     _, ids = kids_of(parent_ref, owner)
+    pieces, width = index_out.shape[1:]
     for place, kid in enumerate(ids):
-        for mask in range(index_out.shape[1]):
-            index_out[place, mask : mask + 1, :] = index_ref[kid, pl.ds(block ^ mask, 1), :]
+        row = index_ref[pl.ds(kid, 1), :]
+        parts = [row[:, start : start + width] for start in range(0, pieces * width, width)]
+        for mask in range(pieces):
+            part = parts[0]
+            for at in range(1, pieces):
+                part = jnp.where((block ^ mask) == at, parts[at], part)
+            index_out[place, mask : mask + 1, :] = part
 
 
 def picks(index, first, rows):
@@ -125,14 +131,16 @@
             pick_low[kid, mask] = rounded(dot(diag_low[...], pick))
 
 
-def kid_kernel(pieces, index, pick_high, pick_low, head, tail, *refs):
+def kid_kernel(pieces, index, pick_high, pick_low, factor, diag_high, diag_low, *refs):
     kids = refs[:pieces]
-    reduced, lift_high, kid_high, kid_sum, inv_high, inv_low, lifted = refs[pieces:]
+    reduced, lift_high, lower_high, weights, kid_sum, inv_high, inv_low, lifted, lower = refs[pieces:]
     _, block = place_of()
-    size, own_border = lifted.shape[0], head.shape[0] + tail.shape[0]
-    kid_block = kid_high.shape[2]
+    size, own_border, border_size = lifted.shape[0], factor.shape[0], lower.shape[0]
+    kid_block = index.shape[2]
     inv_block, own_rows = kids[0].shape[1] - kid_block, size // pieces
-    factor_high = jnp.concatenate([rounded(head[...]), rounded(tail[...])], axis=0)
+    factor_halves = halves(factor[...])
+    for span in spans(size):
+        weights[:, span] = product(factor_halves, (diag_high[:, span], diag_low[:, span]))
     for kid in range(2):
         own_inverse = kids[0][kid, kid_block:]
         for mask in range(pieces):
@@ -143,48 +151,39 @@
         inverse = inv_high[...], inv_low[...]
         for mask in range(pieces):
             weight = halves(product(halves(kids[mask][kid, :kid_block]), inverse))
-            kid_high[kid, mask] = weight[0]
             lifted_part = product((pick_high[kid, mask], pick_low[kid, mask]), weight)
             pick = picks(index[kid, mask : mask + 1, :], size + block * own_border, own_border)
             lower_part = dot(pick, weight[0]) + dot(pick, weight[1])
             lifted[...] = lifted_part if mask == 0 else lifted[...] + lifted_part
             reduced[kid] = lower_part if mask == 0 else reduced[kid] + lower_part
+            part = dot(picks(index[kid, mask : mask + 1, :], size, border_size), weight[0])
+            lower[...] = part if mask == 0 else lower[...] + part
         own = lifted[pl.ds(pl.multiple_of(block * own_rows, 16), own_rows), :]
         kid_sum[kid : kid + 1] = column_sum(own_inverse * own_inverse) + column_sum(own * own)
         lift_high[kid] = rounded(lifted[...])
-        reduced[kid] = reduced[kid] - dot(factor_high, lift_high[kid])
-
-
-def border_kernel(index, border, head, tail, diag_high, diag_low, kid_high, border_high, border_lower, weights):
+        lower_high[kid] = rounded(lower[...])
+        reduced[kid] = reduced[kid] - dot(factor_halves[0], lift_high[kid])
+
+
+def border_kernel(border, lower_high, border_high, border_lower):
     border_high[...] = rounded(border[...])
-    size, border_size = head.shape[1], border.shape[1]
     for kid in range(2):
-        for mask in range(kid_high.shape[1]):
-            pick = picks(index[kid, mask : mask + 1, :], size, border_size)
-            rows = rounded(dot(border_high[...], pick))
-            part = dot(rows, kid_high[kid, mask])
-            border_lower[kid] = part if mask == 0 else border_lower[kid] + part
-    for part, start in ((head, 0), (tail, head.shape[0])):
-        part_halves = halves(part[...])
-        rows = slice(start, start + part.shape[0])
-        for span in spans(size):
-            weights[rows, span] = product(part_halves, (diag_high[:, span], diag_low[:, span]))
+        for span in spans(lower_high.shape[2]):
+            border_lower[kid, :, span] = dot(border_high[...], lower_high[kid, :, span])
 
 
 def image_kernel(pieces, *refs):
-    heads, tails = refs[:pieces], refs[pieces : 2 * pieces]
+    factor = refs[:pieces]
     border_high, border_lower, weights, reduced, lift_high, diag_high, diag_low, parent_sum, kid_sum, out = refs[
-        2 * pieces : 2 * pieces + 10
+        pieces : pieces + 10
     ]
-    factor_high, fold_high, fold_low = refs[2 * pieces + 10 :]
+    factor_high, fold_high, fold_low = refs[pieces + 10 :]
     _, block = place_of()
-    head, size = heads[0].shape
-    tail = tails[0].shape[0]
+    own_border, size = factor[0].shape
     kid_size = reduced.shape[2]
     for mask in range(pieces):
-        start = pl.multiple_of((block ^ mask) * (head + tail), 16)
-        factor_high[pl.ds(start, head), :] = rounded(heads[mask][...])
-        factor_high[pl.ds(pl.multiple_of(start + head, 16), tail), :] = rounded(tails[mask][...])
+        start = pl.multiple_of((block ^ mask) * own_border, 16)
+        factor_high[pl.ds(start, own_border), :] = rounded(factor[mask][...])
     for span in spans(size):
         fold_high[:, span], fold_low[:, span] = halves(dot(border_high[...], factor_high[:, span]))
     fold = fold_high[...], fold_low[...]
@@ -265,27 +264,21 @@
         return [parts[mask] for mask in range(pieces)]
 
     last = pieces - 2
-    head = -(-own_border // 64) * 16
-    factor_head, factor_tail = factor[:head], factor[head:]
-    raw_heads = over_fronts(factor_head)
+    raw_diagonal = over_fronts(diagonal)
     own_diagonal = cross(diagonal)
-    index = child_index.reshape(child_index.shape[0], pieces, kid_block)
     kid_shape = (2, kid_block + kid_inverse.shape[1], kid_size)
     own_kids, index = call(
-        select_kernel,
-        (shape_of(kid_shape), shape_of((2, pieces, kid_block), jnp.int32)),
-        6,
-        scalars=1,
-        loose=4,
-    )(child_parent, index, kid_rows, kid_inverse, exchange(kid_rows, 1, 0), exchange(kid_inverse, 1, 0))
-    own_kids = cross(after(own_kids, own_diagonal, raw_heads[last]))
-    own_tail = cross(after(factor_tail, own_kids))
-    heads = {mask: cross(after(value, own_kids)) for mask, value in raw_heads.items()}
-    own_border_rows = cross(after(border, own_kids))
-
-    diagonal_parts = over_fronts(own_diagonal)
-    kid_parts = over_fronts(after(own_kids, diagonal_parts[last]))
-    diagonal_parts = spread(diagonal_parts, [own_kids], [own_kids])
+        select_kernel, (shape_of(kid_shape), shape_of((2, pieces, kid_block), jnp.int32)), 6, scalars=1, loose=4
+    )(child_parent, child_index, kid_rows, kid_inverse, exchange(kid_rows, 1, 0), exchange(kid_inverse, 1, 0))
+    own_kids = cross(after(own_kids, own_diagonal, raw_diagonal[last]))
+
+    diagonal_parts = {mask: cross(after(value, own_kids)) for mask, value in raw_diagonal.items() if mask}
+    crossed = diagonal_parts[last]
+    diagonal_parts = spread({0: own_diagonal} | diagonal_parts, [own_kids], [own_kids])
+    own_factor = cross(after(factor, own_kids))
+    own_border_rows = cross(after(border, crossed))
+    kid_parts = over_fronts(own_kids)
+
     diag_high, diag_low, pick_high, pick_low, parent_sum = call(
         functools.partial(diagonal_kernel, pieces),
         (
@@ -296,37 +289,35 @@
             shape_of((1, size)),
         ),
         10,
-    )(after(index, own_tail, *heads.values()), *diagonal_parts)
+    )(index, *diagonal_parts)
     kids_here = after(kid_parts[last], pick_high)
-    tails = over_fronts(after(own_tail, kids_here))
-    tails[0] = own_tail
+    factor_parts = over_fronts(after(own_factor, kids_here))
+    factor_parts[0] = own_factor
     kid_parts = spread(kid_parts, [], [pick_high])
-    own_head = heads[0]
-    heads = spread(heads, [kids_here], [kids_here])
-
-    reduced, lift_high, kid_high, kid_sum = call(
+
+    reduced, lift_high, lower_high, weights, kid_sum = call(
         functools.partial(kid_kernel, pieces),
         (
             shape_of((2, own_border, kid_size)),
             shape_of((2, size, kid_size), half),
-            shape_of((2, pieces, kid_block, kid_size), half),
+            shape_of((2, border_size, kid_size), half),
+            shape_of((own_border, size)),
             shape_of((2, kid_size)),
         ),
-        12,
+        20,
         scratch=[
             pltpu.VMEM((kid_size, kid_size), half),
             pltpu.VMEM((kid_size, kid_size), half),
             pltpu.VMEM((size, kid_size), jnp.float32),
+            pltpu.VMEM((border_size, kid_size), jnp.float32),
         ],
-    )(index, pick_high, pick_low, own_head, after(own_tail, *heads), *kid_parts)
-
-    border_high, border_lower, weights = call(
-        border_kernel,
-        (shape_of(border.shape, half), shape_of((2, own_border, kid_size)), shape_of((own_border, size))),
-        12,
-    )(index, own_border_rows, own_head, own_tail, diag_high, diag_low, kid_high)
-
-    tails = spread(tails, [kids_here], [border_lower])
+    )(index, pick_high, pick_low, own_factor, diag_high, diag_low, *kid_parts)
+
+    border_high, border_lower = call(
+        border_kernel, (shape_of(border.shape, half), shape_of((2, own_border, kid_size))), 8
+    )(own_border_rows, lower_high)
+
+    factor_parts = spread(factor_parts, [kids_here], [border_lower])
     total = call(
         functools.partial(image_kernel, pieces),
         shape_of((1, size + 2 * kid_size)),
@@ -337,8 +328,7 @@
             pltpu.VMEM((own_border, size), half),
         ],
     )(
-        *heads,
-        *tails,
+        *factor_parts,
         border_high,
         border_lower,
         weights,

time: 108 us -> 110 us (1.019)
  starting transfers between devices: 44.7 us -> 50.9 us
  local copies, waits for them, and re-layouts: 2.53 us -> 0.01 us
  waiting for transfers between devices: 28.5 us -> 26.9 us
    ppermute x18 -> x15, starting transfers between devices: 39.3 us -> 44.9 us  [exchange(): return lax.ppermute(value, ('leaf', 'front'), pairs)]
    ppermute x18 -> x15, waiting for transfers between devices: 28.5 us -> 26.9 us  [exchange(): return lax.ppermute(value, ('leaf', 'front'), pairs)]
    reshape x1 -> x0, local copies, waits for them, and re-layouts: 1.48 us -> none  [shards(): index = child_index.reshape(child_index.shape[0], pieces, kid_block)]
    ppermute x6 -> x5, starting transfers between devices: 5.35 us -> 6.01 us  [cross(): return lax.ppermute(value, ('leaf', 'front'), pairs)]
  transfers between devices with their start and end apart: 24 -> 20, of which waited for: 10 -> 11; matrix products, arithmetic and copies ran while one was open for 2% -> 0% of each run, Pallas kernels for 24% -> 24%
where the time goes in v2:
time: 110 us; the launch traced here: 109 us
  starting transfers between devices  50.9 us (46%)
  Pallas kernels  30.8 us (28%)
  waiting for transfers between devices  26.9 us (24%)
    ppermute x15, starting transfers between devices, exchange(): return lax.ppermute(value, ('leaf', 'front'), pairs)  44.9 us
    pallas_call x6, Pallas kernels, run(): pl.pallas_call(kernel, out_shape=results, in_specs=specs, out_specs=jax.t...  30.8 us
    ppermute x15, waiting for transfers between devices, exchange(): return lax.ppermute(value, ('leaf', 'front'), pairs)  26.9 us
    ppermute x5, starting transfers between devices, cross(): return lax.ppermute(value, ('leaf', 'front'), pairs)  6.01 us
  transfers between devices with their start and end apart: 20, of which 11 were waited for; matrix products, arithmetic and copies ran while one was open for 0% of the time, Pallas kernels for 24%

profile of v2, /device:TPU:0, one launch (start us, length us, event | category | flops | bytes accessed | tf_op | source)
XLA Modules:
  0.0 109.3 jit_solution(15526677814176821344)
XLA Ops:
  0.6 0.5 collective-permute-start
  1.1 0.0 copy-start
  1.2 1.8 %collective-permute-start.2 = (f32[192,768]{1,0:T(8,128)}, f32[192,768]{1,0:T(8,128)S(1)}, u32[]{:S(2)}, u32[]{:S(2)}) collective-permute-start(f32[192,768]{1,0:T(8,128)} %bitcast.5), channel_id=1, source_target_pairs={{0,0},{1,4},{2,2},{3,6},{4,1},{5,5},{6,3},{7,7},{8,8},{9,12},{10,1... | collective-permute-start | bytes 1769480 | tf_op jit(solution)/shard_map/ppermute | solution.py:35
  3.0 2.5 %collective-permute-start.3 = (f32[192,768]{1,0:T(8,128)}, f32[192,768]{1,0:T(8,128)S(1)}, u32[]{:S(2)}, u32[]{:S(2)}) collective-permute-start(f32[192,768]{1,0:T(8,128)} %bitcast.6), channel_id=1, source_target_pairs={{0,2},{1,3},{2,0},{3,1},{4,6},{5,7},{6,4},{7,5},{8,10},{9,11},{10,... | collective-permute-start | bytes 1769480 | tf_op jit(solution)/shard_map/ppermute | solution.py:25
  5.5 1.6 %collective-permute-start.1 = (f32[2,128,512]{2,1,0:T(8,128)}, f32[2,128,512]{2,1,0:T(8,128)S(1)}, u32[]{:S(2)}, u32[]{:S(2)}) collective-permute-start(f32[2,128,512]{2,1,0:T(8,128)} %own_inverse.1), channel_id=1, source_target_pairs={{0,4},{1,5},{2,6},{3,7},{4,0},{5,1},{6,2},{7,3},{8,12},{9,13},{10,... | collective-permute-start | bytes 1572872 | tf_op jit(solution)/shard_map/ppermute | solution.py:25
  7.1 1.7 %collective-permute-done.1.other_inverse = f32[2,128,512]{2,1,0:T(8,128)S(1)} collective-permute-done((f32[2,128,512]{2,1,0:T(8,128)}, f32[2,128,512]{2,1,0:T(8,128)S(1)}, u32[]{:S(2)}, u32[]{:S(2)}) %collective-permute-start.1) | collective-permute-done | bytes 524320 | tf_op jit(solution)/shard_map/ppermute | solution.py:25
  8.9 0.0 collective-permute-done.other_rows
  8.9 1.6 %shard_map.86 = (f32[2,384,512]{2,1,0:T(8,128)S(1)}, s32[2,4,256]{2,1,0:T(4,128)S(1)}) custom-call(s32[16]{0:T(128)} %parent_ref.3, s32[16,1024]{1,0:T(8,128)} %index_ref.1, f32[2,256,512]{2,1,0:T(8,128)} %own_rows.1, f32[2,128,512]{2,1,0:T(8,128)} %own_inverse.1, f32[2,256,512]{2,1,0:T(8,128)S(1)} %collective-permute-done.other_rows, ...), custom_call_target="tpu_custom_call" | custom-call | bytes 1000 | tf_op jit(solution)/shard_map/pallas_call | solution.py:229
  10.4 0.0 collective-permute-done.2.refs_0_
  10.5 8.2 %collective-permute-done.3 = f32[192,768]{1,0:T(8,128)S(1)} collective-permute-done((f32[192,768]{1,0:T(8,128)}, f32[192,768]{1,0:T(8,128)S(1)}, u32[]{:S(2)}, u32[]{:S(2)}) %collective-permute-start.3) | collective-permute-done | bytes 589856 | tf_op jit(solution)/shard_map/ppermute | solution.py:25
  18.7 0.7 collective-permute-start.4
  19.5 0.0 collective-permute-done.4.refs_0_
  19.5 2.4 %collective-permute-start.6 = (f32[2,384,512]{2,1,0:T(8,128)S(1)}, f32[2,384,512]{2,1,0:T(8,128)S(1)}, u32[]{:S(2)}, u32[]{:S(2)}) collective-permute-start(f32[2,384,512]{2,1,0:T(8,128)S(1)} %collective-permute-done.4.refs_0_), channel_id=1, source_target_pairs={{0,2},{1,3},{2,0},{3,1},{4,6},{5,7},{6,4},{7,5},{8,10},{9,11},{10,... | collective-permute-start | bytes 4718600 | tf_op jit(solution)/shard_map/ppermute | solution.py:25
  21.9 0.7 collective-permute-start.8
  22.6 1.9 %collective-permute-start.5 = (f32[384,768]{1,0:T(8,128)}, f32[384,768]{1,0:T(8,128)S(1)}, u32[]{:S(2)}, u32[]{:S(2)}) collective-permute-start(f32[384,768]{1,0:T(8,128)} %bitcast.4), channel_id=1, source_target_pairs={{0,0},{1,4},{2,2},{3,6},{4,1},{5,5},{6,3},{7,7},{8,8},{9,12},{10,1... | collective-permute-start | bytes 3538952 | tf_op jit(solution)/shard_map/ppermute | solution.py:35
  24.5 0.0 collective-permute-done.8.refs_2_
  24.5 0.0 copy-done
  24.5 0.8 collective-permute-start.12
  25.3 32.6 %collective-permute-start.7 = (f32[192,768]{1,0:T(8,128)S(1)}, f32[192,768]{1,0:T(8,128)S(1)}, u32[]{:S(2)}, u32[]{:S(2)}) collective-permute-start(f32[192,768]{1,0:T(8,128)S(1)} %collective-permute-done.2.refs_0_), channel_id=1, source_target_pairs={{0,4},{1,5},{2,6},{3,7},{4,0},{5,1},{6,2},{7,3},{8,12},{9,13},{10,... | collective-permute-start | bytes 1769480 | tf_op jit(solution)/shard_map/ppermute | solution.py:25
  58.0 0.1 collective-permute-start.9
  58.0 1.6 %collective-permute-done.7.refs_1_ = f32[192,768]{1,0:T(8,128)S(1)} collective-permute-done((f32[192,768]{1,0:T(8,128)S(1)}, f32[192,768]{1,0:T(8,128)S(1)}, u32[]{:S(2)}, u32[]{:S(2)}) %collective-permute-start.7) | collective-permute-done | bytes 589856 | tf_op jit(solution)/shard_map/ppermute | solution.py:25
  59.6 0.4 collective-permute-start.13
  60.0 0.5 collective-permute-done.9.refs_3_
  60.4 5.7 %shard_map.87 = (bf16[768,768]{1,0:T(8,128)(2,1)S(1)}, bf16[768,768]{1,0:T(8,128)(2,1)S(1)}, bf16[2,4,768,256]{3,2,1,0:T(8,128)(2,1)S(1)}, bf16[2,4,768,256]{3,2,1,0:T(8,128)(2,1)S(1)}, f32[1,768]{1,0:T(1,128)S(1)}) custom-call(s32[2,4,256]{2,1,0:T(4,128)S(1)} %get-tuple-element.28.index, f32[192,768]{1,0:T(8,128)S(1)} %collective-permute-done.2.refs_0_, ...), custom_call_target="tpu_custom_call" | custom-call | bytes 1000 | tf_op jit(solution)/shard_map/pallas_call | solution.py:229
  66.2 0.0 collective-permute-done.6.refs_2_
  66.2 0.4 collective-permute-start.14
  66.6 0.0 collective-permute-done.5.factor.refs_0_
  66.6 0.5 collective-permute-start.11
  67.1 0.0 collective-permute-start.10
  67.1 0.0 collective-permute-done.13.refs_1_
  67.1 2.5 %collective-permute-done.14.refs_3_ = f32[2,384,512]{2,1,0:T(8,128)S(1)} collective-permute-done((f32[2,384,512]{2,1,0:T(8,128)S(1)}, f32[2,384,512]{2,1,0:T(8,128)S(1)}, u32[]{:S(2)}, u32[]{:S(2)}) %collective-permute-start.14) | collective-permute-done | bytes 1572896 | tf_op jit(solution)/shard_map/ppermute | solution.py:25
  69.6 17.3 %shard_map.88 = (f32[2,384,512]{2,1,0:T(8,128)S(1)}, bf16[2,768,512]{2,1,0:T(8,128)(2,1)S(1)}, bf16[2,1536,512]{2,1,0:T(8,128)(2,1)S(1)}, f32[384,768]{1,0:T(8,128)S(1)}, f32[2,512]{1,0:T(2,128)S(1)}) custom-call(s32[2,4,256]{2,1,0:T(4,128)S(1)} %get-tuple-element.28.index, bf16[2,4,768,256]{3,2,1,0:T(8,128)(2,1)S(1)} %get-tuple-element.32.pick_high, ...), custom_call_target="tpu_custom_call" | custom-call | bytes 1000 | tf_op jit(solution)/shard_map/pallas_call | solution.py:229
  86.9 0.0 collective-permute-done.12.border
  86.9 1.4 %shard_map.89 = (bf16[384,1536]{1,0:T(8,128)(2,1)S(1)}, f32[2,384,512]{2,1,0:T(8,128)S(1)}) custom-call(f32[384,1536]{1,0:T(8,128)S(1)} %collective-permute-done.12.border, bf16[2,1536,512]{2,1,0:T(8,128)(2,1)S(1)} %get-tuple-element.39.lower_high), custom_call_target="tpu_custom_call" | custom-call | bytes 1000 | tf_op jit(solution)/shard_map/pallas_call | solution.py:229
  88.4 6.6 %collective-permute-done.11.refs_2_ = f32[384,768]{1,0:T(8,128)S(1)} collective-permute-done((f32[384,768]{1,0:T(8,128)S(1)}, f32[384,768]{1,0:T(8,128)S(1)}, u32[]{:S(2)}, u32[]{:S(2)}) %collective-permute-start.11) | collective-permute-done | bytes 1179680 | tf_op jit(solution)/shard_map/ppermute | solution.py:25
  94.9 0.0 collective-permute-start.15
  94.9 0.0 collective-permute-done.10.refs_1_
  94.9 2.8 %collective-permute-done.15.refs_3_ = f32[384,768]{1,0:T(8,128)S(1)} collective-permute-done((f32[384,768]{1,0:T(8,128)S(1)}, f32[384,768]{1,0:T(8,128)S(1)}, u32[]{:S(2)}, u32[]{:S(2)}) %collective-permute-start.15) | collective-permute-done | bytes 1179680 | tf_op jit(solution)/shard_map/ppermute | solution.py:25
  97.8 3.5 %shard_map.90 = f32[1,1792]{1,0:T(1,128)S(1)} custom-call(f32[384,768]{1,0:T(8,128)S(1)} %collective-permute-done.5.factor.refs_0_, f32[384,768]{1,0:T(8,128)S(1)} %collective-permute-done.10.refs_1_, f32[384,768]{1,0:T(8,128)S(1)} %collective-permute-done.11.refs_2_, f32[384,768]{1,0:T(8,128)S(1)} %collective-permute-done.15.refs_3_, ...), custom_call_target="tpu_custom_call" | custom-call | bytes 1000 | tf_op jit(solution)/shard_map/pallas_call | solution.py:229
  101.3 0.2 collective-permute-start.16
  101.5 1.0 collective-permute-done.16
  102.5 0.4 collective-permute-start.17
  102.9 0.5 collective-permute-start.18
  103.4 2.6 %collective-permute-start.19 = (f32[1,1792]{1,0:T(1,128)S(1)}, f32[1,1792]{1,0:T(1,128)S(1)}, u32[]{:S(2)}, u32[]{:S(2)}) collective-permute-start(f32[1,1792]{1,0:T(1,128)S(1)} %add.3.refs_0_), channel_id=1, source_target_pairs={{0,3},{1,2},{2,1},{3,0},{4,7},{5,6},{6,5},{7,4},{8,11},{9,10},{10,... | collective-permute-start | bytes 21512 | tf_op jit(solution)/shard_map/ppermute | solution.py:25
  106.1 0.2 collective-permute-done.17.refs_1_
  106.2 0.4 collective-permute-done.18.refs_2_
  106.6 1.4 %collective-permute-done.19.refs_3_ = f32[1,1792]{1,0:T(1,128)S(1)} collective-permute-done((f32[1,1792]{1,0:T(1,128)S(1)}, f32[1,1792]{1,0:T(1,128)S(1)}, u32[]{:S(2)}, u32[]{:S(2)}) %collective-permute-start.19) | collective-permute-done | bytes 7200 | tf_op jit(solution)/shard_map/ppermute | solution.py:25
  108.0 1.3 %shard_map.91 = (f32[1,768]{1,0:T(1,128)}, f32[2,512]{1,0:T(2,128)}) custom-call(s32[16]{0:T(128)} %parent_ref.3, f32[1,1792]{1,0:T(1,128)S(1)} %add.3.refs_0_, f32[1,1792]{1,0:T(1,128)S(1)} %collective-permute-done.17.refs_1_, f32[1,1792]{1,0:T(1,128)S(1)} %collective-permute-done.18.refs_2_, f32[1,1792]{1,0:T(1,128)S(1)} %collective-permute-done.19.refs_3_), custom_call_target="tpu_custom_call" | custom-call | bytes 1000 | tf_op jit(solution)/shard_map/pallas_call | solution.py:229
  (1 shorter events, 0.0 us)
Async XLA Ops:
  0.6 8.2 %collective-permute-start = (f32[2,256,512]{2,1,0:T(8,128)}, f32[2,256,512]{2,1,0:T(8,128)S(1)}, u32[]{:S(2)}, u32[]{:S(2)}) collective-permute-start(f32[2,256,512]{2,1,0:T(8,128)} %own_rows.1), channel_id=1, source_target_pairs={{0,4},{1,5},{2,6},{3,7},{4,0},{5,1},{6,2},{7,3},{8,12},{9,13},{10,... | collective-permute-start | bytes 3145736 | tf_op jit(solution)/shard_map/ppermute | solution.py:25
  1.1 23.4 %copy-start = (f32[1,384,1536]{2,1,0:T(8,128)S(1)}, f32[1,384,1536]{2,1,0:T(8,128)}, u32[]{:S(2)}) copy-start(f32[1,384,1536]{2,1,0:T(8,128)} %param.7) | copy-start | bytes 7077892
  1.2 9.3 %collective-permute-start.2 = (f32[192,768]{1,0:T(8,128)}, f32[192,768]{1,0:T(8,128)S(1)}, u32[]{:S(2)}, u32[]{:S(2)}) collective-permute-start(f32[192,768]{1,0:T(8,128)} %bitcast.5), channel_id=1, source_target_pairs={{0,0},{1,4},{2,2},{3,6},{4,1},{5,5},{6,3},{7,7},{8,8},{9,12},{10,1... | collective-permute-start | bytes 1769480 | tf_op jit(solution)/shard_map/ppermute | solution.py:35
  3.0 15.7 %collective-permute-start.3 = (f32[192,768]{1,0:T(8,128)}, f32[192,768]{1,0:T(8,128)S(1)}, u32[]{:S(2)}, u32[]{:S(2)}) collective-permute-start(f32[192,768]{1,0:T(8,128)} %bitcast.6), channel_id=1, source_target_pairs={{0,2},{1,3},{2,0},{3,1},{4,6},{5,7},{6,4},{7,5},{8,10},{9,11},{10,... | collective-permute-start | bytes 1769480 | tf_op jit(solution)/shard_map/ppermute | solution.py:25
  5.5 3.3 %collective-permute-start.1 = (f32[2,128,512]{2,1,0:T(8,128)}, f32[2,128,512]{2,1,0:T(8,128)S(1)}, u32[]{:S(2)}, u32[]{:S(2)}) collective-permute-start(f32[2,128,512]{2,1,0:T(8,128)} %own_inverse.1), channel_id=1, source_target_pairs={{0,4},{1,5},{2,6},{3,7},{4,0},{5,1},{6,2},{7,3},{8,12},{9,13},{10,... | collective-permute-start | bytes 1572872 | tf_op jit(solution)/shard_map/ppermute | solution.py:25
  18.7 0.8 collective-permute-start.4
  19.5 46.7 %collective-permute-start.6 = (f32[2,384,512]{2,1,0:T(8,128)S(1)}, f32[2,384,512]{2,1,0:T(8,128)S(1)}, u32[]{:S(2)}, u32[]{:S(2)}) collective-permute-start(f32[2,384,512]{2,1,0:T(8,128)S(1)} %collective-permute-done.4.refs_0_), channel_id=1, source_target_pairs={{0,2},{1,3},{2,0},{3,1},{4,6},{5,7},{6,4},{7,5},{8,10},{9,11},{10,... | collective-permute-start | bytes 4718600 | tf_op jit(solution)/shard_map/ppermute | solution.py:25
  21.9 2.6 %collective-permute-start.8 = (f32[192,768]{1,0:T(8,128)S(1)}, f32[192,768]{1,0:T(8,128)S(1)}, u32[]{:S(2)}, u32[]{:S(2)}) collective-permute-start(f32[192,768]{1,0:T(8,128)S(1)} %collective-permute-done.3), channel_id=1, source_target_pairs={{0,0},{1,4},{2,2},{3,6},{4,1},{5,5},{6,3},{7,7},{8,8},{9,12},{10,1... | collective-permute-start | bytes 1769480 | tf_op jit(solution)/shard_map/ppermute | solution.py:35
  22.6 44.0 %collective-permute-start.5 = (f32[384,768]{1,0:T(8,128)}, f32[384,768]{1,0:T(8,128)S(1)}, u32[]{:S(2)}, u32[]{:S(2)}) collective-permute-start(f32[384,768]{1,0:T(8,128)} %bitcast.4), channel_id=1, source_target_pairs={{0,0},{1,4},{2,2},{3,6},{4,1},{5,5},{6,3},{7,7},{8,8},{9,12},{10,1... | collective-permute-start | bytes 3538952 | tf_op jit(solution)/shard_map/ppermute | solution.py:35
  24.5 62.4 %collective-permute-start.12 = (f32[384,1536]{1,0:T(8,128)S(1)}, f32[384,1536]{1,0:T(8,128)S(1)}, u32[]{:S(2)}, u32[]{:S(2)}) collective-permute-start(f32[384,1536]{1,0:T(8,128)S(1)} %bitcast.3), channel_id=1, source_target_pairs={{0,0},{1,4},{2,2},{3,6},{4,1},{5,5},{6,3},{7,7},{8,8},{9,12},{10,1... | collective-permute-start | bytes 7077896 | tf_op jit(solution)/shard_map/ppermute | solution.py:35
  25.3 34.2 %collective-permute-start.7 = (f32[192,768]{1,0:T(8,128)S(1)}, f32[192,768]{1,0:T(8,128)S(1)}, u32[]{:S(2)}, u32[]{:S(2)}) collective-permute-start(f32[192,768]{1,0:T(8,128)S(1)} %collective-permute-done.2.refs_0_), channel_id=1, source_target_pairs={{0,4},{1,5},{2,6},{3,7},{4,0},{5,1},{6,2},{7,3},{8,12},{9,13},{10,... | collective-permute-start | bytes 1769480 | tf_op jit(solution)/shard_map/ppermute | solution.py:25
  58.0 2.5 %collective-permute-start.9 = (f32[192,768]{1,0:T(8,128)S(1)}, f32[192,768]{1,0:T(8,128)S(1)}, u32[]{:S(2)}, u32[]{:S(2)}) collective-permute-start(f32[192,768]{1,0:T(8,128)S(1)} %collective-permute-done.8.refs_2_), channel_id=1, source_target_pairs={{0,4},{1,5},{2,6},{3,7},{4,0},{5,1},{6,2},{7,3},{8,12},{9,13},{10,... | collective-permute-start | bytes 1769480 | tf_op jit(solution)/shard_map/ppermute | solution.py:25
  59.6 7.5 %collective-permute-start.13 = (f32[2,384,512]{2,1,0:T(8,128)S(1)}, f32[2,384,512]{2,1,0:T(8,128)S(1)}, u32[]{:S(2)}, u32[]{:S(2)}) collective-permute-start(f32[2,384,512]{2,1,0:T(8,128)S(1)} %collective-permute-done.4.refs_0_), channel_id=1, source_target_pairs={{0,4},{1,5},{2,6},{3,7},{4,0},{5,1},{6,2},{7,3},{8,12},{9,13},{10,... | collective-permute-start | bytes 4718600 | tf_op jit(solution)/shard_map/ppermute | solution.py:25
  66.2 3.5 %collective-permute-start.14 = (f32[2,384,512]{2,1,0:T(8,128)S(1)}, f32[2,384,512]{2,1,0:T(8,128)S(1)}, u32[]{:S(2)}, u32[]{:S(2)}) collective-permute-start(f32[2,384,512]{2,1,0:T(8,128)S(1)} %collective-permute-done.6.refs_2_), channel_id=1, source_target_pairs={{0,4},{1,5},{2,6},{3,7},{4,0},{5,1},{6,2},{7,3},{8,12},{9,13},{10,... | collective-permute-start | bytes 4718600 | tf_op jit(solution)/shard_map/ppermute | solution.py:25
  66.6 28.3 %collective-permute-start.11 = (f32[384,768]{1,0:T(8,128)S(1)}, f32[384,768]{1,0:T(8,128)S(1)}, u32[]{:S(2)}, u32[]{:S(2)}) collective-permute-start(f32[384,768]{1,0:T(8,128)S(1)} %collective-permute-done.5.factor.refs_0_), channel_id=1, source_target_pairs={{0,2},{1,3},{2,0},{3,1},{4,6},{5,7},{6,4},{7,5},{8,10},{9,11},{10,... | collective-permute-start | bytes 3538952 | tf_op jit(solution)/shard_map/ppermute | solution.py:25
  67.1 27.8 %collective-permute-start.10 = (f32[384,768]{1,0:T(8,128)S(1)}, f32[384,768]{1,0:T(8,128)S(1)}, u32[]{:S(2)}, u32[]{:S(2)}) collective-permute-start(f32[384,768]{1,0:T(8,128)S(1)} %collective-permute-done.5.factor.refs_0_), channel_id=1, source_target_pairs={{0,4},{1,5},{2,6},{3,7},{4,0},{5,1},{6,2},{7,3},{8,12},{9,13},{10,... | collective-permute-start | bytes 3538952 | tf_op jit(solution)/shard_map/ppermute | solution.py:25
  94.9 2.8 %collective-permute-start.15 = (f32[384,768]{1,0:T(8,128)S(1)}, f32[384,768]{1,0:T(8,128)S(1)}, u32[]{:S(2)}, u32[]{:S(2)}) collective-permute-start(f32[384,768]{1,0:T(8,128)S(1)} %collective-permute-done.11.refs_2_), channel_id=1, source_target_pairs={{0,4},{1,5},{2,6},{3,7},{4,0},{5,1},{6,2},{7,3},{8,12},{9,13},{10,... | collective-permute-start | bytes 3538952 | tf_op jit(solution)/shard_map/ppermute | solution.py:25
  101.3 1.2 %collective-permute-start.16 = (f32[1,1792]{1,0:T(1,128)S(1)}, f32[1,1792]{1,0:T(1,128)S(1)}, u32[]{:S(2)}, u32[]{:S(2)}) collective-permute-start(f32[1,1792]{1,0:T(1,128)S(1)} %shard_map.90), channel_id=1, source_target_pairs={{0,4},{1,5},{2,6},{3,7},{4,0},{5,1},{6,2},{7,3},{8,12},{9,13},{10,... | collective-permute-start | bytes 21512 | tf_op jit(solution)/shard_map/ppermute | solution.py:25
  102.5 3.7 %collective-permute-start.17 = (f32[1,1792]{1,0:T(1,128)S(1)}, f32[1,1792]{1,0:T(1,128)S(1)}, u32[]{:S(2)}, u32[]{:S(2)}) collective-permute-start(f32[1,1792]{1,0:T(1,128)S(1)} %add.3.refs_0_), channel_id=1, source_target_pairs={{0,2},{1,3},{2,0},{3,1},{4,6},{5,7},{6,4},{7,5},{8,10},{9,11},{10,... | collective-permute-start | bytes 21512 | tf_op jit(solution)/shard_map/ppermute | solution.py:25
  102.9 3.6 %collective-permute-start.18 = (f32[1,1792]{1,0:T(1,128)S(1)}, f32[1,1792]{1,0:T(1,128)S(1)}, u32[]{:S(2)}, u32[]{:S(2)}) collective-permute-start(f32[1,1792]{1,0:T(1,128)S(1)} %add.3.refs_0_), channel_id=1, source_target_pairs={{0,1},{1,0},{2,3},{3,2},{4,5},{5,4},{6,7},{7,6},{8,9},{9,8},{10,11... | collective-permute-start | bytes 21512 | tf_op jit(solution)/shard_map/ppermute | solution.py:25
  103.4 4.5 %collective-permute-start.19 = (f32[1,1792]{1,0:T(1,128)S(1)}, f32[1,1792]{1,0:T(1,128)S(1)}, u32[]{:S(2)}, u32[]{:S(2)}) collective-permute-start(f32[1,1792]{1,0:T(1,128)S(1)} %add.3.refs_0_), channel_id=1, source_target_pairs={{0,3},{1,2},{2,1},{3,0},{4,7},{5,6},{6,5},{7,4},{8,11},{9,10},{10,... | collective-permute-start | bytes 21512 | tf_op jit(solution)/shard_map/ppermute | solution.py:25

commit v3 on v2

v3 whole, which is shorter than its diff:
```python
import functools

import jax
import jax.numpy as jnp
from jax import lax
from jax.experimental import pallas as pl
from jax.experimental.pallas import tpu as pltpu
from jax.sharding import PartitionSpec as P

MIB = 1024 * 1024
COLS = 256


def shape_of(shape, dtype=jnp.float32):
    return jax.ShapeDtypeStruct(shape, dtype)


def exchange(value, leaf_mask, front_mask, parity=None):
    fronts = lax.axis_size("front")
    pairs = [
        (leaf * fronts + front, (leaf ^ leaf_mask) * fronts + (front ^ front_mask))
        for leaf in range(lax.axis_size("leaf"))
        for front in range(fronts)
        if parity is None or (leaf ^ front) & 1 == parity
    ]
    return lax.ppermute(value, ("leaf", "front"), pairs)


def cross(value):
    fronts = lax.axis_size("front")
    pairs = []
    for leaf in range(lax.axis_size("leaf")):
        for front in range(fronts):
            flip = (leaf ^ front) & 1
            pairs.append((leaf * fronts + front, (leaf ^ flip) * fronts + (front ^ flip)))
    return lax.ppermute(value, ("leaf", "front"), pairs)


def after(value, *others):
    return lax.optimization_barrier((value, *others))[0]


def kids_of(parent_ref, owner):
    partner = owner ^ 1
    pool = [2 * owner, 2 * owner + 1, 2 * partner, 2 * partner + 1]
    member = [parent_ref[kid] == owner for kid in pool]
    first = jnp.where(member[0], 0, jnp.where(member[1], 1, 2))
    second = jnp.where(member[3], 3, jnp.where(member[2], 2, 1))
    ids = [2 * jnp.where(slot < 2, owner, partner) + (slot & 1) for slot in (first, second)]
    return (first, second), ids


def place_of():
    front, leaf = lax.axis_index("front"), lax.axis_index("leaf")
    owner = (leaf & -2) | (front & 1)
    block = (front & -2) | (leaf & 1)
    return owner, block


def keeps():
    return ((lax.axis_index("leaf") ^ lax.axis_index("front")) & 1) == 0


def store(pair, action):
    for ref, chosen in zip(pair, (keeps(), jnp.logical_not(keeps()))):
        pl.when(chosen)(functools.partial(action, ref))


def rounded(value):
    return value.astype(jnp.bfloat16)


def halves(value):
    high = rounded(value)
    return high, rounded(value - high.astype(jnp.float32))


def dot(left, right):
    return jnp.dot(left, right, preferred_element_type=jnp.float32)


def product(left, right):
    (left_high, left_low), (right_high, right_low) = left, right
    return dot(left_high, right_high) + (dot(left_high, right_low) + dot(left_low, right_high))


def column_sum(value):
    return jnp.sum(value, axis=0, keepdims=True)


def spans(width):
    return [slice(start, start + COLS) for start in range(0, width, COLS)]


def pack(out, diagonal, inverses):
    rows, size = diagonal.shape
    block, kid_size = inverses[0].shape
    left, half = size - kid_size, block // 2
    out[:rows] = diagonal[...]
    out[rows : rows + block, :kid_size] = inverses[0][...]
    out[rows : rows + block, kid_size:] = inverses[1][:, :left]
    out[rows + block :, : kid_size - left] = inverses[1][:half, left:]
    out[rows + block :, kid_size - left : 2 * (kid_size - left)] = inverses[1][half:, left:]


def select_kernel(parent_ref, index_ref, diagonal, own_rows, own_inverse, other_rows, other_inverse, *refs):
    packed, rows_out, index_out, first, second = refs
    leaf = lax.axis_index("leaf")
    slots, _ = kids_of(parent_ref, leaf)
    for place, slot in enumerate(slots):
        for source in range(4):
            rows, inverse = (own_rows, own_inverse) if source < 2 else (other_rows, other_inverse)

            @pl.when(slot == source)
            def _(rows=rows, inverse=inverse, place=place, source=source):
                rows_out[place] = rows[source % 2]
                (first, second)[place][...] = inverse[source % 2]

    packed[...] = jnp.zeros(packed.shape, jnp.float32)
    pack(packed, diagonal, (first, second))
    owner, block = place_of()
    _, ids = kids_of(parent_ref, owner)
    pieces, width = index_out.shape[1:]
    for place, kid in enumerate(ids):
        row = index_ref[pl.ds(kid, 1), :]
        parts = [row[:, start : start + width] for start in range(0, pieces * width, width)]
        for mask in range(pieces):
            part = parts[0]
            for at in range(1, pieces):
                part = jnp.where((block ^ mask) == at, parts[at], part)
            index_out[place, mask : mask + 1, :] = part


def picks(index, first, rows):
    position = lax.broadcasted_iota(jnp.int32, (rows, index.shape[1]), 0) + first
    return rounded(jnp.where(position == index, 1.0, 0.0))


def unpacked(pieces, refs):
    pairs = [(refs[0], refs[0]), (refs[1], refs[1])]
    for at in range(2, 2 * pieces - 2, 4):
        near_keep, near_swap, far_keep, far_swap = refs[at : at + 4]
        pairs += [(near_keep, near_swap), (far_keep, far_swap)]
    return pairs


def diagonal_kernel(pieces, index, factor, *refs):
    packed = refs[:pieces]
    diag_high, diag_low, pick_high, pick_low, inv_high, inv_low, weights, parent_sum, kid_sum = refs[pieces:]
    _, block = place_of()
    size, kid_size = diag_high.shape[0], inv_high.shape[1]
    rows, inv_block = size // pieces, kid_size // pieces
    left, half = size - kid_size, inv_block // 2
    for mask in range(pieces):
        piece = packed[mask]
        values = piece[:rows, :]
        first = piece[rows : rows + inv_block, :kid_size]
        second_left = piece[rows : rows + inv_block, kid_size:]
        second_top = piece[rows + inv_block :, : kid_size - left]
        second_bottom = piece[rows + inv_block :, kid_size - left : 2 * (kid_size - left)]
        if mask == 0:
            parent_sum[...] = column_sum(values * values)
            kid_sum[:1] = column_sum(first * first)
            kid_sum[1:, :left] = column_sum(second_left * second_left)
            kid_sum[1:, left:] = column_sum(second_top * second_top) + column_sum(second_bottom * second_bottom)
        start = pl.multiple_of((block ^ mask) * rows, 16)
        diag_high[pl.ds(start, rows), :], diag_low[pl.ds(start, rows), :] = halves(values)
        start = pl.multiple_of((block ^ mask) * inv_block, 16)
        below = pl.multiple_of(start + half, 16)
        for kid, first_row, lanes, value in (
            (0, start, slice(0, kid_size), first),
            (1, start, slice(0, left), second_left),
            (1, start, slice(left, kid_size), second_top),
            (1, below, slice(left, kid_size), second_bottom),
        ):
            span = pl.ds(first_row, value.shape[0])
            inv_high[kid, span, lanes], inv_low[kid, span, lanes] = halves(value)
    for kid in range(2):
        for mask in range(pieces):
            pick = picks(index[kid, mask : mask + 1, :], 0, size)
            pick_high[kid, mask] = rounded(dot(diag_high[...], pick))
            pick_low[kid, mask] = rounded(dot(diag_low[...], pick))
    factor_halves = halves(factor[...])
    for span in spans(size):
        weights[:, span] = product(factor_halves, (diag_high[:, span], diag_low[:, span]))


def fold(kid, mask, rows, inverse, index, pick_high, pick_low, own_border, border_size):
    _, block = place_of()
    size = pick_high.shape[2]
    weight = halves(product(halves(rows), inverse))
    lifted = product((pick_high[kid, mask], pick_low[kid, mask]), weight)
    places = index[kid, mask : mask + 1, :]
    pick = picks(places, size + block * own_border, own_border)
    own_lower = dot(pick, weight[0]) + dot(pick, weight[1])
    lower = dot(picks(places, size, border_size), weight[0])
    return lifted, own_lower, rounded(lower)


def early_kernel(index, pick_high, pick_low, inv_high, inv_low, own_rows, core_rows, lifted, own_lower, lower):
    for kid in range(2):
        inverse = inv_high[kid], inv_low[kid]
        for mask, rows in enumerate((own_rows, core_rows)):
            parts = fold(
                kid, mask, rows[kid], inverse, index, pick_high, pick_low, own_lower.shape[1], lower.shape[1]
            )
            for ref, part in zip((lifted, own_lower, lower), parts):
                ref[kid] = part if mask == 0 else ref[kid] + part


def late_kernel(pieces, index, pick_high, pick_low, inv_high, inv_low, factor, early_lifted, early_own, early_lower, *refs):
    kid_rows = refs[: 2 * pieces - 4]
    kid_in, reduced, lift_high, lower_high, kid_sum, rows, lifted = refs[2 * pieces - 4 :]
    _, block = place_of()
    size = lifted.shape[0]
    own_rows = size // pieces
    factor_high = rounded(factor[...])
    for mask, pair in enumerate(unpacked(pieces, (None, None) + kid_rows)):
        if mask < 2:
            continue

        def put(ref, mask=mask):
            rows[mask - 2] = ref[...]

        store(pair, put)
    for kid in range(2):
        inverse = inv_high[kid], inv_low[kid]
        for mask in range(2, pieces):
            parts = fold(
                kid, mask, rows[mask - 2, kid], inverse, index, pick_high, pick_low, reduced.shape[1], lower_high.shape[1]
            )
            first = mask == 2
            lifted[...] = (early_lifted[kid] if first else lifted[...]) + parts[0]
            reduced[kid] = (early_own[kid] if first else reduced[kid]) + parts[1]
            lower_high[kid] = (early_lower[kid] if first else lower_high[kid]) + parts[2]
        own = lifted[pl.ds(pl.multiple_of(block * own_rows, 16), own_rows), :]
        kid_sum[kid : kid + 1] = kid_in[kid : kid + 1] + column_sum(own * own)
        lift_high[kid] = rounded(lifted[...])
        reduced[kid] = reduced[kid] - dot(factor_high, lift_high[kid])


def border_kernel(border, lower_high, border_high, border_lower):
    border_high[...] = rounded(border[...])
    for kid in range(2):
        for span in spans(lower_high.shape[2]):
            border_lower[kid, :, span] = dot(border_high[...], lower_high[kid, :, span])


def image_kernel(pieces, *refs):
    factor = unpacked(pieces, refs)
    border_high, border_lower, weights, diag_high, diag_low, parent_sum, reduced, lift_high, kid_sum = refs[
        2 * pieces - 2 : 2 * pieces + 7
    ]
    out, factor_high, fold_high, fold_low = refs[2 * pieces + 7 :]
    _, block = place_of()
    own_border, size = refs[0].shape
    for mask, pair in enumerate(factor):
        start = pl.multiple_of((block ^ mask) * own_border, 16)

        def put(ref, start=start):
            factor_high[pl.ds(start, own_border), :] = rounded(ref[...])

        if mask < 2:
            put(pair[0])
        else:
            store(pair, put)
    for span in spans(size):
        fold_high[:, span], fold_low[:, span] = halves(dot(border_high[...], factor_high[:, span]))
    folded = fold_high[...], fold_low[...]
    for span in spans(size):
        image = product(folded, (diag_high[:, span], diag_low[:, span]))
        out[:, span] = parent_sum[:, span] + column_sum(weights[:, span] * image)
    kid_size = reduced.shape[2]
    for kid in range(2):
        for span in spans(kid_size):
            image = border_lower[kid, :, span] - dot(folded[0], lift_high[kid, :, span])
            target = size + kid * kid_size + span.start
            out[:, target : target + COLS] = kid_sum[kid : kid + 1, span] + column_sum(reduced[kid, :, span] * image)


def finish_kernel(parent_ref, *refs):
    partials, (parent_out, kid_out) = refs[:-2], refs[-2:]
    leaf = lax.axis_index("leaf")
    size, kid_size = parent_out.shape[1], kid_out.shape[1]
    half = len(partials) // 2
    sums = [functools.reduce(jnp.add, [ref[...] for ref in group]) for group in (partials[:half], partials[half:])]
    owner, _ = place_of()
    parent_out[...] = jnp.where(owner == leaf, sums[0][:, :size], sums[1][:, :size])
    for parent, total in ((owner, sums[0]), (owner ^ 1, sums[1])):
        _, ids = kids_of(parent_ref, parent)
        for place in range(2):
            for kid in range(2):

                @pl.when(ids[place] == 2 * leaf + kid)
                def _(total=total, place=place, kid=kid):
                    start = size + place * kid_size
                    kid_out[kid : kid + 1] = total[:, start : start + kid_size]


def call(kernel, out_shape, limit, scalars=0, loose=0, keep=True, scratch=(), moved=1_000):
    def run(*args):
        specs = [pl.BlockSpec(memory_space=pltpu.SMEM if at < scalars else pltpu.VMEM) for at in range(len(args))]
        args = [
            pltpu.with_memory_space_constraint(value, pltpu.HBM if at < loose else pltpu.VMEM)
            for at, value in enumerate(args)
        ]
        results = out_shape
        if keep:
            results = jax.tree.map(lambda leaf: pltpu.VMEM(leaf.shape, leaf.dtype), results)
        return pl.pallas_call(
            kernel,
            out_shape=results,
            in_specs=specs,
            out_specs=jax.tree.map(lambda _: pl.BlockSpec(memory_space=pltpu.VMEM), out_shape),
            scratch_shapes=scratch,
            compiler_params=pltpu.CompilerParams(vmem_limit_bytes=limit * MIB),
            cost_estimate=pl.CostEstimate(flops=0, bytes_accessed=moved, transcendentals=0),
        )(*args)

    return run


def shards(border, factor, diagonal, kid_rows, kid_inverse, child_index, child_parent):
    border, factor, diagonal = border[0], factor[0], diagonal[0]
    pieces = lax.axis_size("front")
    size, kid_size, border_size = diagonal.shape[1], kid_rows.shape[2], border.shape[1]
    own_border = border.shape[0]
    kid_block = kid_rows.shape[1]
    half = jnp.bfloat16

    def over_fronts(value, parity=None):
        parts = {0: value}
        bit = 2
        while bit < pieces:
            for mask in list(parts):
                parts[mask | bit] = exchange(parts[mask], 0, bit, parity)
            bit *= 2
        return parts

    def gathered(own, keep, swap, gate_own, gate_keep, gate_swap):
        result = [own, exchange(after(own, *gate_own), 1, 0)]
        for mask in list(keep)[1:]:
            far_swap = exchange(after(keep[mask], *gate_keep), 1, 0, 0)
            far_keep = exchange(after(swap[mask], *gate_swap), 1, 0, 1)
            result += [keep[mask], swap[mask], far_keep, far_swap]
        return result

    last = pieces - 2
    inv_block = kid_inverse.shape[1]
    keep_factor = over_fronts(factor, 0)
    own_factor = cross(factor)
    packed, kid_rows, index = call(
        select_kernel,
        (
            shape_of((diagonal.shape[0] + inv_block + inv_block // 2, size)),
            shape_of(kid_rows.shape),
            shape_of((2, pieces, kid_block), jnp.int32),
        ),
        10,
        scalars=1,
        loose=5,
        scratch=[pltpu.VMEM(kid_inverse.shape[1:], jnp.float32)] * 2,
    )(child_parent, child_index, diagonal, kid_rows, kid_inverse, exchange(kid_rows, 1, 0), exchange(kid_inverse, 1, 0))
    packed = cross(after(packed, keep_factor[last]))
    own_kids = cross(after(kid_rows, own_factor))
    packed_parts = over_fronts(packed)
    keep_kids = over_fronts(own_kids, 0)
    swap_kids = over_fronts(own_kids, 1)
    own_border_rows = cross(after(border, own_kids, packed_parts[last], keep_kids[last]))
    near, far = list(packed_parts.items())[0], list(packed_parts.items())[1:]
    packed_parts[1] = exchange(after(near[1], own_kids), 1, 0)
    for mask, part in far:
        packed_parts[mask | 1] = exchange(part, 1, 0)
    kids_core = exchange(after(own_kids, packed_parts[last]), 1, 0)

    diag_high, diag_low, pick_high, pick_low, inv_high, inv_low, weights, parent_sum, inv_sum = call(
        functools.partial(diagonal_kernel, pieces),
        (
            shape_of((size, size), half),
            shape_of((size, size), half),
            shape_of((2, pieces, size, kid_block), half),
            shape_of((2, pieces, size, kid_block), half),
            shape_of((2, kid_size, kid_size), half),
            shape_of((2, kid_size, kid_size), half),
            shape_of((own_border, size)),
            shape_of((1, size)),
            shape_of((2, kid_size)),
        ),
        10,
    )(index, own_factor, *[packed_parts[mask] for mask in range(pieces)])
    common = (index, pick_high, pick_low, inv_high, inv_low)
    early = call(
        early_kernel,
        (
            shape_of((2, size, kid_size)),
            shape_of((2, own_border, kid_size)),
            shape_of((2, border_size, kid_size), half),
        ),
        14,
    )(*common, own_kids, kids_core)

    kid_parts = []
    for mask in list(keep_kids)[1:]:
        far_swap = exchange(after(keep_kids[mask], early[0]), 1, 0, 0)
        far_keep = exchange(after(swap_kids[mask], early[0]), 1, 0, 1)
        kid_parts += [keep_kids[mask], swap_kids[mask], far_keep, far_swap]
    swap_factor = over_fronts(after(own_factor, swap_kids[last], early[0]), 1)
    reduced, lift_high, lower_high, kid_sum = call(
        functools.partial(late_kernel, pieces),
        (
            shape_of((2, own_border, kid_size)),
            shape_of((2, size, kid_size), half),
            shape_of((2, border_size, kid_size), half),
            shape_of((2, kid_size)),
        ),
        14,
        scratch=[
            pltpu.VMEM((pieces - 2, *kid_rows.shape), jnp.float32),
            pltpu.VMEM((size, kid_size), jnp.float32),
        ],
    )(*common, own_factor, *early, *kid_parts, inv_sum)

    border_high, border_lower = call(
        border_kernel, (shape_of(border.shape, half), shape_of((2, own_border, kid_size))), 8
    )(own_border_rows, lower_high)

    factor_parts = gathered(own_factor, keep_factor, swap_factor, [own_kids], [own_kids], [border_lower])
    total = call(
        functools.partial(image_kernel, pieces),
        shape_of((1, size + 2 * kid_size)),
        12,
        scratch=[
            pltpu.VMEM((border_size, size), half),
            pltpu.VMEM((own_border, size), half),
            pltpu.VMEM((own_border, size), half),
        ],
    )(*factor_parts, border_high, border_lower, weights, diag_high, diag_low, parent_sum, reduced, lift_high, kid_sum)

    total = total + exchange(total, 1, 0)
    bit = 4
    while bit < pieces:
        total = total + exchange(total, 0, bit)
        bit *= 2
    near = range(min(pieces, 4))
    order = [mask for parity in (0, 1) for mask in near if mask % 2 == parity]
    partials = [exchange(total, 0, mask) if mask else total for mask in order]
    return call(finish_kernel, (shape_of((1, size)), shape_of((2, kid_size))), 2, scalars=1, loose=1, keep=False)(
        child_parent, *partials
    )


def solution(mesh):
    whole = P("leaf", "front", None)
    return jax.shard_map(
        shards,
        mesh=mesh,
        in_specs=(whole,) * 5 + (P(), P()),
        out_specs=(P("leaf", None), P("leaf", None)),
        check_vma=False,
    )
```

time: 110 us -> 121 us (1.10)
  starting transfers between devices: 50.9 us -> 69.6 us
  waiting for transfers between devices: 26.9 us -> 18.3 us
    ppermute x15 -> x19, starting transfers between devices: 44.9 us -> 65.4 us  [exchange(): return lax.ppermute(value, ('leaf', 'front'), pairs)]
    ppermute x15 -> x19, waiting for transfers between devices: 26.9 us -> 18.3 us  [exchange(): return lax.ppermute(value, ('leaf', 'front'), pairs)]
    ppermute x5 -> x4, starting transfers between devices: 6.01 us -> 4.18 us  [cross(): return lax.ppermute(value, ('leaf', 'front'), pairs)]
    pallas_call x6 -> x7, Pallas kernels: 30.8 us -> 31.5 us  [run(): pl.pallas_call(kernel, out_shape=results, in_specs=specs, out_specs=jax.t...]
  transfers between devices with their start and end apart: 20 -> 23, of which waited for: 11 -> 6; matrix products, arithmetic and copies ran while one was open for 0% -> 0% of each run, Pallas kernels for 24% -> 22%
where the time goes in v3:
time: 121 us; the launch traced here: 120 us
  starting transfers between devices  69.6 us (58%)
  Pallas kernels  31.5 us (26%)
  waiting for transfers between devices  18.3 us (15%)
    ppermute x19, starting transfers between devices, exchange(): return lax.ppermute(value, ('leaf', 'front'), pairs)  65.4 us
    pallas_call x7, Pallas kernels, run(): pl.pallas_call(kernel, out_shape=results, in_specs=specs, out_specs=jax.t...  31.5 us
    ppermute x19, waiting for transfers between devices, exchange(): return lax.ppermute(value, ('leaf', 'front'), pairs)  18.3 us
    ppermute x4, starting transfers between devices, cross(): return lax.ppermute(value, ('leaf', 'front'), pairs)  4.18 us
  transfers between devices with their start and end apart: 23, of which 6 were waited for; matrix products, arithmetic and copies ran while one was open for 0% of the time, Pallas kernels for 22%

profile of v3, /device:TPU:0, one launch (start us, length us, event | category | flops | bytes accessed | tf_op | source)
XLA Modules:
  0.0 120.2 jit_solution(13436592558971705205)
XLA Ops:
  0.6 4.9 %collective-permute-start.5 = (f32[384,768]{1,0:T(8,128)}, f32[384,768]{1,0:T(8,128)S(1)}, u32[]{:S(2)}, u32[]{:S(2)}) collective-permute-start(f32[384,768]{1,0:T(8,128)} %bitcast.5), channel_id=1, source_target_pairs={{0,2},{2,0},{5,7},{7,5},{8,10},{10,8},{13,15},{15,13},{16,18},{18,... | collective-permute-start | bytes 3538952 | tf_op jit(solution)/shard_map/ppermute | solution.py:26
  5.5 0.1 collective-permute-start.1
  5.6 1.9 %collective-permute-start = (f32[384,768]{1,0:T(8,128)}, f32[384,768]{1,0:T(8,128)S(1)}, u32[]{:S(2)}, u32[]{:S(2)}) collective-permute-start(f32[384,768]{1,0:T(8,128)} %bitcast.6), channel_id=1, source_target_pairs={{0,0},{1,4},{2,2},{3,6},{4,1},{5,5},{6,3},{7,7},{8,8},{9,12},{10,1... | collective-permute-start | bytes 3538952 | tf_op jit(solution)/shard_map/ppermute | solution.py:36
  7.5 1.2 collective-permute-start.2
  8.7 1.7 %collective-permute-done.2.other_inverse = f32[2,128,512]{2,1,0:T(8,128)S(1)} collective-permute-done((f32[2,128,512]{2,1,0:T(8,128)}, f32[2,128,512]{2,1,0:T(8,128)S(1)}, u32[]{:S(2)}, u32[]{:S(2)}) %collective-permute-start.2) | collective-permute-done | bytes 524320 | tf_op jit(solution)/shard_map/ppermute | solution.py:26
  10.5 0.0 collective-permute-done.1.other_rows
  10.5 0.0 copy-start
  10.5 1.9 %shard_map.86 = (f32[384,768]{1,0:T(8,128)S(1)}, f32[2,256,512]{2,1,0:T(8,128)S(1)}, s32[2,4,256]{2,1,0:T(4,128)S(1)}) custom-call(s32[16]{0:T(128)} %parent_ref.3, s32[16,1024]{1,0:T(8,128)} %index_ref.1, f32[192,768]{1,0:T(8,128)} %bitcast.3, f32[2,256,512]{2,1,0:T(8,128)} %own_rows.1, f32[2,128,512]{2,1,0:T(8,128)} %own_inverse.1, ...), custom_call_target="tpu_custom_call" | custom-call | bytes 1000 | tf_op jit(solution)/shard_map/pallas_call | solution.py:310
  12.4 7.5 %collective-permute-done.5.refs_2_ = f32[384,768]{1,0:T(8,128)S(1)} collective-permute-done((f32[384,768]{1,0:T(8,128)}, f32[384,768]{1,0:T(8,128)S(1)}, u32[]{:S(2)}, u32[]{:S(2)}) %collective-permute-start.5) | collective-permute-done | bytes 1179680 | tf_op jit(solution)/shard_map/ppermute | solution.py:26
  19.9 0.7 collective-permute-start.7
  20.6 0.0 collective-permute-done.factor.refs_0_
  20.6 0.7 collective-permute-start.3
  21.4 0.0 collective-permute-done.7.refs_0_
  21.4 2.1 %collective-permute-start.9 = (f32[384,768]{1,0:T(8,128)S(1)}, f32[384,768]{1,0:T(8,128)S(1)}, u32[]{:S(2)}, u32[]{:S(2)}) collective-permute-start(f32[384,768]{1,0:T(8,128)S(1)} %collective-permute-done.7.refs_0_), channel_id=1, source_target_pairs={{0,2},{1,3},{2,0},{3,1},{4,6},{5,7},{6,4},{7,5},{8,10},{9,11},{10,... | collective-permute-start | bytes 3538952 | tf_op jit(solution)/shard_map/ppermute | solution.py:26
  23.5 0.0 collective-permute-done.3.own_rows
  23.5 1.9 %collective-permute-start.13 = (f32[2,256,512]{2,1,0:T(8,128)S(1)}, f32[2,256,512]{2,1,0:T(8,128)S(1)}, u32[]{:S(2)}, u32[]{:S(2)}) collective-permute-start(f32[2,256,512]{2,1,0:T(8,128)S(1)} %collective-permute-done.3.own_rows), channel_id=1, source_target_pairs={{0,2},{2,0},{5,7},{7,5},{8,10},{10,8},{13,15},{15,13},{16,18},{18,... | collective-permute-start | bytes 3145736 | tf_op jit(solution)/shard_map/ppermute | solution.py:26
  25.4 23.4 %collective-permute-start.8 = (f32[384,768]{1,0:T(8,128)S(1)}, f32[384,768]{1,0:T(8,128)S(1)}, u32[]{:S(2)}, u32[]{:S(2)}) collective-permute-start(f32[384,768]{1,0:T(8,128)S(1)} %collective-permute-done.7.refs_0_), channel_id=1, source_target_pairs={{0,4},{1,5},{2,6},{3,7},{4,0},{5,1},{6,2},{7,3},{8,12},{9,13},{10,... | collective-permute-start | bytes 3538952 | tf_op jit(solution)/shard_map/ppermute | solution.py:26
  48.8 0.0 collective-permute-done.9.refs_2_
  48.8 12.6 %collective-permute-start.10 = (f32[384,768]{1,0:T(8,128)S(1)}, f32[384,768]{1,0:T(8,128)S(1)}, u32[]{:S(2)}, u32[]{:S(2)}) collective-permute-start(f32[384,768]{1,0:T(8,128)S(1)} %collective-permute-done.9.refs_2_), channel_id=1, source_target_pairs={{0,4},{1,5},{2,6},{3,7},{4,0},{5,1},{6,2},{7,3},{8,12},{9,13},{10,... | collective-permute-start | bytes 3538952 | tf_op jit(solution)/shard_map/ppermute | solution.py:26
  61.3 0.0 collective-permute-done.13.refs_0_
  61.3 0.0 copy-done
  61.4 0.8 collective-permute-start.14
  62.2 1.5 %collective-permute-start.11 = (f32[2,256,512]{2,1,0:T(8,128)S(1)}, f32[2,256,512]{2,1,0:T(8,128)S(1)}, u32[]{:S(2)}, u32[]{:S(2)}) collective-permute-start(f32[2,256,512]{2,1,0:T(8,128)S(1)} %collective-permute-done.3.own_rows), channel_id=1, source_target_pairs={{0,4},{1,5},{2,6},{3,7},{4,0},{5,1},{6,2},{7,3},{8,12},{9,13},{10,... | collective-permute-start | bytes 3145736 | tf_op jit(solution)/shard_map/ppermute | solution.py:26
  63.6 0.9 collective-permute-start.6
  64.5 0.0 collective-permute-done.8.refs_1_
  64.5 0.0 collective-permute-done.10.refs_3_
  64.6 7.5 %shard_map.87 = (bf16[768,768]{1,0:T(8,128)(2,1)S(1)}, bf16[768,768]{1,0:T(8,128)(2,1)S(1)}, bf16[2,4,768,256]{3,2,1,0:T(8,128)(2,1)S(1)}, bf16[2,4,768,256]{3,2...) custom-call(s32[2,4,256]{2,1,0:T(4,128)S(1)} %get-tuple-element.37.i, ...), custom_call_target="tpu_custom_call" | custom-call | bytes 1000 | tf_op jit(solution)/shard_map/pallas_call | solution.py:310
  72.1 0.0 collective-permute-done.11.core_rows
  72.1 7.3 %shard_map.88 = (f32[2,768,512]{2,1,0:T(8,128)S(1)}, f32[2,384,512]{2,1,0:T(8,128)S(1)}, bf16[2,1536,512]{2,1,0:T(8,128)(2,1)S(1)}) custom-call(s32[2,4,256]{2,1,0:T(4,128)S(1)} %get-tuple-element.37.index, bf16[2,4,768,256]{3,2,1,0:T(8,128)(2,1)S(1)} %get-tuple-element.41.pick_high, bf16[2,4,768,256]{3,2,1,0:T(8,128)(2,1)S(1)} %get-tuple-element.42.pick_low, ...), custom_call_target="tpu_custom_call" | custom-call | bytes 1000 | tf_op jit(solution)/shard_map/pallas_call | solution.py:310
  79.3 0.0 collective-permute-done.6.refs_1_
  79.3 1.0 collective-permute-start.12
  80.3 5.8 %collective-permute-start.16 = (f32[2,256,512]{2,1,0:T(8,128)S(1)}, f32[2,256,512]{2,1,0:T(8,128)S(1)}, u32[]{:S(2)}, u32[]{:S(2)}) collective-permute-start(f32[2,256,512]{2,1,0:T(8,128)S(1)} %collective-permute-done.13.refs_0_), channel_id=1, source_target_pairs={{0,4},{2,6},{5,1},{7,3},{8,12},{10,14},{13,9},{15,11},{16,20},{18,... | collective-permute-start | bytes 3145736 | tf_op jit(solution)/shard_map/ppermute | solution.py:26
  86.1 1.3 %collective-permute-start.15 = (f32[2,256,512]{2,1,0:T(8,128)S(1)}, f32[2,256,512]{2,1,0:T(8,128)S(1)}, u32[]{:S(2)}, u32[]{:S(2)}) collective-permute-start(f32[2,256,512]{2,1,0:T(8,128)S(1)} %collective-permute-done.6.refs_1_), channel_id=1, source_target_pairs={{1,5},{3,7},{4,0},{6,2},{9,13},{11,15},{12,8},{14,10},{17,21},{19,... | collective-permute-start | bytes 3145736 | tf_op jit(solution)/shard_map/ppermute | solution.py:26
  87.4 1.3 %collective-permute-start.4 = (f32[384,768]{1,0:T(8,128)S(1)}, f32[384,768]{1,0:T(8,128)S(1)}, u32[]{:S(2)}, u32[]{:S(2)}) collective-permute-start(f32[384,768]{1,0:T(8,128)S(1)} %collective-permute-done.factor.refs_0_), channel_id=1, source_target_pairs={{0,4},{1,5},{2,6},{3,7},{4,0},{5,1},{6,2},{7,3},{8,12},{9,13},{10,... | collective-permute-start | bytes 3538952 | tf_op jit(solution)/shard_map/ppermute | solution.py:26
  88.7 0.0 collective-permute-done.16.refs_3_
  88.7 2.0 %collective-permute-start.18 = (f32[384,768]{1,0:T(8,128)S(1)}, f32[384,768]{1,0:T(8,128)S(1)}, u32[]{:S(2)}, u32[]{:S(2)}) collective-permute-start(f32[384,768]{1,0:T(8,128)S(1)} %collective-permute-done.5.refs_2_), channel_id=1, source_target_pairs={{0,4},{2,6},{5,1},{7,3},{8,12},{10,14},{13,9},{15,11},{16,20},{18,... | collective-permute-start | bytes 3538952 | tf_op jit(solution)/shard_map/ppermute | solution.py:26
  90.7 0.0 collective-permute-done.15.refs_2_
  90.7 8.5 %shard_map.89 = (f32[2,384,512]{2,1,0:T(8,128)S(1)}, bf16[2,768,512]{2,1,0:T(8,128)(2,1)S(1)}, bf16[2,1536,512]{2,1,0:T(8,128)(2,1)S(1)}, f32[2,512]{1,0:T(2,128)S(1)}) custom-call(s32[2,4,256]{2,1,0:T(4,128)S(1)} %get-tuple-element.37.index, bf16[2,4,768,256]{3,2,1,0:T(8,128)(2,1)S(1)} %get-tuple-element.41.pick_high, ...), custom_call_target="tpu_custom_call" | custom-call | bytes 1000 | tf_op jit(solution)/shard_map/pallas_call | solution.py:310
  99.3 0.0 collective-permute-done.14.border
  99.3 1.4 %shard_map.90 = (bf16[384,1536]{1,0:T(8,128)(2,1)S(1)}, f32[2,384,512]{2,1,0:T(8,128)S(1)}) custom-call(f32[384,1536]{1,0:T(8,128)S(1)} %collective-permute-done.14.border, bf16[2,1536,512]{2,1,0:T(8,128)(2,1)S(1)} %get-tuple-element.54.lower_high), custom_call_target="tpu_custom_call" | custom-call | bytes 1000 | tf_op jit(solution)/shard_map/pallas_call | solution.py:310
  100.7 0.0 collective-permute-done.12.refs_3_
  100.7 1.3 %collective-permute-start.17 = (f32[384,768]{1,0:T(8,128)S(1)}, f32[384,768]{1,0:T(8,128)S(1)}, u32[]{:S(2)}, u32[]{:S(2)}) collective-permute-start(f32[384,768]{1,0:T(8,128)S(1)} %collective-permute-done.12.refs_3_), channel_id=1, source_target_pairs={{1,5},{3,7},{4,0},{6,2},{9,13},{11,15},{12,8},{14,10},{17,21},{19,... | collective-permute-start | bytes 3538952 | tf_op jit(solution)/shard_map/ppermute | solution.py:26
  102.0 0.0 collective-permute-done.4.refs_1_
  102.0 0.0 collective-permute-done.18.refs_5_
  102.0 3.4 %collective-permute-done.17.refs_4_ = f32[384,768]{1,0:T(8,128)S(1)} collective-permute-done((f32[384,768]{1,0:T(8,128)S(1)}, f32[384,768]{1,0:T(8,128)S(1)}, u32[]{:S(2)}, u32[]{:S(2)}) %collective-permute-start.17) | collective-permute-done | bytes 1179680 | tf_op jit(solution)/shard_map/ppermute | solution.py:26
  105.4 3.6 %shard_map.91 = f32[1,1792]{1,0:T(1,128)S(1)} custom-call(f32[384,768]{1,0:T(8,128)S(1)} %collective-permute-done.factor.refs_0_, f32[384,768]{1,0:T(8,128)S(1)} %collective-permute-done.4.refs_1_, f32[384,768]{1,0:T(8,128)S(1)} %collective-permute-done.5.refs_2_, f32[384,768]{1,0:T(8,128)S(1)} %collective-permute-done.12.refs_3_, ...), custom_call_target="tpu_custom_call" | custom-call | bytes 1000 | tf_op jit(solution)/shard_map/pallas_call | solution.py:310
  109.0 0.2 collective-permute-start.19
  109.2 1.0 collective-permute-done.19
  110.2 1.8 %collective-permute-start.20 = (f32[1,1792]{1,0:T(1,128)S(1)}, f32[1,1792]{1,0:T(1,128)S(1)}, u32[]{:S(2)}, u32[]{:S(2)}) collective-permute-start(f32[1,1792]{1,0:T(1,128)S(1)} %add.3.refs_0_), channel_id=1, source_target_pairs={{0,2},{1,3},{2,0},{3,1},{4,6},{5,7},{6,4},{7,5},{8,10},{9,11},{10,... | collective-permute-start | bytes 21512 | tf_op jit(solution)/shard_map/ppermute | solution.py:26
  112.0 2.4 %collective-permute-start.21 = (f32[1,1792]{1,0:T(1,128)S(1)}, f32[1,1792]{1,0:T(1,128)S(1)}, u32[]{:S(2)}, u32[]{:S(2)}) collective-permute-start(f32[1,1792]{1,0:T(1,128)S(1)} %add.3.refs_0_), channel_id=1, source_target_pairs={{0,1},{1,0},{2,3},{3,2},{4,5},{5,4},{6,7},{7,6},{8,9},{9,8},{10,11... | collective-permute-start | bytes 21512 | tf_op jit(solution)/shard_map/ppermute | solution.py:26
  114.4 0.0 collective-permute-start.22
  114.4 0.0 collective-permute-done.20.refs_1_
  114.4 1.6 %collective-permute-done.21.refs_2_ = f32[1,1792]{1,0:T(1,128)S(1)} collective-permute-done((f32[1,1792]{1,0:T(1,128)S(1)}, f32[1,1792]{1,0:T(1,128)S(1)}, u32[]{:S(2)}, u32[]{:S(2)}) %collective-permute-start.21) | collective-permute-done | bytes 7200 | tf_op jit(solution)/shard_map/ppermute | solution.py:26
  116.0 2.9 %collective-permute-done.22.refs_3_ = f32[1,1792]{1,0:T(1,128)S(1)} collective-permute-done((f32[1,1792]{1,0:T(1,128)S(1)}, f32[1,1792]{1,0:T(1,128)S(1)}, u32[]{:S(2)}, u32[]{:S(2)}) %collective-permute-start.22) | collective-permute-done | bytes 7200 | tf_op jit(solution)/shard_map/ppermute | solution.py:26
  118.9 1.3 %shard_map.92 = (f32[1,768]{1,0:T(1,128)}, f32[2,512]{1,0:T(2,128)}) custom-call(s32[16]{0:T(128)} %parent_ref.3, f32[1,1792]{1,0:T(1,128)S(1)} %add.3.refs_0_, f32[1,1792]{1,0:T(1,128)S(1)} %collective-permute-done.20.refs_1_, f32[1,1792]{1,0:T(1,128)S(1)} %collective-permute-done.21.refs_2_, f32[1,1792]{1,0:T(1,128)S(1)} %collective-permute-done.22.refs_3_), custom_call_target="tpu_custom_call" | custom-call | bytes 1000 | tf_op jit(solution)/shard_map/pallas_call | solution.py:310
  (1 shorter events, 0.0 us)
Async XLA Ops:
  0.6 19.3 %collective-permute-start.5 = (f32[384,768]{1,0:T(8,128)}, f32[384,768]{1,0:T(8,128)S(1)}, u32[]{:S(2)}, u32[]{:S(2)}) collective-permute-start(f32[384,768]{1,0:T(8,128)} %bitcast.5), channel_id=1, source_target_pairs={{0,2},{2,0},{5,7},{7,5},{8,10},{10,8},{13,15},{15,13},{16,18},{18,... | collective-permute-start | bytes 3538952 | tf_op jit(solution)/shard_map/ppermute | solution.py:26
  5.5 4.9 %collective-permute-start.1 = (f32[2,256,512]{2,1,0:T(8,128)}, f32[2,256,512]{2,1,0:T(8,128)S(1)}, u32[]{:S(2)}, u32[]{:S(2)}) collective-permute-start(f32[2,256,512]{2,1,0:T(8,128)} %own_rows.1), channel_id=1, source_target_pairs={{0,4},{1,5},{2,6},{3,7},{4,0},{5,1},{6,2},{7,3},{8,12},{9,13},{10,... | collective-permute-start | bytes 3145736 | tf_op jit(solution)/shard_map/ppermute | solution.py:26
  5.6 15.0 %collective-permute-start = (f32[384,768]{1,0:T(8,128)}, f32[384,768]{1,0:T(8,128)S(1)}, u32[]{:S(2)}, u32[]{:S(2)}) collective-permute-start(f32[384,768]{1,0:T(8,128)} %bitcast.6), channel_id=1, source_target_pairs={{0,0},{1,4},{2,2},{3,6},{4,1},{5,5},{6,3},{7,7},{8,8},{9,12},{10,1... | collective-permute-start | bytes 3538952 | tf_op jit(solution)/shard_map/ppermute | solution.py:36
  7.5 2.9 %collective-permute-start.2 = (f32[2,128,512]{2,1,0:T(8,128)}, f32[2,128,512]{2,1,0:T(8,128)S(1)}, u32[]{:S(2)}, u32[]{:S(2)}) collective-permute-start(f32[2,128,512]{2,1,0:T(8,128)} %own_inverse.1), channel_id=1, source_target_pairs={{0,4},{1,5},{2,6},{3,7},{4,0},{5,1},{6,2},{7,3},{8,12},{9,13},{10,... | collective-permute-start | bytes 1572872 | tf_op jit(solution)/shard_map/ppermute | solution.py:26
  10.5 50.9 %copy-start = (f32[1,384,1536]{2,1,0:T(8,128)S(1)}, f32[1,384,1536]{2,1,0:T(8,128)}, u32[]{:S(2)}) copy-start(f32[1,384,1536]{2,1,0:T(8,128)} %param.7) | copy-start | bytes 7077892
  19.9 1.5 %collective-permute-start.7 = (f32[384,768]{1,0:T(8,128)S(1)}, f32[384,768]{1,0:T(8,128)S(1)}, u32[]{:S(2)}, u32[]{:S(2)}) collective-permute-start(f32[384,768]{1,0:T(8,128)S(1)} %get-tuple-element.39), channel_id=1, source_target_pairs={{0,0},{1,4},{2,2},{3,6},{4,1},{5,5},{6,3},{7,7},{8,8},{9,12},{10,1... | collective-permute-start | bytes 3538952 | tf_op jit(solution)/shard_map/ppermute | solution.py:36
  20.6 2.8 %collective-permute-start.3 = (f32[2,256,512]{2,1,0:T(8,128)S(1)}, f32[2,256,512]{2,1,0:T(8,128)S(1)}, u32[]{:S(2)}, u32[]{:S(2)}) collective-permute-start(f32[2,256,512]{2,1,0:T(8,128)S(1)} %get-tuple-element.35), channel_id=1, source_target_pairs={{0,0},{1,4},{2,2},{3,6},{4,1},{5,5},{6,3},{7,7},{8,8},{9,12},{10,1... | collective-permute-start | bytes 3145736 | tf_op jit(solution)/shard_map/ppermute | solution.py:36
  21.4 27.4 %collective-permute-start.9 = (f32[384,768]{1,0:T(8,128)S(1)}, f32[384,768]{1,0:T(8,128)S(1)}, u32[]{:S(2)}, u32[]{:S(2)}) collective-permute-start(f32[384,768]{1,0:T(8,128)S(1)} %collective-permute-done.7.refs_0_), channel_id=1, source_target_pairs={{0,2},{1,3},{2,0},{3,1},{4,6},{5,7},{6,4},{7,5},{8,10},{9,11},{10,... | collective-permute-start | bytes 3538952 | tf_op jit(solution)/shard_map/ppermute | solution.py:26
  23.5 37.9 %collective-permute-start.13 = (f32[2,256,512]{2,1,0:T(8,128)S(1)}, f32[2,256,512]{2,1,0:T(8,128)S(1)}, u32[]{:S(2)}, u32[]{:S(2)}) collective-permute-start(f32[2,256,512]{2,1,0:T(8,128)S(1)} %collective-permute-done.3.own_rows), channel_id=1, source_target_pairs={{0,2},{2,0},{5,7},{7,5},{8,10},{10,8},{13,15},{15,13},{16,18},{18,... | collective-permute-start | bytes 3145736 | tf_op jit(solution)/shard_map/ppermute | solution.py:26
  25.4 39.1 %collective-permute-start.8 = (f32[384,768]{1,0:T(8,128)S(1)}, f32[384,768]{1,0:T(8,128)S(1)}, u32[]{:S(2)}, u32[]{:S(2)}) collective-permute-start(f32[384,768]{1,0:T(8,128)S(1)} %collective-permute-done.7.refs_0_), channel_id=1, source_target_pairs={{0,4},{1,5},{2,6},{3,7},{4,0},{5,1},{6,2},{7,3},{8,12},{9,13},{10,... | collective-permute-start | bytes 3538952 | tf_op jit(solution)/shard_map/ppermute | solution.py:26
  48.8 15.8 %collective-permute-start.10 = (f32[384,768]{1,0:T(8,128)S(1)}, f32[384,768]{1,0:T(8,128)S(1)}, u32[]{:S(2)}, u32[]{:S(2)}) collective-permute-start(f32[384,768]{1,0:T(8,128)S(1)} %collective-permute-done.9.refs_2_), channel_id=1, source_target_pairs={{0,4},{1,5},{2,6},{3,7},{4,0},{5,1},{6,2},{7,3},{8,12},{9,13},{10,... | collective-permute-start | bytes 3538952 | tf_op jit(solution)/shard_map/ppermute | solution.py:26
  61.4 37.9 %collective-permute-start.14 = (f32[384,1536]{1,0:T(8,128)S(1)}, f32[384,1536]{1,0:T(8,128)S(1)}, u32[]{:S(2)}, u32[]{:S(2)}) collective-permute-start(f32[384,1536]{1,0:T(8,128)S(1)} %bitcast.4), channel_id=1, source_target_pairs={{0,0},{1,4},{2,2},{3,6},{4,1},{5,5},{6,3},{7,7},{8,8},{9,12},{10,1... | collective-permute-start | bytes 7077896 | tf_op jit(solution)/shard_map/ppermute | solution.py:36
  62.2 9.9 %collective-permute-start.11 = (f32[2,256,512]{2,1,0:T(8,128)S(1)}, f32[2,256,512]{2,1,0:T(8,128)S(1)}, u32[]{:S(2)}, u32[]{:S(2)}) collective-permute-start(f32[2,256,512]{2,1,0:T(8,128)S(1)} %collective-permute-done.3.own_rows), channel_id=1, source_target_pairs={{0,4},{1,5},{2,6},{3,7},{4,0},{5,1},{6,2},{7,3},{8,12},{9,13},{10,... | collective-permute-start | bytes 3145736 | tf_op jit(solution)/shard_map/ppermute | solution.py:26
  63.6 15.7 %collective-permute-start.6 = (f32[2,256,512]{2,1,0:T(8,128)S(1)}, f32[2,256,512]{2,1,0:T(8,128)S(1)}, u32[]{:S(2)}, u32[]{:S(2)}) collective-permute-start(f32[2,256,512]{2,1,0:T(8,128)S(1)} %collective-permute-done.3.own_rows), channel_id=1, source_target_pairs={{1,3},{3,1},{4,6},{6,4},{9,11},{11,9},{12,14},{14,12},{17,19},{19,... | collective-permute-start | bytes 3145736 | tf_op jit(solution)/shard_map/ppermute | solution.py:26
  79.3 21.3 %collective-permute-start.12 = (f32[384,768]{1,0:T(8,128)S(1)}, f32[384,768]{1,0:T(8,128)S(1)}, u32[]{:S(2)}, u32[]{:S(2)}) collective-permute-start(f32[384,768]{1,0:T(8,128)S(1)} %collective-permute-done.factor.refs_0_), channel_id=1, source_target_pairs={{1,3},{3,1},{4,6},{6,4},{9,11},{11,9},{12,14},{14,12},{17,19},{19,... | collective-permute-start | bytes 3538952 | tf_op jit(solution)/shard_map/ppermute | solution.py:26
  80.3 8.4 %collective-permute-start.16 = (f32[2,256,512]{2,1,0:T(8,128)S(1)}, f32[2,256,512]{2,1,0:T(8,128)S(1)}, u32[]{:S(2)}, u32[]{:S(2)}) collective-permute-start(f32[2,256,512]{2,1,0:T(8,128)S(1)} %collective-permute-done.13.refs_0_), channel_id=1, source_target_pairs={{0,4},{2,6},{5,1},{7,3},{8,12},{10,14},{13,9},{15,11},{16,20},{18,... | collective-permute-start | bytes 3145736 | tf_op jit(solution)/shard_map/ppermute | solution.py:26
  86.1 4.6 %collective-permute-start.15 = (f32[2,256,512]{2,1,0:T(8,128)S(1)}, f32[2,256,512]{2,1,0:T(8,128)S(1)}, u32[]{:S(2)}, u32[]{:S(2)}) collective-permute-start(f32[2,256,512]{2,1,0:T(8,128)S(1)} %collective-permute-done.6.refs_1_), channel_id=1, source_target_pairs={{1,5},{3,7},{4,0},{6,2},{9,13},{11,15},{12,8},{14,10},{17,21},{19,... | collective-permute-start | bytes 3145736 | tf_op jit(solution)/shard_map/ppermute | solution.py:26
  87.4 14.6 %collective-permute-start.4 = (f32[384,768]{1,0:T(8,128)S(1)}, f32[384,768]{1,0:T(8,128)S(1)}, u32[]{:S(2)}, u32[]{:S(2)}) collective-permute-start(f32[384,768]{1,0:T(8,128)S(1)} %collective-permute-done.factor.refs_0_), channel_id=1, source_target_pairs={{0,4},{1,5},{2,6},{3,7},{4,0},{5,1},{6,2},{7,3},{8,12},{9,13},{10,... | collective-permute-start | bytes 3538952 | tf_op jit(solution)/shard_map/ppermute | solution.py:26
  88.7 13.3 %collective-permute-start.18 = (f32[384,768]{1,0:T(8,128)S(1)}, f32[384,768]{1,0:T(8,128)S(1)}, u32[]{:S(2)}, u32[]{:S(2)}) collective-permute-start(f32[384,768]{1,0:T(8,128)S(1)} %collective-permute-done.5.refs_2_), channel_id=1, source_target_pairs={{0,4},{2,6},{5,1},{7,3},{8,12},{10,14},{13,9},{15,11},{16,20},{18,... | collective-permute-start | bytes 3538952 | tf_op jit(solution)/shard_map/ppermute | solution.py:26
  100.7 4.7 %collective-permute-start.17 = (f32[384,768]{1,0:T(8,128)S(1)}, f32[384,768]{1,0:T(8,128)S(1)}, u32[]{:S(2)}, u32[]{:S(2)}) collective-permute-start(f32[384,768]{1,0:T(8,128)S(1)} %collective-permute-done.12.refs_3_), channel_id=1, source_target_pairs={{1,5},{3,7},{4,0},{6,2},{9,13},{11,15},{12,8},{14,10},{17,21},{19,... | collective-permute-start | bytes 3538952 | tf_op jit(solution)/shard_map/ppermute | solution.py:26
  109.0 1.2 %collective-permute-start.19 = (f32[1,1792]{1,0:T(1,128)S(1)}, f32[1,1792]{1,0:T(1,128)S(1)}, u32[]{:S(2)}, u32[]{:S(2)}) collective-permute-start(f32[1,1792]{1,0:T(1,128)S(1)} %shard_map.91), channel_id=1, source_target_pairs={{0,4},{1,5},{2,6},{3,7},{4,0},{5,1},{6,2},{7,3},{8,12},{9,13},{10,... | collective-permute-start | bytes 21512 | tf_op jit(solution)/shard_map/ppermute | solution.py:26
  110.2 4.1 %collective-permute-start.20 = (f32[1,1792]{1,0:T(1,128)S(1)}, f32[1,1792]{1,0:T(1,128)S(1)}, u32[]{:S(2)}, u32[]{:S(2)}) collective-permute-start(f32[1,1792]{1,0:T(1,128)S(1)} %add.3.refs_0_), channel_id=1, source_target_pairs={{0,2},{1,3},{2,0},{3,1},{4,6},{5,7},{6,4},{7,5},{8,10},{9,11},{10,... | collective-permute-start | bytes 21512 | tf_op jit(solution)/shard_map/ppermute | solution.py:26
  112.0 4.0 %collective-permute-start.21 = (f32[1,1792]{1,0:T(1,128)S(1)}, f32[1,1792]{1,0:T(1,128)S(1)}, u32[]{:S(2)}, u32[]{:S(2)}) collective-permute-start(f32[1,1792]{1,0:T(1,128)S(1)} %add.3.refs_0_), channel_id=1, source_target_pairs={{0,1},{1,0},{2,3},{3,2},{4,5},{5,4},{6,7},{7,6},{8,9},{9,8},{10,11... | collective-permute-start | bytes 21512 | tf_op jit(solution)/shard_map/ppermute | solution.py:26
  114.4 4.5 %collective-permute-start.22 = (f32[1,1792]{1,0:T(1,128)S(1)}, f32[1,1792]{1,0:T(1,128)S(1)}, u32[]{:S(2)}, u32[]{:S(2)}) collective-permute-start(f32[1,1792]{1,0:T(1,128)S(1)} %add.3.refs_0_), channel_id=1, source_target_pairs={{0,3},{1,2},{2,1},{3,0},{4,7},{5,6},{6,5},{7,4},{8,11},{9,10},{10,... | collective-permute-start | bytes 21512 | tf_op jit(solution)/shard_map/ppermute | solution.py:26

commit v4 on v2

--- a/solution.py
+++ b/solution.py
@@ -15,12 +15,13 @@
     return jax.ShapeDtypeStruct(shape, dtype)
 
 
-def exchange(value, leaf_mask, front_mask):
+def exchange(value, leaf_mask, front_mask, parity=None):
     fronts = lax.axis_size("front")
     pairs = [
         (leaf * fronts + front, (leaf ^ leaf_mask) * fronts + (front ^ front_mask))
         for leaf in range(lax.axis_size("leaf"))
         for front in range(fronts)
+        if parity is None or (leaf ^ front) & 1 == parity
     ]
     return lax.ppermute(value, ("leaf", "front"), pairs)
 
@@ -54,6 +55,15 @@
     owner = (leaf & -2) | (front & 1)
     block = (front & -2) | (leaf & 1)
     return owner, block
+
+
+def keeps():
+    return ((lax.axis_index("leaf") ^ lax.axis_index("front")) & 1) == 0
+
+
+def store(pair, action):
+    for ref, chosen in zip(pair, (keeps(), jnp.logical_not(keeps()))):
+        pl.when(chosen)(functools.partial(action, ref))
 
 
 def rounded(value):
@@ -113,17 +123,30 @@
     return rounded(jnp.where(position == index, 1.0, 0.0))
 
 
+def unpacked(pieces, refs):
+    pairs = [(refs[0], refs[0]), (refs[1], refs[1])]
+    for at in range(2, 2 * pieces - 2, 4):
+        near_keep, near_swap, far_keep, far_swap = refs[at : at + 4]
+        pairs += [(near_keep, near_swap), (far_keep, far_swap)]
+    return pairs
+
+
 def diagonal_kernel(pieces, index, *refs):
-    diagonal = refs[:pieces]
-    diag_high, diag_low, pick_high, pick_low, parent_sum = refs[pieces:]
+    diagonal = unpacked(pieces, refs)
+    diag_high, diag_low, pick_high, pick_low, parent_sum = refs[2 * pieces - 2 :]
     _, block = place_of()
-    own_rows, size = diagonal[0].shape
-    parent_sum[...] = column_sum(diagonal[0][...] * diagonal[0][...])
-    for mask in range(pieces):
+    own_rows, size = refs[0].shape
+    parent_sum[...] = column_sum(refs[0][...] * refs[0][...])
+    for mask, pair in enumerate(diagonal):
         start = pl.multiple_of((block ^ mask) * own_rows, 16)
-        high, low = halves(diagonal[mask][...])
-        diag_high[pl.ds(start, own_rows), :] = high
-        diag_low[pl.ds(start, own_rows), :] = low
+
+        def put(ref, start=start):
+            diag_high[pl.ds(start, own_rows), :], diag_low[pl.ds(start, own_rows), :] = halves(ref[...])
+
+        if mask < 2:
+            put(pair[0])
+        else:
+            store(pair, put)
     for kid in range(2):
         for mask in range(pieces):
             pick = picks(index[kid, mask : mask + 1, :], 0, size)
@@ -247,37 +270,37 @@
     kid_block = kid_rows.shape[1]
     half = jnp.bfloat16
 
-    def over_fronts(value):
+    def over_fronts(value, parity=None):
         parts = {0: value}
         bit = 2
         while bit < pieces:
             for mask in list(parts):
-                parts[mask | bit] = exchange(parts[mask], 0, bit)
+                parts[mask | bit] = exchange(parts[mask], 0, bit, parity)
             bit *= 2
         return parts
 
     def spread(parts, gate_own, gate_rest):
-        shared = {1: exchange(after(parts[0], *gate_own), 1, 0)}
-        for mask in list(parts)[1:]:
-            shared[mask | 1] = exchange(after(parts[mask], *gate_rest), 1, 0)
-        parts = parts | shared
+        others = {mask | 1: exchange(after(part, *(gate_rest if mask else gate_own)), 1, 0) for mask, part in parts.items()}
+        parts = parts | others
         return [parts[mask] for mask in range(pieces)]
 
     last = pieces - 2
-    raw_diagonal = over_fronts(diagonal)
+    keep_diagonal = over_fronts(diagonal, 0)
     own_diagonal = cross(diagonal)
     kid_shape = (2, kid_block + kid_inverse.shape[1], kid_size)
     own_kids, index = call(
         select_kernel, (shape_of(kid_shape), shape_of((2, pieces, kid_block), jnp.int32)), 6, scalars=1, loose=4
     )(child_parent, child_index, kid_rows, kid_inverse, exchange(kid_rows, 1, 0), exchange(kid_inverse, 1, 0))
-    own_kids = cross(after(own_kids, own_diagonal, raw_diagonal[last]))
-
-    diagonal_parts = {mask: cross(after(value, own_kids)) for mask, value in raw_diagonal.items() if mask}
-    crossed = diagonal_parts[last]
-    diagonal_parts = spread({0: own_diagonal} | diagonal_parts, [own_kids], [own_kids])
+    own_kids = cross(after(own_kids, own_diagonal, keep_diagonal[last]))
+    swap_diagonal = over_fronts(own_diagonal, 1)
     own_factor = cross(after(factor, own_kids))
-    own_border_rows = cross(after(border, crossed))
-    kid_parts = over_fronts(own_kids)
+    kid_parts = over_fronts(after(own_kids, swap_diagonal[last]))
+
+    diagonal_parts = [own_diagonal, exchange(after(own_diagonal, own_kids), 1, 0)]
+    for mask in list(keep_diagonal)[1:]:
+        far_swap = exchange(after(keep_diagonal[mask], own_kids), 1, 0, 0)
+        far_keep = exchange(after(swap_diagonal[mask], own_kids), 1, 0, 1)
+        diagonal_parts += [keep_diagonal[mask], swap_diagonal[mask], far_keep, far_swap]
 
     diag_high, diag_low, pick_high, pick_low, parent_sum = call(
         functools.partial(diagonal_kernel, pieces),
@@ -290,10 +313,11 @@
         ),
         10,
     )(index, *diagonal_parts)
-    kids_here = after(kid_parts[last], pick_high)
+    own_border_rows = cross(after(border, own_factor, pick_high))
+    kids_here = kid_parts[last]
     factor_parts = over_fronts(after(own_factor, kids_here))
     factor_parts[0] = own_factor
-    kid_parts = spread(kid_parts, [], [pick_high])
+    kid_parts = spread(kid_parts, [own_kids], [pick_high])
 
     reduced, lift_high, lower_high, weights, kid_sum = call(
         functools.partial(kid_kernel, pieces),

time: 110 us -> 105 us (0.955)
  waiting for transfers between devices: 26.9 us -> 22.7 us
    ppermute x15 -> x17, waiting for transfers between devices: 26.9 us -> 22.7 us  [exchange(): return lax.ppermute(value, ('leaf', 'front'), pairs)]
    ppermute x15 -> x17, starting transfers between devices: 44.9 us -> 46.7 us  [exchange(): return lax.ppermute(value, ('leaf', 'front'), pairs)]
    ppermute x5 -> x4, starting transfers between devices: 6.01 us -> 4.32 us  [cross(): return lax.ppermute(value, ('leaf', 'front'), pairs)]
  transfers between devices with their start and end apart: 20 -> 21, of which waited for: 11 -> 11; matrix products, arithmetic and copies ran while one was open for 0% -> 0% of each run, Pallas kernels for 24% -> 25%
where the time goes in v4:
time: 105 us
  starting transfers between devices  51 us (49%)
  Pallas kernels  30.6 us (29%)
  waiting for transfers between devices  22.7 us (22%)
    ppermute x17, starting transfers between devices, exchange(): return lax.ppermute(value, ('leaf', 'front'), pairs)  46.7 us
    pallas_call x6, Pallas kernels, run(): pl.pallas_call(kernel, out_shape=results, in_specs=specs, out_specs=jax.t...  30.6 us
    ppermute x17, waiting for transfers between devices, exchange(): return lax.ppermute(value, ('leaf', 'front'), pairs)  22.7 us
    ppermute x4, starting transfers between devices, cross(): return lax.ppermute(value, ('leaf', 'front'), pairs)  4.32 us
  transfers between devices with their start and end apart: 21, of which 11 were waited for; matrix products, arithmetic and copies ran while one was open for 0% of the time, Pallas kernels for 25%

profile of v4, /device:TPU:0, one launch (start us, length us, event | category | flops | bytes accessed | tf_op | source)
XLA Modules:
  0.0 105.2 jit_solution(2069241829136988127)
XLA Ops:
  0.6 0.5 collective-permute-start
  1.1 0.0 copy-start.1
  1.2 1.8 %collective-permute-start.2 = (f32[192,768]{1,0:T(8,128)}, f32[192,768]{1,0:T(8,128)S(1)}, u32[]{:S(2)}, u32[]{:S(2)}) collective-permute-start(f32[192,768]{1,0:T(8,128)} %bitcast.5), channel_id=1, source_target_pairs={{0,0},{1,4},{2,2},{3,6},{4,1},{5,5},{6,3},{7,7},{8,8},{9,12},{10,1... | collective-permute-start | bytes 1769480 | tf_op jit(solution)/shard_map/ppermute | solution.py:36
  3.0 4.4 %collective-permute-start.3 = (f32[192,768]{1,0:T(8,128)}, f32[192,768]{1,0:T(8,128)S(1)}, u32[]{:S(2)}, u32[]{:S(2)}) collective-permute-start(f32[192,768]{1,0:T(8,128)} %bitcast.6), channel_id=1, source_target_pairs={{0,2},{2,0},{5,7},{7,5},{8,10},{10,8},{13,15},{15,13},{16,18},{18,... | collective-permute-start | bytes 1769480 | tf_op jit(solution)/shard_map/ppermute | solution.py:26
  7.4 0.1 collective-permute-start.1
  7.5 2.1 %collective-permute-done.1.other_inverse = f32[2,128,512]{2,1,0:T(8,128)S(1)} collective-permute-done((f32[2,128,512]{2,1,0:T(8,128)}, f32[2,128,512]{2,1,0:T(8,128)S(1)}, u32[]{:S(2)}, u32[]{:S(2)}) %collective-permute-start.1) | collective-permute-done | bytes 524320 | tf_op jit(solution)/shard_map/ppermute | solution.py:26
  9.6 0.0 collective-permute-done.other_rows
  9.6 1.6 %shard_map.86 = (f32[2,384,512]{2,1,0:T(8,128)S(1)}, s32[2,4,256]{2,1,0:T(4,128)S(1)}) custom-call(s32[16]{0:T(128)} %parent_ref.3, s32[16,1024]{1,0:T(8,128)} %index_ref.1, f32[2,256,512]{2,1,0:T(8,128)} %own_rows.1, f32[2,128,512]{2,1,0:T(8,128)} %own_inverse.1, f32[2,256,512]{2,1,0:T(8,128)S(1)} %collective-permute-done.other_rows, ...), custom_call_target="tpu_custom_call" | custom-call | bytes 1000 | tf_op jit(solution)/shard_map/pallas_call | solution.py:252
  11.2 0.0 collective-permute-done.2.refs_0_
  11.2 4.3 %collective-permute-done.3.refs_2_ = f32[192,768]{1,0:T(8,128)S(1)} collective-permute-done((f32[192,768]{1,0:T(8,128)}, f32[192,768]{1,0:T(8,128)S(1)}, u32[]{:S(2)}, u32[]{:S(2)}) %collective-permute-start.3) | collective-permute-done | bytes 589856 | tf_op jit(solution)/shard_map/ppermute | solution.py:26
  15.5 0.8 collective-permute-start.4
  16.3 0.7 collective-permute-start.6
  17.0 0.0 collective-permute-done.4.refs_0_
  17.0 0.0 copy-done.1
  17.0 0.7 collective-permute-start.5
  17.7 0.0 collective-permute-done.6.refs_3_
  17.7 2.1 %collective-permute-start.7 = (f32[2,384,512]{2,1,0:T(8,128)S(1)}, f32[2,384,512]{2,1,0:T(8,128)S(1)}, u32[]{:S(2)}, u32[]{:S(2)}) collective-permute-start(f32[2,384,512]{2,1,0:T(8,128)S(1)} %collective-permute-done.4.refs_0_), channel_id=1, source_target_pairs={{0,2},{1,3},{2,0},{3,1},{4,6},{5,7},{6,4},{7,5},{8,10},{9,11},{10,... | collective-permute-start | bytes 4718600 | tf_op jit(solution)/shard_map/ppermute | solution.py:26
  19.8 1.3 %collective-permute-start.11 = (f32[192,768]{1,0:T(8,128)S(1)}, f32[192,768]{1,0:T(8,128)S(1)}, u32[]{:S(2)}, u32[]{:S(2)}) collective-permute-start(f32[192,768]{1,0:T(8,128)S(1)} %collective-permute-done.6.refs_3_), channel_id=1, source_target_pairs={{1,5},{3,7},{4,0},{6,2},{9,13},{11,15},{12,8},{14,10},{17,21},{19,... | collective-permute-start | bytes 1769480 | tf_op jit(solution)/shard_map/ppermute | solution.py:26
  21.1 20.5 %collective-permute-start.10 = (f32[192,768]{1,0:T(8,128)S(1)}, f32[192,768]{1,0:T(8,128)S(1)}, u32[]{:S(2)}, u32[]{:S(2)}) collective-permute-start(f32[192,768]{1,0:T(8,128)S(1)} %collective-permute-done.2.refs_0_), channel_id=1, source_target_pairs={{0,4},{1,5},{2,6},{3,7},{4,0},{5,1},{6,2},{7,3},{8,12},{9,13},{10,... | collective-permute-start | bytes 1769480 | tf_op jit(solution)/shard_map/ppermute | solution.py:26
  41.7 2.0 %collective-permute-start.12 = (f32[192,768]{1,0:T(8,128)S(1)}, f32[192,768]{1,0:T(8,128)S(1)}, u32[]{:S(2)}, u32[]{:S(2)}) collective-permute-start(f32[192,768]{1,0:T(8,128)S(1)} %collective-permute-done.3.refs_2_), channel_id=1, source_target_pairs={{0,4},{2,6},{5,1},{7,3},{8,12},{10,14},{13,9},{15,11},{16,20},{18,... | collective-permute-start | bytes 1769480 | tf_op jit(solution)/shard_map/ppermute | solution.py:26
  43.6 0.0 collective-permute-done.11.refs_4_
  43.6 0.2 collective-permute-done.10.refs_1_
  43.9 1.3 %collective-permute-done.12.refs_5_ = f32[192,768]{1,0:T(8,128)S(1)} collective-permute-done((f32[192,768]{1,0:T(8,128)S(1)}, f32[192,768]{1,0:T(8,128)S(1)}, u32[]{:S(2)}, u32[]{:S(2)}) %collective-permute-start.12) | collective-permute-done | bytes 589856 | tf_op jit(solution)/shard_map/ppermute | solution.py:26
  45.2 0.0 copy-start
  45.2 5.5 %shard_map.87 = (bf16[768,768]{1,0:T(8,128)(2,1)S(1)}, bf16[768,768]{1,0:T(8,128)(2,1)S(1)}, bf16[2,4,768,256]{3,2,1,0:T(8,128)(2,1)S(1)}, bf16[2,4,768,256]{3,2,1,0:T(8,128)(2,1)S(1)}, f32[1,768]{1,0:T(1,128)S(1)}) custom-call(s32[2,4,256]{2,1,0:T(4,128)S(1)} %get-tuple-element.32.index, f32[192,768]{1,0:T(8,128)S(1)} %collective-permute-done.2.refs_0_, ...), custom_call_target="tpu_custom_call" | custom-call | bytes 1000 | tf_op jit(solution)/shard_map/pallas_call | solution.py:252
  50.7 0.0 collective-permute-done.5.factor.refs_0_
  50.8 0.0 copy-done
  50.8 1.0 collective-permute-start.13
  51.8 4.9 %collective-permute-start.14 = (f32[2,384,512]{2,1,0:T(8,128)S(1)}, f32[2,384,512]{2,1,0:T(8,128)S(1)}, u32[]{:S(2)}, u32[]{:S(2)}) collective-permute-start(f32[2,384,512]{2,1,0:T(8,128)S(1)} %collective-permute-done.4.refs_0_), channel_id=1, source_target_pairs={{0,4},{1,5},{2,6},{3,7},{4,0},{5,1},{6,2},{7,3},{8,12},{9,13},{10,... | collective-permute-start | bytes 4718600 | tf_op jit(solution)/shard_map/ppermute | solution.py:26
  56.7 0.0 collective-permute-done.7.refs_2_
  56.7 4.5 %collective-permute-start.15 = (f32[2,384,512]{2,1,0:T(8,128)S(1)}, f32[2,384,512]{2,1,0:T(8,128)S(1)}, u32[]{:S(2)}, u32[]{:S(2)}) collective-permute-start(f32[2,384,512]{2,1,0:T(8,128)S(1)} %collective-permute-done.7.refs_2_), channel_id=1, source_target_pairs={{0,4},{1,5},{2,6},{3,7},{4,0},{5,1},{6,2},{7,3},{8,12},{9,13},{10,... | collective-permute-start | bytes 4718600 | tf_op jit(solution)/shard_map/ppermute | solution.py:26
  61.2 1.9 %collective-permute-start.9 = (f32[384,768]{1,0:T(8,128)S(1)}, f32[384,768]{1,0:T(8,128)S(1)}, u32[]{:S(2)}, u32[]{:S(2)}) collective-permute-start(f32[384,768]{1,0:T(8,128)S(1)} %collective-permute-done.5.factor.refs_0_), channel_id=1, source_target_pairs={{0,2},{1,3},{2,0},{3,1},{4,6},{5,7},{6,4},{7,5},{8,10},{9,11},{10,... | collective-permute-start | bytes 3538952 | tf_op jit(solution)/shard_map/ppermute | solution.py:26
  63.1 0.0 collective-permute-start.8
  63.1 0.0 collective-permute-done.14.refs_1_
  63.1 1.2 %collective-permute-done.15.refs_3_ = f32[2,384,512]{2,1,0:T(8,128)S(1)} collective-permute-done((f32[2,384,512]{2,1,0:T(8,128)S(1)}, f32[2,384,512]{2,1,0:T(8,128)S(1)}, u32[]{:S(2)}, u32[]{:S(2)}) %collective-permute-start.15) | collective-permute-done | bytes 1572896 | tf_op jit(solution)/shard_map/ppermute | solution.py:26
  64.3 17.3 %shard_map.88 = (f32[2,384,512]{2,1,0:T(8,128)S(1)}, bf16[2,768,512]{2,1,0:T(8,128)(2,1)S(1)}, bf16[2,1536,512]{2,1,0:T(8,128)(2,1)S(1)}, f32[384,768]{1,0:T(8,128)S(1)}, f32[2,512]{1,0:T(2,128)S(1)}) custom-call(s32[2,4,256]{2,1,0:T(4,128)S(1)} %get-tuple-element.32.index, bf16[2,4,768,256]{3,2,1,0:T(8,128)(2,1)S(1)} %get-tuple-element.36.pick_high, ...), custom_call_target="tpu_custom_call" | custom-call | bytes 1000 | tf_op jit(solution)/shard_map/pallas_call | solution.py:252
  81.6 0.0 collective-permute-done.13.border
  81.6 1.4 %shard_map.89 = (bf16[384,1536]{1,0:T(8,128)(2,1)S(1)}, f32[2,384,512]{2,1,0:T(8,128)S(1)}) custom-call(f32[384,1536]{1,0:T(8,128)S(1)} %collective-permute-done.13.border, bf16[2,1536,512]{2,1,0:T(8,128)(2,1)S(1)} %get-tuple-element.43.lower_high), custom_call_target="tpu_custom_call" | custom-call | bytes 1000 | tf_op jit(solution)/shard_map/pallas_call | solution.py:252
  83.0 6.2 %collective-permute-done.9.refs_2_ = f32[384,768]{1,0:T(8,128)S(1)} collective-permute-done((f32[384,768]{1,0:T(8,128)S(1)}, f32[384,768]{1,0:T(8,128)S(1)}, u32[]{:S(2)}, u32[]{:S(2)}) %collective-permute-start.9) | collective-permute-done | bytes 1179680 | tf_op jit(solution)/shard_map/ppermute | solution.py:26
  89.2 0.0 collective-permute-start.16
  89.2 0.0 collective-permute-done.8.refs_1_
  89.2 2.8 %collective-permute-done.16.refs_3_ = f32[384,768]{1,0:T(8,128)S(1)} collective-permute-done((f32[384,768]{1,0:T(8,128)S(1)}, f32[384,768]{1,0:T(8,128)S(1)}, u32[]{:S(2)}, u32[]{:S(2)}) %collective-permute-start.16) | collective-permute-done | bytes 1179680 | tf_op jit(solution)/shard_map/ppermute | solution.py:26
  92.1 3.5 %shard_map.90 = f32[1,1792]{1,0:T(1,128)S(1)} custom-call(f32[384,768]{1,0:T(8,128)S(1)} %collective-permute-done.5.factor.refs_0_, f32[384,768]{1,0:T(8,128)S(1)} %collective-permute-done.8.refs_1_, f32[384,768]{1,0:T(8,128)S(1)} %collective-permute-done.9.refs_2_, f32[384,768]{1,0:T(8,128)S(1)} %collective-permute-done.16.refs_3_, ...), custom_call_target="tpu_custom_call" | custom-call | bytes 1000 | tf_op jit(solution)/shard_map/pallas_call | solution.py:252
  95.5 0.2 collective-permute-start.17
  95.8 1.0 collective-permute-done.17
  96.8 1.8 %collective-permute-start.18 = (f32[1,1792]{1,0:T(1,128)S(1)}, f32[1,1792]{1,0:T(1,128)S(1)}, u32[]{:S(2)}, u32[]{:S(2)}) collective-permute-start(f32[1,1792]{1,0:T(1,128)S(1)} %add.3.refs_0_), channel_id=1, source_target_pairs={{0,2},{1,3},{2,0},{3,1},{4,6},{5,7},{6,4},{7,5},{8,10},{9,11},{10,... | collective-permute-start | bytes 21512 | tf_op jit(solution)/shard_map/ppermute | solution.py:26
  98.6 0.7 collective-permute-start.19
  99.3 1.1 %collective-permute-start.20 = (f32[1,1792]{1,0:T(1,128)S(1)}, f32[1,1792]{1,0:T(1,128)S(1)}, u32[]{:S(2)}, u32[]{:S(2)}) collective-permute-start(f32[1,1792]{1,0:T(1,128)S(1)} %add.3.refs_0_), channel_id=1, source_target_pairs={{0,3},{1,2},{2,1},{3,0},{4,7},{5,6},{6,5},{7,4},{8,11},{9,10},{10,... | collective-permute-start | bytes 21512 | tf_op jit(solution)/shard_map/ppermute | solution.py:26
  100.3 0.2 collective-permute-done.18.refs_1_
  100.5 1.8 %collective-permute-done.19.refs_2_ = f32[1,1792]{1,0:T(1,128)S(1)} collective-permute-done((f32[1,1792]{1,0:T(1,128)S(1)}, f32[1,1792]{1,0:T(1,128)S(1)}, u32[]{:S(2)}, u32[]{:S(2)}) %collective-permute-start.19) | collective-permute-done | bytes 7200 | tf_op jit(solution)/shard_map/ppermute | solution.py:26
  102.3 1.6 %collective-permute-done.20.refs_3_ = f32[1,1792]{1,0:T(1,128)S(1)} collective-permute-done((f32[1,1792]{1,0:T(1,128)S(1)}, f32[1,1792]{1,0:T(1,128)S(1)}, u32[]{:S(2)}, u32[]{:S(2)}) %collective-permute-start.20) | collective-permute-done | bytes 7200 | tf_op jit(solution)/shard_map/ppermute | solution.py:26
  103.8 1.3 %shard_map.91 = (f32[1,768]{1,0:T(1,128)}, f32[2,512]{1,0:T(2,128)}) custom-call(s32[16]{0:T(128)} %parent_ref.3, f32[1,1792]{1,0:T(1,128)S(1)} %add.3.refs_0_, f32[1,1792]{1,0:T(1,128)S(1)} %collective-permute-done.18.refs_1_, f32[1,1792]{1,0:T(1,128)S(1)} %collective-permute-done.19.refs_2_, f32[1,1792]{1,0:T(1,128)S(1)} %collective-permute-done.20.refs_3_), custom_call_target="tpu_custom_call" | custom-call | bytes 1000 | tf_op jit(solution)/shard_map/pallas_call | solution.py:252
  (1 shorter events, 0.0 us)
Async XLA Ops:
  0.6 9.0 %collective-permute-start = (f32[2,256,512]{2,1,0:T(8,128)}, f32[2,256,512]{2,1,0:T(8,128)S(1)}, u32[]{:S(2)}, u32[]{:S(2)}) collective-permute-start(f32[2,256,512]{2,1,0:T(8,128)} %own_rows.1), channel_id=1, source_target_pairs={{0,4},{1,5},{2,6},{3,7},{4,0},{5,1},{6,2},{7,3},{8,12},{9,13},{10,... | collective-permute-start | bytes 3145736 | tf_op jit(solution)/shard_map/ppermute | solution.py:26
  1.1 15.8 %copy-start.1 = (f32[1,384,768]{2,1,0:T(8,128)S(1)}, f32[1,384,768]{2,1,0:T(8,128)}, u32[]{:S(2)}) copy-start(f32[1,384,768]{2,1,0:T(8,128)} %param.8) | copy-start | bytes 3538948
  1.2 10.1 %collective-permute-start.2 = (f32[192,768]{1,0:T(8,128)}, f32[192,768]{1,0:T(8,128)S(1)}, u32[]{:S(2)}, u32[]{:S(2)}) collective-permute-start(f32[192,768]{1,0:T(8,128)} %bitcast.5), channel_id=1, source_target_pairs={{0,0},{1,4},{2,2},{3,6},{4,1},{5,5},{6,3},{7,7},{8,8},{9,12},{10,1... | collective-permute-start | bytes 1769480 | tf_op jit(solution)/shard_map/ppermute | solution.py:36
  3.0 12.5 %collective-permute-start.3 = (f32[192,768]{1,0:T(8,128)}, f32[192,768]{1,0:T(8,128)S(1)}, u32[]{:S(2)}, u32[]{:S(2)}) collective-permute-start(f32[192,768]{1,0:T(8,128)} %bitcast.6), channel_id=1, source_target_pairs={{0,2},{2,0},{5,7},{7,5},{8,10},{10,8},{13,15},{15,13},{16,18},{18,... | collective-permute-start | bytes 1769480 | tf_op jit(solution)/shard_map/ppermute | solution.py:26
  7.4 2.2 %collective-permute-start.1 = (f32[2,128,512]{2,1,0:T(8,128)}, f32[2,128,512]{2,1,0:T(8,128)S(1)}, u32[]{:S(2)}, u32[]{:S(2)}) collective-permute-start(f32[2,128,512]{2,1,0:T(8,128)} %own_inverse.1), channel_id=1, source_target_pairs={{0,4},{1,5},{2,6},{3,7},{4,0},{5,1},{6,2},{7,3},{8,12},{9,13},{10,... | collective-permute-start | bytes 1572872 | tf_op jit(solution)/shard_map/ppermute | solution.py:26
  15.5 1.5 %collective-permute-start.4 = (f32[2,384,512]{2,1,0:T(8,128)S(1)}, f32[2,384,512]{2,1,0:T(8,128)S(1)}, u32[]{:S(2)}, u32[]{:S(2)}) collective-permute-start(f32[2,384,512]{2,1,0:T(8,128)S(1)} %get-tuple-element.28), channel_id=1, source_target_pairs={{0,0},{1,4},{2,2},{3,6},{4,1},{5,5},{6,3},{7,7},{8,8},{9,12},{10,1... | collective-permute-start | bytes 4718600 | tf_op jit(solution)/shard_map/ppermute | solution.py:36
  16.3 1.5 %collective-permute-start.6 = (f32[192,768]{1,0:T(8,128)S(1)}, f32[192,768]{1,0:T(8,128)S(1)}, u32[]{:S(2)}, u32[]{:S(2)}) collective-permute-start(f32[192,768]{1,0:T(8,128)S(1)} %collective-permute-done.2.refs_0_), channel_id=1, source_target_pairs={{1,3},{3,1},{4,6},{6,4},{9,11},{11,9},{12,14},{14,12},{17,19},{19,... | collective-permute-start | bytes 1769480 | tf_op jit(solution)/shard_map/ppermute | solution.py:26
  17.0 33.8 %collective-permute-start.5 = (f32[384,768]{1,0:T(8,128)S(1)}, f32[384,768]{1,0:T(8,128)S(1)}, u32[]{:S(2)}, u32[]{:S(2)}) collective-permute-start(f32[384,768]{1,0:T(8,128)S(1)} %bitcast.4), channel_id=1, source_target_pairs={{0,0},{1,4},{2,2},{3,6},{4,1},{5,5},{6,3},{7,7},{8,8},{9,12},{10,1... | collective-permute-start | bytes 3538952 | tf_op jit(solution)/shard_map/ppermute | solution.py:36
  17.7 39.0 %collective-permute-start.7 = (f32[2,384,512]{2,1,0:T(8,128)S(1)}, f32[2,384,512]{2,1,0:T(8,128)S(1)}, u32[]{:S(2)}, u32[]{:S(2)}) collective-permute-start(f32[2,384,512]{2,1,0:T(8,128)S(1)} %collective-permute-done.4.refs_0_), channel_id=1, source_target_pairs={{0,2},{1,3},{2,0},{3,1},{4,6},{5,7},{6,4},{7,5},{8,10},{9,11},{10,... | collective-permute-start | bytes 4718600 | tf_op jit(solution)/shard_map/ppermute | solution.py:26
  19.8 23.8 %collective-permute-start.11 = (f32[192,768]{1,0:T(8,128)S(1)}, f32[192,768]{1,0:T(8,128)S(1)}, u32[]{:S(2)}, u32[]{:S(2)}) collective-permute-start(f32[192,768]{1,0:T(8,128)S(1)} %collective-permute-done.6.refs_3_), channel_id=1, source_target_pairs={{1,5},{3,7},{4,0},{6,2},{9,13},{11,15},{12,8},{14,10},{17,21},{19,... | collective-permute-start | bytes 1769480 | tf_op jit(solution)/shard_map/ppermute | solution.py:26
  21.1 22.8 %collective-permute-start.10 = (f32[192,768]{1,0:T(8,128)S(1)}, f32[192,768]{1,0:T(8,128)S(1)}, u32[]{:S(2)}, u32[]{:S(2)}) collective-permute-start(f32[192,768]{1,0:T(8,128)S(1)} %collective-permute-done.2.refs_0_), channel_id=1, source_target_pairs={{0,4},{1,5},{2,6},{3,7},{4,0},{5,1},{6,2},{7,3},{8,12},{9,13},{10,... | collective-permute-start | bytes 1769480 | tf_op jit(solution)/shard_map/ppermute | solution.py:26
  41.7 3.5 %collective-permute-start.12 = (f32[192,768]{1,0:T(8,128)S(1)}, f32[192,768]{1,0:T(8,128)S(1)}, u32[]{:S(2)}, u32[]{:S(2)}) collective-permute-start(f32[192,768]{1,0:T(8,128)S(1)} %collective-permute-done.3.refs_2_), channel_id=1, source_target_pairs={{0,4},{2,6},{5,1},{7,3},{8,12},{10,14},{13,9},{15,11},{16,20},{18,... | collective-permute-start | bytes 1769480 | tf_op jit(solution)/shard_map/ppermute | solution.py:26
  45.2 5.6 %copy-start = (f32[1,384,1536]{2,1,0:T(8,128)S(1)}, f32[1,384,1536]{2,1,0:T(8,128)}, u32[]{:S(2)}) copy-start(f32[1,384,1536]{2,1,0:T(8,128)} %param.7) | copy-start | bytes 7077892
  50.8 30.8 %collective-permute-start.13 = (f32[384,1536]{1,0:T(8,128)S(1)}, f32[384,1536]{1,0:T(8,128)S(1)}, u32[]{:S(2)}, u32[]{:S(2)}) collective-permute-start(f32[384,1536]{1,0:T(8,128)S(1)} %bitcast.3), channel_id=1, source_target_pairs={{0,0},{1,4},{2,2},{3,6},{4,1},{5,5},{6,3},{7,7},{8,8},{9,12},{10,1... | collective-permute-start | bytes 7077896 | tf_op jit(solution)/shard_map/ppermute | solution.py:36
  51.8 11.3 %collective-permute-start.14 = (f32[2,384,512]{2,1,0:T(8,128)S(1)}, f32[2,384,512]{2,1,0:T(8,128)S(1)}, u32[]{:S(2)}, u32[]{:S(2)}) collective-permute-start(f32[2,384,512]{2,1,0:T(8,128)S(1)} %collective-permute-done.4.refs_0_), channel_id=1, source_target_pairs={{0,4},{1,5},{2,6},{3,7},{4,0},{5,1},{6,2},{7,3},{8,12},{9,13},{10,... | collective-permute-start | bytes 4718600 | tf_op jit(solution)/shard_map/ppermute | solution.py:26
  56.7 7.5 %collective-permute-start.15 = (f32[2,384,512]{2,1,0:T(8,128)S(1)}, f32[2,384,512]{2,1,0:T(8,128)S(1)}, u32[]{:S(2)}, u32[]{:S(2)}) collective-permute-start(f32[2,384,512]{2,1,0:T(8,128)S(1)} %collective-permute-done.7.refs_2_), channel_id=1, source_target_pairs={{0,4},{1,5},{2,6},{3,7},{4,0},{5,1},{6,2},{7,3},{8,12},{9,13},{10,... | collective-permute-start | bytes 4718600 | tf_op jit(solution)/shard_map/ppermute | solution.py:26
  61.2 28.0 %collective-permute-start.9 = (f32[384,768]{1,0:T(8,128)S(1)}, f32[384,768]{1,0:T(8,128)S(1)}, u32[]{:S(2)}, u32[]{:S(2)}) collective-permute-start(f32[384,768]{1,0:T(8,128)S(1)} %collective-permute-done.5.factor.refs_0_), channel_id=1, source_target_pairs={{0,2},{1,3},{2,0},{3,1},{4,6},{5,7},{6,4},{7,5},{8,10},{9,11},{10,... | collective-permute-start | bytes 3538952 | tf_op jit(solution)/shard_map/ppermute | solution.py:26
  63.1 26.1 %collective-permute-start.8 = (f32[384,768]{1,0:T(8,128)S(1)}, f32[384,768]{1,0:T(8,128)S(1)}, u32[]{:S(2)}, u32[]{:S(2)}) collective-permute-start(f32[384,768]{1,0:T(8,128)S(1)} %collective-permute-done.5.factor.refs_0_), channel_id=1, source_target_pairs={{0,4},{1,5},{2,6},{3,7},{4,0},{5,1},{6,2},{7,3},{8,12},{9,13},{10,... | collective-permute-start | bytes 3538952 | tf_op jit(solution)/shard_map/ppermute | solution.py:26
  89.2 2.8 %collective-permute-start.16 = (f32[384,768]{1,0:T(8,128)S(1)}, f32[384,768]{1,0:T(8,128)S(1)}, u32[]{:S(2)}, u32[]{:S(2)}) collective-permute-start(f32[384,768]{1,0:T(8,128)S(1)} %collective-permute-done.9.refs_2_), channel_id=1, source_target_pairs={{0,4},{1,5},{2,6},{3,7},{4,0},{5,1},{6,2},{7,3},{8,12},{9,13},{10,... | collective-permute-start | bytes 3538952 | tf_op jit(solution)/shard_map/ppermute | solution.py:26
  95.5 1.2 %collective-permute-start.17 = (f32[1,1792]{1,0:T(1,128)S(1)}, f32[1,1792]{1,0:T(1,128)S(1)}, u32[]{:S(2)}, u32[]{:S(2)}) collective-permute-start(f32[1,1792]{1,0:T(1,128)S(1)} %shard_map.90), channel_id=1, source_target_pairs={{0,4},{1,5},{2,6},{3,7},{4,0},{5,1},{6,2},{7,3},{8,12},{9,13},{10,... | collective-permute-start | bytes 21512 | tf_op jit(solution)/shard_map/ppermute | solution.py:26
  96.8 3.7 %collective-permute-start.18 = (f32[1,1792]{1,0:T(1,128)S(1)}, f32[1,1792]{1,0:T(1,128)S(1)}, u32[]{:S(2)}, u32[]{:S(2)}) collective-permute-start(f32[1,1792]{1,0:T(1,128)S(1)} %add.3.refs_0_), channel_id=1, source_target_pairs={{0,2},{1,3},{2,0},{3,1},{4,6},{5,7},{6,4},{7,5},{8,10},{9,11},{10,... | collective-permute-start | bytes 21512 | tf_op jit(solution)/shard_map/ppermute | solution.py:26
  98.6 3.6 %collective-permute-start.19 = (f32[1,1792]{1,0:T(1,128)S(1)}, f32[1,1792]{1,0:T(1,128)S(1)}, u32[]{:S(2)}, u32[]{:S(2)}) collective-permute-start(f32[1,1792]{1,0:T(1,128)S(1)} %add.3.refs_0_), channel_id=1, source_target_pairs={{0,1},{1,0},{2,3},{3,2},{4,5},{5,4},{6,7},{7,6},{8,9},{9,8},{10,11... | collective-permute-start | bytes 21512 | tf_op jit(solution)/shard_map/ppermute | solution.py:26
  99.3 4.5 %collective-permute-start.20 = (f32[1,1792]{1,0:T(1,128)S(1)}, f32[1,1792]{1,0:T(1,128)S(1)}, u32[]{:S(2)}, u32[]{:S(2)}) collective-permute-start(f32[1,1792]{1,0:T(1,128)S(1)} %add.3.refs_0_), channel_id=1, source_target_pairs={{0,3},{1,2},{2,1},{3,0},{4,7},{5,6},{6,5},{7,4},{8,11},{9,10},{10,... | collective-permute-start | bytes 21512 | tf_op jit(solution)/shard_map/ppermute | solution.py:26
